TPU v7x, 32 devices: a whole 2x2x4 slice. The times are simulated.
32 devices in a mesh: mem: 4 (over x, core), grid: 8 (over z, y).
Axes of the slice: x: 2, y: 2, z: 4, core: 2. Of those that a mesh axis runs over, the one named last changes fastest.
Arguments:
- hidden: bfloat16 [8, 1024, 16384], P('mem', None, 'grid'), may hold values from -6 to 6
- target: float32 [100, 16384], P(None, 'grid'), may hold values from -5 to 5
- area: float32 [16384], P('grid'), may hold values from 0.2 to 2
- var_weight: float32 [100], replicated, may hold values from 0.2 to 2
- w_inner: bfloat16 [1024, 1024], replicated, may hold values from -0.1875 to 0.1875
- b_inner: float32 [1024], replicated, may hold values from -3 to 3
- w_out: bfloat16 [100, 1024], replicated, may hold values from -0.1875 to 0.1875
- b_out: float32 [100], replicated, may hold values from -3 to 3
Outputs:
- loss: float32 [], replicated
- grad_hidden: bfloat16 [8, 1024, 16384], P('mem', None, 'grid')
- grad_inner: float32 [1024, 1024], P('grid')
- grad_out: float32 [100, 1024], replicated
All inputs are finite; a program needn't handle non-finite values.
Results may differ from a plain program's by a relative error of at most 0.0025.
The roundings to bfloat16 on the way count: a program that leaves them out, or rounds other values in their place, can miss the bound.
Values sent between devices are 32-bit elements; how exact they have to be, the bound alone decides.
No kernel may reach another device: no remote copies, remote signals or barrier semaphores. Data moves between devices by JAX's collectives and lax.ppermute only.
A program may use at most 128 MiB of HBM per device.

v0:
```python
import functools
import math

import jax
import jax.numpy as jnp
from jax import lax
from jax.experimental import pallas as pl
from jax.experimental.pallas import tpu as pltpu
from jax.sharding import PartitionSpec as P

EIGHTHS = (2, 3, 3)
TILE = 256
EPS = 0.0004
K0 = math.sqrt(2.0 / math.pi)
K1 = K0 * 0.044715
SLAB = 512
EXTRA_ROWS = 8
VMEM = 8 * 1024 * 1024
NT = (((1,), (1,)), ((), ()))


def column(row, size):
    r = lax.broadcasted_iota(jnp.int32, (size, size), 0)
    c = lax.broadcasted_iota(jnp.int32, (size, size), 1)
    return jnp.sum(jnp.where(r == c, row, 0.0), axis=1, keepdims=True)


def field_rows(v, mloc, m, r0):
    full = v // 8 * 8
    if r0 < full:
        return pl.ds(m * full + r0, 8)
    return pl.ds(mloc * full + m * (v - full), v - full)


def forward_kernel(hid_ref, w_ref, b_ref, wo_ref, bo_ref, act_ref, slope_ref, f_ref, bias, half, fields, *slabs):
    step = pl.program_id(0)
    last = pl.num_programs(0) - 1
    mloc, h, t = hid_ref.shape
    v = half.shape[0]
    size = h // len(slabs)

    @pl.when(step == 0)
    def _():
        for k in range(h // 128):
            bias[pl.ds(k * 128, 128), :] = jnp.broadcast_to(
                column(b_ref[:, pl.ds(k * 128, 128)], 128), (128, 128)
            )
        half[...] = wo_ref[...] * jnp.bfloat16(0.5)

    def multiply(k):
        hid = jnp.concatenate([hid_ref[m] for m in range(mloc)], axis=1)
        rows = pl.ds(k * size, size)
        slabs[k][...] = jnp.dot(w_ref[rows, :], hid, preferred_element_type=jnp.float32)

    def gelu(tile, k):
        for r in range(0, size, 16):
            rows = pl.ds(k * size + r, 16)
            b = jnp.concatenate([bias[rows, :]] * (t // 128), axis=1)
            for m in range(mloc):
                x = slabs[k][pl.ds(r, 16), pl.ds(m * t, t)] + b
                q = x * x * K1
                th = jnp.tanh(x * (K0 + q))
                up = 1.0 + th
                act = x * up
                act_ref[tile, m, rows, :] = act.astype(jnp.bfloat16)
                slope_ref[tile, m, rows, :] = up + act * ((1.0 - th) * (K0 + 3.0 * q))
        rows = pl.ds(k * size, size)
        act = jnp.concatenate([act_ref[tile, m, rows, :] for m in range(mloc)], axis=1)
        return jnp.dot(half[:, rows], act, preferred_element_type=jnp.float32)

    def finish():
        out = fields[...] + gelu(lax.max(step - 1, 0), 1)
        for m in range(mloc):
            for r0 in range(0, v, 8):
                f_ref[field_rows(v, mloc, m, r0), :] = out[r0 : r0 + 8, m * t : (m + 1) * t]

    @pl.when(step < last)
    def _():
        multiply(0)
        finish()
        multiply(1)
        fields[...] = gelu(step, 0) + column(bo_ref[...], v)

    @pl.when(step == last)
    def _():
        finish()


def forward(start, p, hidden, w_inner, b_inner, w_out, b_out, vmem):
    mloc, h, n = hidden.shape
    v = w_out.shape[0]
    t = TILE
    tiles = p // t
    whole = lambda s: (0, 0)
    once = pl.Buffered(1)
    shape = (p // t, mloc, h, t)
    held = pl.BlockSpec(shape, lambda s: (0, 0, 0, 0))
    return pl.pallas_call(
        forward_kernel,
        grid=(tiles + 1,),
        in_specs=[
            pl.BlockSpec((mloc, h, t), lambda s: (0, 0, start // t + jnp.minimum(s, tiles - 1))),
            pl.BlockSpec((h, h), whole, pipeline_mode=once),
            pl.BlockSpec((1, h), whole, pipeline_mode=once),
            pl.BlockSpec((v, h), whole, pipeline_mode=once),
            pl.BlockSpec((1, v), whole, pipeline_mode=once),
        ],
        out_specs=[
            held,
            held,
            pl.BlockSpec((mloc * v, t), lambda s: (0, jnp.maximum(s - 1, 0))),
        ],
        out_shape=[
            pltpu.VMEM(shape, jnp.bfloat16),
            pltpu.VMEM(shape, jnp.float32),
            jax.ShapeDtypeStruct((mloc * v, p), jnp.float32),
        ],
        scratch_shapes=[
            pltpu.VMEM((h, 128), jnp.float32),
            pltpu.VMEM((v, h), jnp.bfloat16),
            pltpu.VMEM((v, mloc * t), jnp.float32),
            pltpu.VMEM((h // 2, mloc * t), jnp.float32),
            pltpu.VMEM((h // 2, mloc * t), jnp.float32),
        ],
        compiler_params=pltpu.CompilerParams(vmem_limit_bytes=vmem),
        cost_estimate=pl.CostEstimate(
            flops=2 * h * h, bytes_accessed=2 * h * h, transcendentals=0
        ),
        name="forward_part",
    )(hidden, w_inner, b_inner, w_out, b_out)


def backward_kernel(
    first, last, dims, members,
    f_ref, fc_ref, fx_ref, fxc_ref, target_ref, area_ref, vw_ref, act_ref, slope_ref, hid_ref,
    wot_ref, acc_in, extra_in, gp_ref, extra_ref, *refs,
):
    acc, *refs = refs
    if last:
        keep_x, send_x, keep_y, send_y, *refs = refs
    (gf,) = refs
    step = pl.program_id(0)
    end = pl.num_programs(0) - 1
    mloc, _, t = hid_ref.shape
    v = target_ref.shape[0]
    h = wot_ref.shape[0]
    denom = members * (members - 1)

    def pair(a, b):
        d = a - b
        s = d * d + EPS
        r = lax.rsqrt(s)
        return d * r, s * r

    def scores(r0, vw, area):
        rows = pl.ds(r0, min(8, v - r0))
        places = [field_rows(v, mloc, m, r0) for m in range(mloc)]
        own = [f_ref[place, :] for place in places]
        others = [ref[place, :] for ref in (fc_ref, fx_ref, fxc_ref) for place in places]
        target = target_ref[rows, :]
        dsum = [jnp.zeros_like(target) for _ in range(mloc)]
        obs = []
        cross = inner = near = jnp.zeros_like(target)
        n_cross = n_inner = 0
        for i in range(mloc):
            sl, ph = pair(own[i], target)
            obs.append(sl)
            near = near + ph
            for b in others:
                sl, ph = pair(own[i], b)
                dsum[i] = dsum[i] + sl
                cross = cross + ph
                n_cross += 1
            for j in range(i + 1, mloc):
                sl, ph = pair(own[i], own[j])
                dsum[i] = dsum[i] + sl
                dsum[j] = dsum[j] - sl
                inner = inner + ph
                n_inner += 1
        weight = vw[r0 : r0 + 8] * area
        for m in range(mloc):
            gf[m, rows, :] = weight * (obs[m] * (1.0 / members) - dsum[m] * (1.0 / denom))
        near = (near - 0.02 * mloc) * (1.0 / members)
        pairs = (inner - 0.02 * n_inner) + 0.5 * (cross - 0.02 * n_cross)
        return jnp.sum(weight * (near - pairs * (1.0 / denom)), axis=0, keepdims=True)

    def weights(k):
        rows = pl.ds(k, SLAB)
        hid = jnp.concatenate([hid_ref[m] for m in range(mloc)], axis=1)
        acc[rows, :] += lax.dot_general(
            gp_ref[step - 1, rows, :], hid, NT, preferred_element_type=jnp.float32
        )

    def work(with_weights):
        vw, area = column(vw_ref[...], v), area_ref[...]
        starts = list(range(0, v, 8))
        slabs = list(range(0, h, SLAB)) if with_weights else [None]
        loss = jnp.zeros((1, t), jnp.float32)
        for k, slab in enumerate(slabs):
            if with_weights:
                weights(slab)
            for r0 in starts[k :: len(slabs)]:
                loss = loss + scores(r0, vw, area)
        for m in range(mloc):
            gf[m, pl.ds(v, gf.shape[1] - v), :] = jnp.zeros((gf.shape[1] - v, t), jnp.float32)
        g = jnp.concatenate([gf[m] for m in range(mloc)], axis=1).astype(jnp.bfloat16)
        for k in range(0, h, 256):
            rows = pl.ds(k, 256)
            ga = jnp.dot(wot_ref[rows, :], g, preferred_element_type=jnp.float32)
            for m in range(mloc):
                piece = ga[:, m * t : (m + 1) * t] * slope_ref[step, m, rows, :]
                gp_ref[step, rows, pl.ds(m * t, t)] = piece.astype(jnp.bfloat16)
        act = jnp.concatenate([act_ref[step, m] for m in range(mloc)], axis=1)
        extra_ref[...] += lax.dot_general(g, act, NT, preferred_element_type=jnp.float32)
        extra_ref[pl.ds(v, 1), pl.ds(0, t)] += loss

    @pl.when(step == 0)
    def _():
        if first:
            acc[...] = jnp.zeros_like(acc)
            extra_ref[...] = jnp.zeros_like(extra_ref)
        else:
            extra_ref[...] = extra_in[...]
        work(False)

    @pl.when((step > 0) & (step < end))
    def _():
        work(True)

    @pl.when(step == end)
    def _():
        for k in range(0, h, SLAB):
            weights(k)

    if last:
        n_hi, n_lo = dims

        @pl.when(step == end)
        def _():
            mem = lax.axis_index("mem")
            grid = lax.axis_index("grid")
            x, core = mem // 2, mem % 2
            hi, lo = grid // n_lo, grid % n_lo
            r = h // (2 * n_hi * n_lo)
            cx = keep_x.shape[4]
            for dlo in range(n_lo):
                for dhi in range(n_hi):
                    g = lax.rem(hi + dhi, n_hi) * n_lo + lax.rem(lo + dlo, n_lo)
                    block = dhi * n_lo + lax.rem(lo + dlo, n_lo)
                    for c, to_x, to_y in ((core, keep_x, keep_y), (1 - core, send_x, send_y)):
                        r0 = pl.multiple_of((g * 2 + c) * r, r)
                        total = acc[pl.ds(r0, r), :]
                        e0 = (c * (n_hi * n_lo) + block) * EXTRA_ROWS
                        at = pl.multiple_of(
                            jnp.minimum(e0, extra_ref.shape[0] - EXTRA_ROWS), EXTRA_ROWS
                        )
                        e = jnp.where(
                            e0 < extra_ref.shape[0], extra_ref[pl.ds(at, EXTRA_ROWS), :], 0.0
                        )
                        for values, rows in ((total, pl.ds(0, r)), (e, pl.ds(r, EXTRA_ROWS))):
                            q = [values[:, k * cx : (k + 1) * cx] for k in range(4)]
                            for d in range(2):
                                own = x == d
                                to_x[d, dlo, dhi, rows, :] = jnp.where(own, q[0], q[1])
                                to_y[dlo, d, dhi, rows, :] = jnp.where(own, q[2], q[3])


def backward(start, p, first, last, dims, members, fields, rest, acc, extra):
    target, area, vw, act, slope, hidden, wot = rest
    mloc, h, n = hidden.shape
    v = target.shape[0]
    vp = wot.shape[1]
    t = TILE
    off = start // t
    once = pl.Buffered(1)
    steps = p // t
    ahead = lambda s: jnp.minimum(s, steps - 1)
    f_spec = pl.BlockSpec((mloc * v, t), lambda s: (0, ahead(s)))
    whole = lambda s: (0, 0)
    const = lambda a: pl.BlockSpec(a.shape, whole, pipeline_mode=once)
    held = lambda a: pl.BlockSpec(a.shape, lambda s: (0,) * len(a.shape))
    in_specs = [f_spec] * 4 + [
        pl.BlockSpec((v, t), lambda s: (0, off + ahead(s))),
        pl.BlockSpec((1, t), lambda s: (0, off + ahead(s))),
        const(vw), held(act), held(slope),
        pl.BlockSpec((mloc, h, t), lambda s: (0, 0, off + jnp.maximum(s - 1, 0))),
        const(wot),
    ]
    act, slope = (pltpu.with_memory_space_constraint(a, pltpu.VMEM) for a in (act, slope))
    args = [*fields, target, area, vw, act, slope, hidden, wot]
    kernel = functools.partial(backward_kernel, first, last, dims, members)
    if first:
        kernel_fn = lambda *refs: kernel(*refs[:11], None, None, *refs[11:])
        aliases = {}
    else:
        kernel_fn = kernel
        in_specs += [held(acc), const(extra)]
        args += [acc, extra]
        aliases = {11: 2}
    out_shape = [
        pltpu.VMEM((p // t, h, mloc * t), jnp.bfloat16),
        jax.ShapeDtypeStruct((vp, h), jnp.float32),
        pltpu.VMEM((h, h), jnp.float32),
    ]
    if last:
        n_hi, n_lo = dims
        r = h // (2 * n_hi * n_lo)
        cx = h // 4
        out_shape += [pltpu.VMEM((2, n_lo, n_hi, r + EXTRA_ROWS, cx), jnp.float32)] * 2
        out_shape += [pltpu.VMEM((n_lo, 2, n_hi, r + EXTRA_ROWS, cx), jnp.float32)] * 2
    out_specs = [held(a) for a in out_shape]
    return pl.pallas_call(
        kernel_fn,
        grid=(steps + 1,),
        in_specs=in_specs,
        out_specs=out_specs,
        out_shape=out_shape,
        scratch_shapes=[pltpu.VMEM((mloc, vp, t), jnp.float32)],
        input_output_aliases=aliases,
        compiler_params=pltpu.CompilerParams(vmem_limit_bytes=VMEM),
        cost_estimate=pl.CostEstimate(
            flops=2 * h * h, bytes_accessed=2 * h * h, transcendentals=0
        ),
        name="backward_part",
    )(*args)


def transposes_kernel(w_ref, wo_ref, wt_ref, wot_ref):
    wt_ref[...] = w_ref[...].astype(jnp.float32).T.astype(jnp.bfloat16)

    @pl.when(pl.program_id(0) == 0)
    def _():
        v, h = wo_ref.shape
        rows = jnp.concatenate(
            [wo_ref[...].astype(jnp.float32) * 0.5, jnp.zeros((wot_ref.shape[1] - v, h), jnp.float32)], 0
        )
        wot_ref[...] = rows.T.astype(jnp.bfloat16)


def transposes(w_inner, w_out, vp):
    v, h = w_out.shape
    t = TILE
    return pl.pallas_call(
        transposes_kernel,
        grid=(h // t,),
        in_specs=[
            pl.BlockSpec((t, h), lambda s: (s, 0)),
            pl.BlockSpec((v, h), lambda s: (0, 0)),
        ],
        out_specs=[
            pl.BlockSpec((h, t), lambda s: (0, s)),
            pl.BlockSpec((h, vp), lambda s: (0, 0)),
        ],
        out_shape=[pltpu.VMEM((h, h), jnp.bfloat16), pltpu.VMEM((h, vp), jnp.bfloat16)],
        compiler_params=pltpu.CompilerParams(vmem_limit_bytes=VMEM),
        cost_estimate=pl.CostEstimate(flops=2 * h, bytes_accessed=2 * h, transcendentals=0),
        name="transposes",
    )(w_inner, w_out)


def input_kernel(wt_ref, gp_ref, *refs):
    mloc, h, t = refs[-1].shape
    for k in range(0, h, SLAB):
        rows = pl.ds(k, SLAB)
        out = jnp.dot(wt_ref[rows, :], gp_ref[pl.program_id(0)], preferred_element_type=jnp.float32)
        for m in range(mloc):
            refs[-1][m, rows, :] = out[:, m * t : (m + 1) * t].astype(jnp.bfloat16)


def input_gradient(start, p, n, wt, gp, gh):
    steps, h, width = gp.shape
    t = TILE
    mloc = width // t
    off = start // t
    in_specs = [
        pl.BlockSpec((h, h), lambda s: (0, 0), pipeline_mode=pl.Buffered(1)),
        pl.BlockSpec(gp.shape, lambda s: (0, 0, 0)),
    ]
    args = [wt, gp]
    if gh is not None:
        in_specs.append(pl.BlockSpec(memory_space=pl.ANY))
        args.append(gh)
    return pl.pallas_call(
        input_kernel,
        grid=(steps,),
        in_specs=in_specs,
        out_specs=pl.BlockSpec((mloc, h, t), lambda s: (0, 0, off + s)),
        out_shape=jax.ShapeDtypeStruct((mloc, h, n), jnp.bfloat16),
        input_output_aliases={} if gh is None else {2: 0},
        compiler_params=pltpu.CompilerParams(vmem_limit_bytes=VMEM),
        cost_estimate=pl.CostEstimate(
            flops=2 * h * h, bytes_accessed=2 * h * h, transcendentals=0
        ),
        name="grad_hidden_part",
    )(*args)


def after(value, *others):
    return lax.optimization_barrier((value,) + others)[0]


def shards(hidden, target, area, var_weight, w_inner, b_inner, w_out, b_out):
    mloc, h, n = hidden.shape
    n_mem = lax.axis_size("mem")
    n_grid = lax.axis_size("grid")
    members = mloc * n_mem
    npoints = n * n_grid
    v = w_out.shape[0]
    vp = 128
    n_lo = 2
    while n_lo * n_lo * 4 <= n_grid:
        n_lo *= 2
    n_hi = n_grid // n_lo

    swap_x = [(i, (i + n_mem // 2) % n_mem) for i in range(n_mem)]
    swap_core = [(i, i ^ 1) for i in range(n_mem)]

    def shift_lo(k):
        return [(a * n_lo + b, a * n_lo + (b + k) % n_lo) for a in range(n_hi) for b in range(n_lo)]

    def shift_hi(k):
        return [(a * n_lo + b, (a + k) % n_hi * n_lo + b) for a in range(n_hi) for b in range(n_lo)]

    to_x = lambda a: lax.ppermute(a, "mem", swap_x)
    to_core = lambda a: lax.ppermute(a, "mem", swap_core)
    to_lo = lambda a, k: lax.ppermute(a, "grid", shift_lo(k))
    to_hi = lambda a, k: lax.ppermute(a, "grid", shift_hi(k))

    mem, grid = lax.axis_index("mem"), lax.axis_index("grid")
    at_zero = {("mem", bit): mem & bit == 0 for bit in (1, n_mem // 2)}
    bit = 1
    while bit < n_lo:
        at_zero["grid", bit] = grid & bit == 0
        bit *= 2
    hidden, at_zero = lax.optimization_barrier((hidden, at_zero))
    hidden, w_out, b_inner, b_out = (
        pltpu.with_memory_space_constraint(a, pltpu.HBM)
        for a in (hidden, w_out, b_inner.reshape(1, h), b_out.reshape(1, v))
    )
    unit = n // sum(EIGHTHS)
    starts = [unit * sum(EIGHTHS[:k]) for k in range(len(EIGHTHS))]
    spans = [(start, unit * size) for start, size in zip(starts, EIGHTHS)]
    parts, far = [], []
    for start, p in spans:
        w, vmem = w_inner, VMEM
        if parts:
            b_out = after(b_out, parts[-1][2])
        else:
            w = pltpu.with_memory_space_constraint(w_inner, pltpu.HBM)
            vmem += 4 * h * h
        parts.append(forward(start, p, hidden, w, b_inner, w_out, b_out, vmem))
        far.append(to_x(parts[-1][2]))
    near = [to_core(fields) for _, _, fields in parts]
    wt, wot = transposes(after(w_inner, parts[-1][2]), w_out, vp)
    vw, area = var_weight.reshape(1, v), area.reshape(1, n)
    acc = extra = gh = None
    grad_pre = []
    for k, (start, p) in enumerate(spans):
        act, slope, fields = parts[k]
        first, last = k == 0, k == len(spans) - 1
        if k:
            far[k] = after(far[k], parts[-1][2] if k == 1 else grad_pre[k - 2])
        gp, extra, acc, *accs = backward(
            start, p, first, last, (n_hi, n_lo), members,
            (fields, near[k], far[k], to_core(far[k])),
            (target, area, vw, act, slope, hidden, wot), acc, extra,
        )
        grad_pre.append(gp)
    keep_x, send_x, keep_y, send_y = accs

    def gathered(block, axis, name, bit):
        n = lax.axis_size(name)
        other = lax.ppermute(block, name, [(i, i ^ bit) for i in range(n)])
        return ordered(block, other, axis, name, bit)

    def ordered(block, other, axis, name, bit):
        return jnp.where(
            at_zero[name, bit],
            jnp.concatenate([block, other], axis),
            jnp.concatenate([other, block], axis),
        )

    def beside(k, gh, start_after, wait_for):
        gh = input_gradient(*spans[k], n, wt, after(grad_pre[k], start_after), gh)
        return lax.optimization_barrier((gh, wait_for))

    r, cx = h // (2 * n_grid), keep_x.shape[-1]
    others = range(1, n_lo)
    got_x = to_core(send_x)
    got_y = to_core(send_y)
    out_x = keep_x[1] + got_x[1]
    out_y = [keep_y[k] + got_y[k] for k in others]
    from_x = to_x(out_x)
    from_y = [to_lo(out_y[k - 1], k) for k in others]
    gh, (keep_x, keep_y) = beside(0, gh, (out_x, out_y), (keep_x, keep_y))
    own_x = keep_x[0] + got_x[0] + from_x
    own_y = sum(from_y, keep_y[0] + got_y[0])
    own_x, own_y = [own_x[k] for k in range(n_lo)], [own_y[k] for k in range(2)]
    from_y = [to_lo(own_x[k], k) for k in others]
    from_x = to_x(own_y[1])
    gh, (own_x, own_y) = beside(1, gh, (own_x[1:], own_y[1]), (own_x[0], own_y[0]))
    sums = [sum(from_y, own_x), own_y + from_x]

    extra = [part[:, r:].reshape(-1, cx) for part in sums]
    pieces = [jnp.concatenate([part[k, :r] for part in sums] + extra, 0) for k in range(n_hi)]
    from_hi = [to_hi(pieces[k], k) for k in range(1, n_hi)]
    gh, own = beside(2, gh, pieces[1:], pieces[0])
    total = sum(from_hi, own)
    far = to_x(total)
    mine = total[2 * r :][None]
    beyond = lax.ppermute(mine, "grid", [(g, g ^ 1) for g in range(n_grid)])
    pairs = [(m * n_grid + g, (m + n_mem // 2) % n_mem * n_grid + (g ^ 1)) for m in range(n_mem) for g in range(n_grid)]
    across = lax.ppermute(mine, ("mem", "grid"), pairs)

    scale = 1.0 / math.sqrt(members * npoints)
    halves = [ordered(total[k : k + r], far[k : k + r], 1, "mem", n_mem // 2) for k in (0, r)]
    grad_inner = gathered(jnp.concatenate(halves, 1) * scale, 0, "mem", 1)

    sides = [ordered(mine, far[2 * r :][None], 0, "mem", n_mem // 2)]
    sides.append(ordered(beyond, across, 0, "mem", n_mem // 2))
    extra = ordered(*(side[None] for side in sides), 0, "grid", 1)
    bit = 2
    while bit < n_lo:
        extra = gathered(extra, 0, "grid", bit)
        bit *= 2
    extra = gathered(extra[None], 0, "mem", 1)
    extra = extra.reshape(2, n_lo, 2, 2, n_hi, EXTRA_ROWS, cx)
    extra = extra.transpose(0, 4, 1, 5, 3, 2, 6).reshape(2 * n_grid * EXTRA_ROWS, h)
    loss = jnp.sum(extra[v]) / npoints
    return (loss, gh, grad_inner, extra[:v] * (0.5 * scale))


def solution(mesh):
    in_specs = (P("mem", None, "grid"), P(None, "grid"), P("grid"), P(), P(), P(), P(), P())
    out_specs = (P(), P("mem", None, "grid"), P("grid", None), P())
    return jax.shard_map(shards, mesh=mesh, in_specs=in_specs, out_specs=out_specs, check_vma=False)
```

profile of v0, /device:TPU:9, one launch (start us, length us, event | category | flops | bytes accessed | tf_op | source)
XLA Modules:
  0.0 128.5 jit_solution(10942790655155893341)
XLA Ops:
  0.7 7.5 %forward_part.3 = (bf16[2,2,1024,256]{3,2,1,0:T(8,128)(2,1)S(1)}, f32[2,2,1024,256]{3,2,1,0:T(8,128)S(1)}, f32[200,512]{1,0:T(8,128)S(1)}) custom-call(bf16[2,1024,2048]{2,1,0:T(8,128)(2,1)} %hid_ref.4, bf16[1024,1024]{1,0:T(8,128)(2,1)} %w_ref.6, f32[1,1024]{1,0:T(1,128)} %bitcast.83, bf16[100,1024]{1,0:T(8,128)(2,1)} %wo_ref.7, f32[1,100]{1,0:T(1,128)} %bitcast.86), custom_call_target="tpu_custom_call" | custom-call | flops 2097152 | bytes 2097152 | tf_op jit(solution)/shard_map/forward_part/pallas_call | solution.py:98
  8.2 1.3 collective-permute-start.3
  9.4 8.9 %forward_part.4 = (bf16[3,2,1024,256]{3,2,1,0:T(8,128)(2,1)S(1)}, f32[3,2,1024,256]{3,2,1,0:T(8,128)S(1)}, f32[200,768]{1,0:T(8,128)S(1)}) custom-call(bf16[2,1024,2048]{2,1,0:T(8,128)(2,1)} %hid_ref.4, bf16[1024,1024]{1,0:T(8,128)(2,1)S(1)} %copy-done, f32[1,1024]{1,0:T(1,128)} %bitcast.84, bf16[100,1024]{1,0:T(8,128)(2,1)} %wo_ref.7, f32[1,100]{1,0:T(1,128)} %bitcast.87), custom_call_target="tpu_custom_call" | custom-call | flops 2097152 | bytes 2097152 | tf_op jit(solution)/shard_map/forward_part/pallas_call | solution.py:98
  18.3 0.3 collective-permute-start.7
  18.7 8.9 %forward_part.5 = (bf16[3,2,1024,256]{3,2,1,0:T(8,128)(2,1)S(1)}, f32[3,2,1024,256]{3,2,1,0:T(8,128)S(1)}, f32[200,768]{1,0:T(8,128)S(1)}) custom-call(bf16[2,1024,2048]{2,1,0:T(8,128)(2,1)} %hid_ref.4, bf16[1024,1024]{1,0:T(8,128)(2,1)S(1)} %copy-done, f32[1,1024]{1,0:T(1,128)} %bitcast.85, bf16[100,1024]{1,0:T(8,128)(2,1)} %wo_ref.7, f32[1,100]{1,0:T(1,128)} %bitcast.88), custom_call_target="tpu_custom_call" | custom-call | flops 2097152 | bytes 2097152 | tf_op jit(solution)/shard_map/forward_part/pallas_call | solution.py:98
  27.6 1.3 collective-permute-start.1
  28.9 1.5 %collective-permute-start.2 = (f32[200,512]{1,0:T(8,128)S(1)}, f32[200,512]{1,0:T(8,128)S(1)}, u32[]{:S(2)}, u32[]{:S(2)}) collective-permute-start(f32[200,512]{1,0:T(8,128)S(1)} %get-tuple-element.50.refs_0_), channel_id=1, source_target_pairs={{0,8},{8,0},{16,24},{24,16},{1,9},{9,1},{17,25},{25,17},{2,10},{10... | collective-permute-start | bytes 1228808 | tf_op jit(solution)/shard_map/ppermute | solution.py:425
  30.4 0.5 collective-permute-start.6
  30.9 2.2 %transposes.1 = (bf16[1024,1024]{1,0:T(8,128)(2,1)S(1)}, bf16[1024,128]{1,0:T(8,128)(2,1)S(1)}) custom-call(bf16[1024,1024]{1,0:T(8,128)(2,1)S(1)} %copy-done, bf16[100,1024]{1,0:T(8,128)(2,1)} %wo_ref.7), custom_call_target="tpu_custom_call" | custom-call | flops 2048 | bytes 2048 | tf_op jit(solution)/shard_map/transposes/pallas_call | solution.py:343
  33.1 3.0 %collective-permute-start = (f32[200,768]{1,0:T(8,128)S(1)}, f32[200,768]{1,0:T(8,128)S(1)}, u32[]{:S(2)}, u32[]{:S(2)}) collective-permute-start(f32[200,768]{1,0:T(8,128)S(1)} %get-tuple-element.54.f_ref), channel_id=1, source_target_pairs={{0,8},{8,0},{16,24},{24,16},{1,9},{9,1},{17,25},{25,17},{2,10},{10... | collective-permute-start | bytes 1843208 | tf_op jit(solution)/shard_map/ppermute | solution.py:425
  36.2 6.7 %backward_part.3 = (bf16[2,1024,512]{2,1,0:T(8,128)(2,1)S(1)}, f32[128,1024]{1,0:T(8,128)S(1)}, f32[1024,1024]{1,0:T(8,128)S(1)}) custom-call(f32[200,512]{1,0:T(8,128)S(1)} %get-tuple-element.50.refs_0_, f32[200,512]{1,0:T(8,128)S(1)} %collective-permute-done.2.refs_1_, f32[200,512]{1,0:T(8,128)S(1)} %collective-permute-done.3.refs_2_, ...), custom_call_target="tpu_custom_call" | custom-call | flops 2097152 | bytes 2097152 | tf_op jit(solution)/shard_map/backward_part/pallas_call | solution.py:312
  42.9 3.0 %collective-permute-done.1.fx_ref = f32[200,768]{1,0:T(8,128)S(1)} collective-permute-done((f32[200,768]{1,0:T(8,128)S(1)}, f32[200,768]{1,0:T(8,128)S(1)}, u32[]{:S(2)}, u32[]{:S(2)}) %collective-permute-start.1) | collective-permute-done | bytes 614432 | tf_op jit(solution)/shard_map/ppermute | solution.py:424
  46.0 1.9 %collective-permute-start.5 = (f32[200,768]{1,0:T(8,128)S(1)}, f32[200,768]{1,0:T(8,128)S(1)}, u32[]{:S(2)}, u32[]{:S(2)}) collective-permute-start(f32[200,768]{1,0:T(8,128)S(1)} %collective-permute-done.1.fx_ref), channel_id=1, source_target_pairs={{0,8},{8,0},{16,24},{24,16},{1,9},{9,1},{17,25},{25,17},{2,10},{10... | collective-permute-start | bytes 1843208 | tf_op jit(solution)/shard_map/ppermute | solution.py:425
  47.9 8.8 %backward_part.4 = (bf16[3,1024,512]{2,1,0:T(8,128)(2,1)S(1)}, f32[128,1024]{1,0:T(8,128)S(1)}, f32[1024,1024]{1,0:T(8,128)S(1)}) custom-call(f32[200,768]{1,0:T(8,128)S(1)} %get-tuple-element.52.f_ref, f32[200,768]{1,0:T(8,128)S(1)} %collective-permute-done.6.fc_ref, ...), custom_call_target="tpu_custom_call", output_to_operand_aliasing={{2}: (11, {})} | custom-call | flops 2097152 | bytes 2097152 | tf_op jit(solution)/shard_map/backward_part/pallas_call | solution.py:312
  56.7 10.1 %backward_part.5 = (bf16[3,1024,512]{2,1,0:T(8,128)(2,1)S(1)}, f32[128,1024]{1,0:T(8,128)}, f32[1024,1024]{1,0:T(8,128)S(1)}, f32[2,2,4,72,256]{4,3,2,1,0:T(8,12...) custom-call(f32[200,768]{1,0:T(8,128)S(1)} %get-tuple-element.54.f_r, ...), custom_call_target="tpu_custom_call", output_to_operand_aliasing={{2}: (11, {})} | custom-call | flops 2097152 | bytes 2097152 | tf_op jit(solution)/shard_map/backward_part/pallas_call | solution.py:312
  66.8 0.5 collective-permute-start.9
  67.3 2.3 %collective-permute-done.10 = f32[2,2,4,72,256]{4,3,2,1,0:T(8,128)S(1)} collective-permute-done((f32[2,2,4,72,256]{4,3,2,1,0:T(8,128)S(1)}, f32[2,2,4,72,256]{4,3,2,1,0:T(8,128)S(1)}, u32[]{:S(2)}, u32[]{:S(2)}) %collective-permute-start.10) | collective-permute-done | bytes 1179680 | tf_op jit(solution)/shard_map/ppermute | solution.py:425
  69.6 0.1 fusion.4
  69.7 1.3 %collective-permute-start.12 = (f32[2,4,72,256]{3,2,1,0:T(8,128)S(1)}, f32[2,4,72,256]{3,2,1,0:T(8,128)S(1)}, u32[]{:S(2)}, u32[]{:S(2)}) collective-permute-start(f32[2,4,72,256]{3,2,1,0:T(8,128)S(1)} %fusion.4), channel_id=1, source_target_pairs={{0,1},{1,0},{2,3},{3,2},{4,5},{5,4},{6,7},{7,6},{8,9},{9,8},{10,11... | collective-permute-start | bytes 1769480 | tf_op jit(solution)/shard_map/ppermute | solution.py:426
  71.0 0.3 collective-permute-done.9
  71.4 0.3 collective-permute-start.11
  71.7 3.5 %grad_hidden_part.3.refs_0_ = bf16[2,1024,2048]{2,1,0:T(8,128)(2,1)} custom-call(bf16[1024,1024]{1,0:T(8,128)(2,1)S(1)} %get-tuple-element.56.wt_ref, bf16[2,1024,512]{2,1,0:T(8,128)(2,1)S(1)} %get-tuple-element.77.gp_ref), custom_call_target="tpu_custom_call" | custom-call | flops 2097152 | bytes 2097152 | tf_op jit(solution)/shard_map/grad_hidden_part/pallas_call | solution.py:383
  75.2 9.4 %collective-permute-done.12 = f32[2,4,72,256]{3,2,1,0:T(8,128)S(1)} collective-permute-done((f32[2,4,72,256]{3,2,1,0:T(8,128)S(1)}, f32[2,4,72,256]{3,2,1,0:T(8,128)S(1)}, u32[]{:S(2)}, u32[]{:S(2)}) %collective-permute-start.12) | collective-permute-done | bytes 589856 | tf_op jit(solution)/shard_map/ppermute | solution.py:426
  84.5 0.1 fusion.1
  84.7 0.3 collective-permute-start.14
  85.0 1.2 collective-permute-done.11
  86.2 0.1 fusion.3
  86.4 1.3 %collective-permute-start.13 = (f32[4,72,256]{2,1,0:T(8,128)S(1)}, f32[4,72,256]{2,1,0:T(8,128)S(1)}, u32[]{:S(2)}, u32[]{:S(2)}) collective-permute-start(f32[4,72,256]{2,1,0:T(8,128)S(1)} %get-tuple-element.91), channel_id=1, source_target_pairs={{0,1},{1,0},{2,3},{3,2},{4,5},{5,4},{6,7},{7,6},{8,9},{9,8},{10,11... | collective-permute-start | bytes 884744 | tf_op jit(solution)/shard_map/ppermute | solution.py:426
  87.7 4.8 %grad_hidden_part.4.refs_0_ = bf16[2,1024,2048]{2,1,0:T(8,128)(2,1)} custom-call(bf16[1024,1024]{1,0:T(8,128)(2,1)S(1)} %get-tuple-element.56.wt_ref, bf16[3,1024,512]{2,1,0:T(8,128)(2,1)S(1)} %get-tuple-element.80.gp_ref, bf16[2,1024,2048]{2,1,0:T(8,128)(2,1)} %grad_hidden_part.3.refs_0_), custom_call_target="tpu_custom_call", output_to_operand_aliasing={{}: (2, {})} | custom-call | flops 2097152 | bytes 2097152 | tf_op jit(solution)/shard_map/grad_hidden_part/pallas_call | solution.py:383
  92.6 1.5 %collective-permute-done.13 = f32[4,72,256]{2,1,0:T(8,128)S(1)} collective-permute-done((f32[4,72,256]{2,1,0:T(8,128)S(1)}, f32[4,72,256]{2,1,0:T(8,128)S(1)}, u32[]{:S(2)}, u32[]{:S(2)}) %collective-permute-start.13) | collective-permute-done | bytes 294944 | tf_op jit(solution)/shard_map/ppermute | solution.py:426
  94.2 0.2 collective-permute-start.17
  94.4 2.3 %collective-permute-start.16 = (f32[192,256]{1,0:T(8,128)S(1)}, f32[192,256]{1,0:T(8,128)S(1)}, u32[]{:S(2)}, u32[]{:S(2)}) collective-permute-start(f32[192,256]{1,0:T(8,128)S(1)} %get-tuple-element.110), channel_id=1, source_target_pairs={{0,4},{1,5},{2,6},{3,7},{4,0},{5,1},{6,2},{7,3},{8,12},{9,13},{10,... | collective-permute-start | bytes 589832 | tf_op jit(solution)/shard_map/ppermute | solution.py:427
  96.7 2.2 %collective-permute-start.15 = (f32[192,256]{1,0:T(8,128)S(1)}, f32[192,256]{1,0:T(8,128)S(1)}, u32[]{:S(2)}, u32[]{:S(2)}) collective-permute-start(f32[192,256]{1,0:T(8,128)S(1)} %get-tuple-element.112), channel_id=1, source_target_pairs={{0,2},{1,3},{2,4},{3,5},{4,6},{5,7},{6,0},{7,1},{8,10},{9,11},{10,... | collective-permute-start | bytes 589832 | tf_op jit(solution)/shard_map/ppermute | solution.py:427
  98.9 4.7 %grad_hidden_part.5 = bf16[2,1024,2048]{2,1,0:T(8,128)(2,1)} custom-call(bf16[1024,1024]{1,0:T(8,128)(2,1)S(1)} %get-tuple-element.56.wt_ref, bf16[3,1024,512]{2,1,0:T(8,128)(2,1)S(1)} %get-tuple-element.84.gp_ref, bf16[2,1024,2048]{2,1,0:T(8,128)(2,1)} %grad_hidden_part.4.refs_0_), custom_call_target="tpu_custom_call", output_to_operand_aliasing={{}: (2, {})} | custom-call | flops 2097152 | bytes 2097152 | tf_op jit(solution)/shard_map/grad_hidden_part/pallas_call | solution.py:383
  103.6 5.2 %collective-permute-done.16 = f32[192,256]{1,0:T(8,128)S(1)} collective-permute-done((f32[192,256]{1,0:T(8,128)S(1)}, f32[192,256]{1,0:T(8,128)S(1)}, u32[]{:S(2)}, u32[]{:S(2)}) %collective-permute-start.16) | collective-permute-done | bytes 196640 | tf_op jit(solution)/shard_map/ppermute | solution.py:427
  108.8 4.4 %collective-permute-done.15 = f32[192,256]{1,0:T(8,128)S(1)} collective-permute-done((f32[192,256]{1,0:T(8,128)S(1)}, f32[192,256]{1,0:T(8,128)S(1)}, u32[]{:S(2)}, u32[]{:S(2)}) %collective-permute-start.15) | collective-permute-done | bytes 196640 | tf_op jit(solution)/shard_map/ppermute | solution.py:427
  113.3 1.2 collective-permute-start.20
  114.5 0.2 collective-permute-start.19
  114.7 1.3 collective-permute-start.18
  116.0 1.4 %collective-permute-done.20 = f32[1,64,256]{2,1,0:T(8,128)S(1)} collective-permute-done((f32[1,64,256]{2,1,0:T(8,128)S(1)}, f32[1,64,256]{2,1,0:T(8,128)S(1)}, u32[]{:S(2)}, u32[]{:S(2)}) %collective-permute-start.20) | collective-permute-done | bytes 65568 | tf_op jit(solution)/shard_map/ppermute | solution.py:513
  117.4 0.7 collective-permute-done.19
  118.1 2.8 %collective-permute-done.18 = f32[192,256]{1,0:T(8,128)S(1)} collective-permute-done((f32[192,256]{1,0:T(8,128)S(1)}, f32[192,256]{1,0:T(8,128)S(1)}, u32[]{:S(2)}, u32[]{:S(2)}) %collective-permute-start.18) | collective-permute-done | bytes 196640 | tf_op jit(solution)/shard_map/ppermute | solution.py:424
  120.9 2.3 %collective-permute-start.21 = (f32[1,2,2,64,256]{4,3,2,1,0:T(8,128)S(1)}, f32[1,2,2,64,256]{4,3,2,1,0:T(8,128)S(1)}, u32[]{:S(2)}, u32[]{:S(2)}) collective-permute-start(f32[1,2,2,64,256]{4,3,2,1,0:T(8,128)S(1)} %maximum_select_fusion.3), channel_id=1, source_target_pairs={{0,8},{8,0},{16,24},{24,16},{1,9},{9,1},{17,25},{25,17},{2,10},{10... | collective-permute-start | bytes 786440 | tf_op jit(solution)/shard_map/ppermute | solution.py:473
  123.3 0.1 collective-permute-start.22
  123.4 1.0 collective-permute-done.21
  124.5 0.6 slice_reduce_fusion
  125.7 0.8 slice_multiply_fusion
  126.5 0.8 maximum_select_fusion.1
  (45 shorter events, 0.8 us)
Async XLA Ops:
  0.6 8.8 %copy-start = (bf16[1024,1024]{1,0:T(8,128)(2,1)S(1)}, bf16[1024,1024]{1,0:T(8,128)(2,1)}, u32[]{:S(2)}) copy-start(bf16[1024,1024]{1,0:T(8,128)(2,1)} %w_ref.6) | copy-start | bytes 6291460
  8.2 22.3 %collective-permute-start.3 = (f32[200,512]{1,0:T(8,128)S(1)}, f32[200,512]{1,0:T(8,128)S(1)}, u32[]{:S(2)}, u32[]{:S(2)}) collective-permute-start(f32[200,512]{1,0:T(8,128)S(1)} %get-tuple-element.50.refs_0_), channel_id=1, source_target_pairs={{0,16},{8,24},{16,0},{24,8},{1,17},{9,25},{17,1},{25,9},{2,18},{10... | collective-permute-start | bytes 1228808 | tf_op jit(solution)/shard_map/ppermute | solution.py:424
  18.3 14.8 %collective-permute-start.7 = (f32[200,768]{1,0:T(8,128)S(1)}, f32[200,768]{1,0:T(8,128)S(1)}, u32[]{:S(2)}, u32[]{:S(2)}) collective-permute-start(f32[200,768]{1,0:T(8,128)S(1)} %get-tuple-element.52.f_ref), channel_id=1, source_target_pairs={{0,16},{8,24},{16,0},{24,8},{1,17},{9,25},{17,1},{25,9},{2,18},{10... | collective-permute-start | bytes 1843208 | tf_op jit(solution)/shard_map/ppermute | solution.py:424
  27.6 8.6 %copy-start.1 = (f32[100,2048]{1,0:T(8,128)S(1)}, f32[100,2048]{1,0:T(8,128)}, u32[]{:S(2)}) copy-start(f32[100,2048]{1,0:T(8,128)} %target_ref.3) | copy-start | bytes 2457604
  27.6 8.6 %copy-start.2 = (f32[2048]{0:T(1024)S(1)}, f32[2048]{0:T(1024)}, u32[]{:S(2)}) copy-start(f32[2048]{0:T(1024)} %param.10) | copy-start | bytes 24580
  27.6 8.6 %copy-start.3 = (f32[100]{0:T(128)S(1)}, f32[100]{0:T(128)}, u32[]{:S(2)}) copy-start(f32[100]{0:T(128)} %param.11) | copy-start | bytes 1204
  27.6 18.4 %collective-permute-start.1 = (f32[200,768]{1,0:T(8,128)S(1)}, f32[200,768]{1,0:T(8,128)S(1)}, u32[]{:S(2)}, u32[]{:S(2)}) collective-permute-start(f32[200,768]{1,0:T(8,128)S(1)} %get-tuple-element.54.f_ref), channel_id=1, source_target_pairs={{0,16},{8,24},{16,0},{24,8},{1,17},{9,25},{17,1},{25,9},{2,18},{10... | collective-permute-start | bytes 1843208 | tf_op jit(solution)/shard_map/ppermute | solution.py:424
  28.9 7.3 %collective-permute-start.2 = (f32[200,512]{1,0:T(8,128)S(1)}, f32[200,512]{1,0:T(8,128)S(1)}, u32[]{:S(2)}, u32[]{:S(2)}) collective-permute-start(f32[200,512]{1,0:T(8,128)S(1)} %get-tuple-element.50.refs_0_), channel_id=1, source_target_pairs={{0,8},{8,0},{16,24},{24,16},{1,9},{9,1},{17,25},{25,17},{2,10},{10... | collective-permute-start | bytes 1228808 | tf_op jit(solution)/shard_map/ppermute | solution.py:425
  30.4 5.7 %collective-permute-start.4 = (f32[200,512]{1,0:T(8,128)S(1)}, f32[200,512]{1,0:T(8,128)S(1)}, u32[]{:S(2)}, u32[]{:S(2)}) collective-permute-start(f32[200,512]{1,0:T(8,128)S(1)} %collective-permute-done.3.refs_2_), channel_id=1, source_target_pairs={{0,8},{8,0},{16,24},{24,16},{1,9},{9,1},{17,25},{25,17},{2,10},{10... | collective-permute-start | bytes 1228808 | tf_op jit(solution)/shard_map/ppermute | solution.py:425
  30.4 17.4 %collective-permute-start.6 = (f32[200,768]{1,0:T(8,128)S(1)}, f32[200,768]{1,0:T(8,128)S(1)}, u32[]{:S(2)}, u32[]{:S(2)}) collective-permute-start(f32[200,768]{1,0:T(8,128)S(1)} %get-tuple-element.52.f_ref), channel_id=1, source_target_pairs={{0,8},{8,0},{16,24},{24,16},{1,9},{9,1},{17,25},{25,17},{2,10},{10... | collective-permute-start | bytes 1843208 | tf_op jit(solution)/shard_map/ppermute | solution.py:425
  33.1 23.5 %collective-permute-start = (f32[200,768]{1,0:T(8,128)S(1)}, f32[200,768]{1,0:T(8,128)S(1)}, u32[]{:S(2)}, u32[]{:S(2)}) collective-permute-start(f32[200,768]{1,0:T(8,128)S(1)} %get-tuple-element.54.f_ref), channel_id=1, source_target_pairs={{0,8},{8,0},{16,24},{24,16},{1,9},{9,1},{17,25},{25,17},{2,10},{10... | collective-permute-start | bytes 1843208 | tf_op jit(solution)/shard_map/ppermute | solution.py:425
  36.2 11.7 %collective-permute-start.8 = (f32[200,768]{1,0:T(8,128)S(1)}, f32[200,768]{1,0:T(8,128)S(1)}, u32[]{:S(2)}, u32[]{:S(2)}) collective-permute-start(f32[200,768]{1,0:T(8,128)S(1)} %collective-permute-done.7.fx_ref), channel_id=1, source_target_pairs={{0,8},{8,0},{16,24},{24,16},{1,9},{9,1},{17,25},{25,17},{2,10},{10... | collective-permute-start | bytes 1843208 | tf_op jit(solution)/shard_map/ppermute | solution.py:425
  46.0 10.7 %collective-permute-start.5 = (f32[200,768]{1,0:T(8,128)S(1)}, f32[200,768]{1,0:T(8,128)S(1)}, u32[]{:S(2)}, u32[]{:S(2)}) collective-permute-start(f32[200,768]{1,0:T(8,128)S(1)} %collective-permute-done.1.fx_ref), channel_id=1, source_target_pairs={{0,8},{8,0},{16,24},{24,16},{1,9},{9,1},{17,25},{25,17},{2,10},{10... | collective-permute-start | bytes 1843208 | tf_op jit(solution)/shard_map/ppermute | solution.py:425
  66.8 2.8 %collective-permute-start.10 = (f32[2,2,4,72,256]{4,3,2,1,0:T(8,128)S(1)}, f32[2,2,4,72,256]{4,3,2,1,0:T(8,128)S(1)}, u32[]{:S(2)}, u32[]{:S(2)}) collective-permute-start(f32[2,2,4,72,256]{4,3,2,1,0:T(8,128)S(1)} %get-tuple-element.76), channel_id=1, source_target_pairs={{0,8},{8,0},{16,24},{24,16},{1,9},{9,1},{17,25},{25,17},{2,10},{10... | collective-permute-start | bytes 3538952 | tf_op jit(solution)/shard_map/ppermute | solution.py:425
  66.8 4.5 %collective-permute-start.9 = (f32[2,2,4,72,256]{4,3,2,1,0:T(8,128)S(1)}, f32[2,2,4,72,256]{4,3,2,1,0:T(8,128)S(1)}, u32[]{:S(2)}, u32[]{:S(2)}) collective-permute-start(f32[2,2,4,72,256]{4,3,2,1,0:T(8,128)S(1)} %get-tuple-element.74), channel_id=1, source_target_pairs={{0,8},{8,0},{16,24},{24,16},{1,9},{9,1},{17,25},{25,17},{2,10},{10... | collective-permute-start | bytes 3538952 | tf_op jit(solution)/shard_map/ppermute | solution.py:425
  69.7 14.9 %collective-permute-start.12 = (f32[2,4,72,256]{3,2,1,0:T(8,128)S(1)}, f32[2,4,72,256]{3,2,1,0:T(8,128)S(1)}, u32[]{:S(2)}, u32[]{:S(2)}) collective-permute-start(f32[2,4,72,256]{3,2,1,0:T(8,128)S(1)} %fusion.4), channel_id=1, source_target_pairs={{0,1},{1,0},{2,3},{3,2},{4,5},{5,4},{6,7},{7,6},{8,9},{9,8},{10,11... | collective-permute-start | bytes 1769480 | tf_op jit(solution)/shard_map/ppermute | solution.py:426
  71.4 14.9 %collective-permute-start.11 = (f32[2,4,72,256]{3,2,1,0:T(8,128)S(1)}, f32[2,4,72,256]{3,2,1,0:T(8,128)S(1)}, u32[]{:S(2)}, u32[]{:S(2)}) collective-permute-start(f32[2,4,72,256]{3,2,1,0:T(8,128)S(1)} %fusion.5), channel_id=1, source_target_pairs={{0,16},{8,24},{16,0},{24,8},{1,17},{9,25},{17,1},{25,9},{2,18},{10... | collective-permute-start | bytes 1769480 | tf_op jit(solution)/shard_map/ppermute | solution.py:424
  84.7 7.8 %collective-permute-start.14 = (f32[4,72,256]{2,1,0:T(8,128)S(1)}, f32[4,72,256]{2,1,0:T(8,128)S(1)}, u32[]{:S(2)}, u32[]{:S(2)}) collective-permute-start(f32[4,72,256]{2,1,0:T(8,128)S(1)} %get-tuple-element.89), channel_id=1, source_target_pairs={{0,16},{8,24},{16,0},{24,8},{1,17},{9,25},{17,1},{25,9},{2,18},{10... | collective-permute-start | bytes 884744 | tf_op jit(solution)/shard_map/ppermute | solution.py:424
  86.4 7.6 %collective-permute-start.13 = (f32[4,72,256]{2,1,0:T(8,128)S(1)}, f32[4,72,256]{2,1,0:T(8,128)S(1)}, u32[]{:S(2)}, u32[]{:S(2)}) collective-permute-start(f32[4,72,256]{2,1,0:T(8,128)S(1)} %get-tuple-element.91), channel_id=1, source_target_pairs={{0,1},{1,0},{2,3},{3,2},{4,5},{5,4},{6,7},{7,6},{8,9},{9,8},{10,11... | collective-permute-start | bytes 884744 | tf_op jit(solution)/shard_map/ppermute | solution.py:426
  94.2 9.5 %collective-permute-start.17 = (f32[192,256]{1,0:T(8,128)S(1)}, f32[192,256]{1,0:T(8,128)S(1)}, u32[]{:S(2)}, u32[]{:S(2)}) collective-permute-start(f32[192,256]{1,0:T(8,128)S(1)} %get-tuple-element.111), channel_id=1, source_target_pairs={{0,6},{1,7},{2,0},{3,1},{4,2},{5,3},{6,4},{7,5},{8,14},{9,15},{10,... | collective-permute-start | bytes 589832 | tf_op jit(solution)/shard_map/ppermute | solution.py:427
  94.4 14.4 %collective-permute-start.16 = (f32[192,256]{1,0:T(8,128)S(1)}, f32[192,256]{1,0:T(8,128)S(1)}, u32[]{:S(2)}, u32[]{:S(2)}) collective-permute-start(f32[192,256]{1,0:T(8,128)S(1)} %get-tuple-element.110), channel_id=1, source_target_pairs={{0,4},{1,5},{2,6},{3,7},{4,0},{5,1},{6,2},{7,3},{8,12},{9,13},{10,... | collective-permute-start | bytes 589832 | tf_op jit(solution)/shard_map/ppermute | solution.py:427
  96.7 16.5 %collective-permute-start.15 = (f32[192,256]{1,0:T(8,128)S(1)}, f32[192,256]{1,0:T(8,128)S(1)}, u32[]{:S(2)}, u32[]{:S(2)}) collective-permute-start(f32[192,256]{1,0:T(8,128)S(1)} %get-tuple-element.112), channel_id=1, source_target_pairs={{0,2},{1,3},{2,4},{3,5},{4,6},{5,7},{6,0},{7,1},{8,10},{9,11},{10,... | collective-permute-start | bytes 589832 | tf_op jit(solution)/shard_map/ppermute | solution.py:427
  113.3 4.1 %collective-permute-start.20 = (f32[1,64,256]{2,1,0:T(8,128)S(1)}, f32[1,64,256]{2,1,0:T(8,128)S(1)}, u32[]{:S(2)}, u32[]{:S(2)}) collective-permute-start(f32[1,64,256]{2,1,0:T(8,128)S(1)} %get-tuple-element.101), channel_id=1, source_target_pairs={{0,17},{1,16},{2,19},{3,18},{4,21},{5,20},{6,23},{7,22},{8,25},{9,... | collective-permute-start | bytes 196616 | tf_op jit(solution)/shard_map/ppermute | solution.py:513
  114.5 3.6 %collective-permute-start.19 = (f32[1,64,256]{2,1,0:T(8,128)S(1)}, f32[1,64,256]{2,1,0:T(8,128)S(1)}, u32[]{:S(2)}, u32[]{:S(2)}) collective-permute-start(f32[1,64,256]{2,1,0:T(8,128)S(1)} %get-tuple-element.101), channel_id=1, source_target_pairs={{0,1},{1,0},{2,3},{3,2},{4,5},{5,4},{6,7},{7,6},{8,9},{9,8},{10,11... | collective-permute-start | bytes 196616 | tf_op jit(solution)/shard_map/ppermute | solution.py:511
  114.7 6.1 %collective-permute-start.18 = (f32[192,256]{1,0:T(8,128)S(1)}, f32[192,256]{1,0:T(8,128)S(1)}, u32[]{:S(2)}, u32[]{:S(2)}) collective-permute-start(f32[192,256]{1,0:T(8,128)S(1)} %add_add_fusion), channel_id=1, source_target_pairs={{0,16},{8,24},{16,0},{24,8},{1,17},{9,25},{17,1},{25,9},{2,18},{10... | collective-permute-start | bytes 589832 | tf_op jit(solution)/shard_map/ppermute | solution.py:424
  120.9 3.4 %collective-permute-start.21 = (f32[1,2,2,64,256]{4,3,2,1,0:T(8,128)S(1)}, f32[1,2,2,64,256]{4,3,2,1,0:T(8,128)S(1)}, u32[]{:S(2)}, u32[]{:S(2)}) collective-permute-start(f32[1,2,2,64,256]{4,3,2,1,0:T(8,128)S(1)} %maximum_select_fusion.3), channel_id=1, source_target_pairs={{0,8},{8,0},{16,24},{24,16},{1,9},{9,1},{17,25},{25,17},{2,10},{10... | collective-permute-start | bytes 786440 | tf_op jit(solution)/shard_map/ppermute | solution.py:473
  123.3 3.3 %collective-permute-start.22 = (f32[64,1024]{1,0:T(8,128)S(1)}, f32[64,1024]{1,0:T(8,128)S(1)}, u32[]{:S(2)}, u32[]{:S(2)}) collective-permute-start(f32[64,1024]{1,0:T(8,128)S(1)} %maximum_multiply_fusion), channel_id=1, source_target_pairs={{0,8},{8,0},{16,24},{24,16},{1,9},{9,1},{17,25},{25,17},{2,10},{10... | collective-permute-start | bytes 786440 | tf_op jit(solution)/shard_map/ppermute | solution.py:473
where the time goes:
time: 131 us; the launch traced here: 129 us
  Pallas kernels  66.1 us (50%)
  waiting for transfers between devices  33.1 us (25%)
  starting transfers between devices  23.3 us (18%)
  other arithmetic  3.04 us (2%)
  between operations  2.73 us (2%)
    pallas_call x3, Pallas kernels, backward(): pl.pallas_call(kernel_fn, grid=(steps + 1,), in_specs=in_specs, out_specs...  25.6 us
    pallas_call x3, Pallas kernels, forward(): pl.pallas_call(forward_kernel, grid=(tiles + 1,), in_specs=[pl.BlockSpec(...  25.3 us
    pallas_call x3, Pallas kernels, input_gradient(): pl.pallas_call(input_kernel, grid=(steps,), in_specs=in_specs, out_specs=...  13 us
    ppermute x2, waiting for transfers between devices, shards(): to_lo = lambda a, k: lax.ppermute(a, 'grid', shift_lo(k))  10.8 us
    ppermute x3, waiting for transfers between devices, shards(): to_hi = lambda a, k: lax.ppermute(a, 'grid', shift_hi(k))  9.55 us
    ppermute x8, starting transfers between devices, shards(): to_core = lambda a: lax.ppermute(a, 'mem', swap_core)  7.42 us
    ppermute x6, waiting for transfers between devices, shards(): to_x = lambda a: lax.ppermute(a, 'mem', swap_x)  7 us
    ppermute x6, starting transfers between devices, shards(): to_x = lambda a: lax.ppermute(a, 'mem', swap_x)  4.76 us
  transfers between devices with their start and end apart: 23, of which 12 were waited for; matrix products, arithmetic and copies ran while one was open for 2% of the time, Pallas kernels for 38%

commit v1 on v0

--- a/solution.py
+++ b/solution.py
@@ -8,7 +8,7 @@
 from jax.experimental.pallas import tpu as pltpu
 from jax.sharding import PartitionSpec as P
 
-EIGHTHS = (2, 3, 3)
+EIGHTHS = (2, 2, 2, 2)
 TILE = 256
 EPS = 0.0004
 K0 = math.sqrt(2.0 / math.pi)
@@ -32,9 +32,8 @@
     return pl.ds(mloc * full + m * (v - full), v - full)
 
 
-def forward_kernel(hid_ref, w_ref, b_ref, wo_ref, bo_ref, act_ref, slope_ref, f_ref, bias, half, fields, *slabs):
+def forward_kernel(hid_ref, w_ref, b_ref, wo_ref, bo_ref, act_ref, slope_ref, f_ref, bias, half, *slabs):
     step = pl.program_id(0)
-    last = pl.num_programs(0) - 1
     mloc, h, t = hid_ref.shape
     v = half.shape[0]
     size = h // len(slabs)
@@ -47,43 +46,29 @@
             )
         half[...] = wo_ref[...] * jnp.bfloat16(0.5)
 
-    def multiply(k):
-        hid = jnp.concatenate([hid_ref[m] for m in range(mloc)], axis=1)
+    hid = jnp.concatenate([hid_ref[m] for m in range(mloc)], axis=1)
+    for k, slab in enumerate(slabs):
         rows = pl.ds(k * size, size)
-        slabs[k][...] = jnp.dot(w_ref[rows, :], hid, preferred_element_type=jnp.float32)
-
-    def gelu(tile, k):
+        slab[...] = jnp.dot(w_ref[rows, :], hid, preferred_element_type=jnp.float32)
+    out = jnp.broadcast_to(column(bo_ref[...], v), (v, mloc * t))
+    for k, slab in enumerate(slabs):
         for r in range(0, size, 16):
             rows = pl.ds(k * size + r, 16)
             b = jnp.concatenate([bias[rows, :]] * (t // 128), axis=1)
             for m in range(mloc):
-                x = slabs[k][pl.ds(r, 16), pl.ds(m * t, t)] + b
+                x = slab[pl.ds(r, 16), pl.ds(m * t, t)] + b
                 q = x * x * K1
                 th = jnp.tanh(x * (K0 + q))
                 up = 1.0 + th
                 act = x * up
-                act_ref[tile, m, rows, :] = act.astype(jnp.bfloat16)
-                slope_ref[tile, m, rows, :] = up + act * ((1.0 - th) * (K0 + 3.0 * q))
+                act_ref[step, m, rows, :] = act.astype(jnp.bfloat16)
+                slope_ref[step, m, rows, :] = up + act * ((1.0 - th) * (K0 + 3.0 * q))
         rows = pl.ds(k * size, size)
-        act = jnp.concatenate([act_ref[tile, m, rows, :] for m in range(mloc)], axis=1)
-        return jnp.dot(half[:, rows], act, preferred_element_type=jnp.float32)
-
-    def finish():
-        out = fields[...] + gelu(lax.max(step - 1, 0), 1)
-        for m in range(mloc):
-            for r0 in range(0, v, 8):
-                f_ref[field_rows(v, mloc, m, r0), :] = out[r0 : r0 + 8, m * t : (m + 1) * t]
-
-    @pl.when(step < last)
-    def _():
-        multiply(0)
-        finish()
-        multiply(1)
-        fields[...] = gelu(step, 0) + column(bo_ref[...], v)
-
-    @pl.when(step == last)
-    def _():
-        finish()
+        act = jnp.concatenate([act_ref[step, m, rows, :] for m in range(mloc)], axis=1)
+        out = out + jnp.dot(half[:, rows], act, preferred_element_type=jnp.float32)
+    for m in range(mloc):
+        for r0 in range(0, v, 8):
+            f_ref[field_rows(v, mloc, m, r0), :] = out[r0 : r0 + 8, m * t : (m + 1) * t]
 
 
 def forward(start, p, hidden, w_inner, b_inner, w_out, b_out, vmem):
@@ -97,9 +82,9 @@
     held = pl.BlockSpec(shape, lambda s: (0, 0, 0, 0))
     return pl.pallas_call(
         forward_kernel,
-        grid=(tiles + 1,),
+        grid=(tiles,),
         in_specs=[
-            pl.BlockSpec((mloc, h, t), lambda s: (0, 0, start // t + jnp.minimum(s, tiles - 1))),
+            pl.BlockSpec((mloc, h, t), lambda s: (0, 0, start // t + s)),
             pl.BlockSpec((h, h), whole, pipeline_mode=once),
             pl.BlockSpec((1, h), whole, pipeline_mode=once),
             pl.BlockSpec((v, h), whole, pipeline_mode=once),
@@ -108,7 +93,7 @@
         out_specs=[
             held,
             held,
-            pl.BlockSpec((mloc * v, t), lambda s: (0, jnp.maximum(s - 1, 0))),
+            pl.BlockSpec((mloc * v, t), lambda s: (0, s)),
         ],
         out_shape=[
             pltpu.VMEM(shape, jnp.bfloat16),
@@ -118,7 +103,6 @@
         scratch_shapes=[
             pltpu.VMEM((h, 128), jnp.float32),
             pltpu.VMEM((v, h), jnp.bfloat16),
-            pltpu.VMEM((v, mloc * t), jnp.float32),
             pltpu.VMEM((h // 2, mloc * t), jnp.float32),
             pltpu.VMEM((h // 2, mloc * t), jnp.float32),
         ],
@@ -492,19 +476,20 @@
     out_y = [keep_y[k] + got_y[k] for k in others]
     from_x = to_x(out_x)
     from_y = [to_lo(out_y[k - 1], k) for k in others]
-    gh, (keep_x, keep_y) = beside(0, gh, (out_x, out_y), (keep_x, keep_y))
+    for k in (0, 1):
+        gh, (keep_x, keep_y) = beside(k, gh, (out_x, out_y), (keep_x, keep_y))
     own_x = keep_x[0] + got_x[0] + from_x
     own_y = sum(from_y, keep_y[0] + got_y[0])
     own_x, own_y = [own_x[k] for k in range(n_lo)], [own_y[k] for k in range(2)]
     from_y = [to_lo(own_x[k], k) for k in others]
     from_x = to_x(own_y[1])
-    gh, (own_x, own_y) = beside(1, gh, (own_x[1:], own_y[1]), (own_x[0], own_y[0]))
+    gh, (own_x, own_y) = beside(2, gh, (own_x[1:], own_y[1]), (own_x[0], own_y[0]))
     sums = [sum(from_y, own_x), own_y + from_x]
 
     extra = [part[:, r:].reshape(-1, cx) for part in sums]
     pieces = [jnp.concatenate([part[k, :r] for part in sums] + extra, 0) for k in range(n_hi)]
     from_hi = [to_hi(pieces[k], k) for k in range(1, n_hi)]
-    gh, own = beside(2, gh, pieces[1:], pieces[0])
+    gh, own = beside(3, gh, pieces[1:], pieces[0])
     total = sum(from_hi, own)
     far = to_x(total)
     mine = total[2 * r :][None]

time: 131 us -> 129 us (0.985); the launches traced: 129 us -> 129 us
  Pallas kernels: 66.1 us -> 68 us
    ppermute x2, waiting for transfers between devices: 10.8 us -> 1.2 us  [shards(): to_lo = lambda a, k: lax.ppermute(a, 'grid', shift_lo(k))]
    ppermute x6 -> x7, waiting for transfers between devices: 7 us -> 11.6 us  [shards(): to_x = lambda a: lax.ppermute(a, 'mem', swap_x)]
    ppermute x3, waiting for transfers between devices: 9.55 us -> 13.1 us  [shards(): to_hi = lambda a, k: lax.ppermute(a, 'grid', shift_hi(k))]
    pallas_call x3 -> x4, Pallas kernels: 25.6 us -> 27 us  [backward(): pl.pallas_call(kernel_fn, grid=(steps + 1,), in_specs=in_specs, out_specs...]
    ppermute x8 -> x10, starting transfers between devices: 7.42 us -> 6.09 us  [shards(): to_core = lambda a: lax.ppermute(a, 'mem', swap_core)]
    ppermute x6 -> x7, starting transfers between devices: 4.76 us -> 5.91 us  [shards(): to_x = lambda a: lax.ppermute(a, 'mem', swap_x)]
    pallas_call x3 -> x4, Pallas kernels: 13 us -> 13.9 us  [input_gradient(): pl.pallas_call(input_kernel, grid=(steps,), in_specs=in_specs, out_specs=...]
    pallas_call x3 -> x4, Pallas kernels: 25.3 us -> 25 us  [forward(): pl.pallas_call(forward_kernel, grid=(tiles,), in_specs=[pl.BlockSpec((mlo...]
  transfers between devices with their start and end apart: 23 -> 26, of which waited for: 12 -> 13; matrix products, arithmetic and copies ran while one was open for 2% -> 2% of each run, Pallas kernels for 38% -> 42%
where the time goes in v1:
time: 129 us
  Pallas kernels  68 us (53%)
  waiting for transfers between devices  32.2 us (25%)
  starting transfers between devices  22.3 us (17%)
  other arithmetic  3 us (2%)
  between operations  2.76 us (2%)
    pallas_call x4, Pallas kernels, backward(): pl.pallas_call(kernel_fn, grid=(steps + 1,), in_specs=in_specs, out_specs...  27 us
    pallas_call x4, Pallas kernels, forward(): pl.pallas_call(forward_kernel, grid=(tiles,), in_specs=[pl.BlockSpec((mlo...  25 us
    pallas_call x4, Pallas kernels, input_gradient(): pl.pallas_call(input_kernel, grid=(steps,), in_specs=in_specs, out_specs=...  13.9 us
    ppermute x3, waiting for transfers between devices, shards(): to_hi = lambda a, k: lax.ppermute(a, 'grid', shift_hi(k))  13.1 us
    ppermute x7, waiting for transfers between devices, shards(): to_x = lambda a: lax.ppermute(a, 'mem', swap_x)  11.6 us
    ppermute x10, starting transfers between devices, shards(): to_core = lambda a: lax.ppermute(a, 'mem', swap_core)  6.09 us
    ppermute x7, starting transfers between devices, shards(): to_x = lambda a: lax.ppermute(a, 'mem', swap_x)  5.91 us
    ppermute x3, starting transfers between devices, shards(): to_hi = lambda a, k: lax.ppermute(a, 'grid', shift_hi(k))  3.83 us
  transfers between devices with their start and end apart: 26, of which 13 were waited for; matrix products, arithmetic and copies ran while one was open for 2% of the time, Pallas kernels for 42%

profile of v1, /device:TPU:9, one launch (start us, length us, event | category | flops | bytes accessed | tf_op | source)
XLA Modules:
  0.0 128.6 jit_solution(9512317694275841283)
XLA Ops:
  0.7 6.9 %forward_part.4 = (bf16[2,2,1024,256]{3,2,1,0:T(8,128)(2,1)S(1)}, f32[2,2,1024,256]{3,2,1,0:T(8,128)S(1)}, f32[200,512]{1,0:T(8,128)S(1)}) custom-call(bf16[2,1024,2048]{2,1,0:T(8,128)(2,1)} %hid_ref.6, bf16[1024,1024]{1,0:T(8,128)(2,1)} %w_ref.8, f32[1,1024]{1,0:T(1,128)} %bitcast.85, bf16[100,1024]{1,0:T(8,128)(2,1)} %wo_ref.9, f32[1,100]{1,0:T(1,128)} %bitcast.89), custom_call_target="tpu_custom_call" | custom-call | flops 2097152 | bytes 2097152 | tf_op jit(solution)/shard_map/forward_part/pallas_call | solution.py:83
  7.6 1.3 collective-permute-start.6
  8.9 6.0 %forward_part.5 = (bf16[2,2,1024,256]{3,2,1,0:T(8,128)(2,1)S(1)}, f32[2,2,1024,256]{3,2,1,0:T(8,128)S(1)}, f32[200,512]{1,0:T(8,128)S(1)}) custom-call(bf16[2,1024,2048]{2,1,0:T(8,128)(2,1)} %hid_ref.6, bf16[1024,1024]{1,0:T(8,128)(2,1)S(1)} %copy-done, f32[1,1024]{1,0:T(1,128)} %bitcast.86, bf16[100,1024]{1,0:T(8,128)(2,1)} %wo_ref.9, f32[1,100]{1,0:T(1,128)} %bitcast.90), custom_call_target="tpu_custom_call" | custom-call | flops 2097152 | bytes 2097152 | tf_op jit(solution)/shard_map/forward_part/pallas_call | solution.py:83
  14.9 0.3 collective-permute-start.3
  15.2 1.2 collective-permute-start.5
  16.5 1.5 %collective-permute-done.6.refs_2_ = f32[200,512]{1,0:T(8,128)S(1)} collective-permute-done((f32[200,512]{1,0:T(8,128)S(1)}, f32[200,512]{1,0:T(8,128)S(1)}, u32[]{:S(2)}, u32[]{:S(2)}) %collective-permute-start.6) | collective-permute-done | bytes 409632 | tf_op jit(solution)/shard_map/ppermute | solution.py:408
  18.0 2.7 %collective-permute-start.7 = (f32[200,512]{1,0:T(8,128)S(1)}, f32[200,512]{1,0:T(8,128)S(1)}, u32[]{:S(2)}, u32[]{:S(2)}) collective-permute-start(f32[200,512]{1,0:T(8,128)S(1)} %collective-permute-done.6.refs_2_), channel_id=1, source_target_pairs={{0,8},{8,0},{16,24},{24,16},{1,9},{9,1},{17,25},{25,17},{2,10},{10... | collective-permute-start | bytes 1228808 | tf_op jit(solution)/shard_map/ppermute | solution.py:409
  20.7 6.0 %forward_part.6 = (bf16[2,2,1024,256]{3,2,1,0:T(8,128)(2,1)S(1)}, f32[2,2,1024,256]{3,2,1,0:T(8,128)S(1)}, f32[200,512]{1,0:T(8,128)S(1)}) custom-call(bf16[2,1024,2048]{2,1,0:T(8,128)(2,1)} %hid_ref.6, bf16[1024,1024]{1,0:T(8,128)(2,1)S(1)} %copy-done, f32[1,1024]{1,0:T(1,128)} %bitcast.87, bf16[100,1024]{1,0:T(8,128)(2,1)} %wo_ref.9, f32[1,100]{1,0:T(1,128)} %bitcast.91), custom_call_target="tpu_custom_call" | custom-call | flops 2097152 | bytes 2097152 | tf_op jit(solution)/shard_map/forward_part/pallas_call | solution.py:83
  26.7 1.3 collective-permute-start.10
  28.0 6.0 %forward_part.7 = (bf16[2,2,1024,256]{3,2,1,0:T(8,128)(2,1)S(1)}, f32[2,2,1024,256]{3,2,1,0:T(8,128)S(1)}, f32[200,512]{1,0:T(8,128)S(1)}) custom-call(bf16[2,1024,2048]{2,1,0:T(8,128)(2,1)} %hid_ref.6, bf16[1024,1024]{1,0:T(8,128)(2,1)S(1)} %copy-done, f32[1,1024]{1,0:T(1,128)} %bitcast.88, bf16[100,1024]{1,0:T(8,128)(2,1)} %wo_ref.9, f32[1,100]{1,0:T(1,128)} %bitcast.92), custom_call_target="tpu_custom_call" | custom-call | flops 2097152 | bytes 2097152 | tf_op jit(solution)/shard_map/forward_part/pallas_call | solution.py:83
  34.0 0.3 collective-permute-start.4
  34.4 0.3 collective-permute-start.1
  34.7 2.2 %transposes.1 = (bf16[1024,1024]{1,0:T(8,128)(2,1)S(1)}, bf16[1024,128]{1,0:T(8,128)(2,1)S(1)}) custom-call(bf16[1024,1024]{1,0:T(8,128)(2,1)S(1)} %copy-done, bf16[100,1024]{1,0:T(8,128)(2,1)} %wo_ref.9), custom_call_target="tpu_custom_call" | custom-call | flops 2048 | bytes 2048 | tf_op jit(solution)/shard_map/transposes/pallas_call | solution.py:327
  36.9 0.6 collective-permute-start.9
  37.5 6.8 %backward_part.4 = (bf16[2,1024,512]{2,1,0:T(8,128)(2,1)S(1)}, f32[128,1024]{1,0:T(8,128)S(1)}, f32[1024,1024]{1,0:T(8,128)S(1)}) custom-call(f32[200,512]{1,0:T(8,128)S(1)} %get-tuple-element.62.refs_0_, f32[200,512]{1,0:T(8,128)S(1)} %collective-permute-done.5.refs_1_, f32[200,512]{1,0:T(8,128)S(1)} %collective-permute-done.6.refs_2_, ...), custom_call_target="tpu_custom_call" | custom-call | flops 2097152 | bytes 2097152 | tf_op jit(solution)/shard_map/backward_part/pallas_call | solution.py:296
  44.3 0.5 collective-permute-start.11
  44.8 6.3 %backward_part.5 = (bf16[2,1024,512]{2,1,0:T(8,128)(2,1)S(1)}, f32[128,1024]{1,0:T(8,128)S(1)}, f32[1024,1024]{1,0:T(8,128)S(1)}) custom-call(f32[200,512]{1,0:T(8,128)S(1)} %get-tuple-element.64.f_ref, f32[200,512]{1,0:T(8,128)S(1)} %collective-permute-done.2.fc_ref, ...), custom_call_target="tpu_custom_call", output_to_operand_aliasing={{2}: (11, {})} | custom-call | flops 2097152 | bytes 2097152 | tf_op jit(solution)/shard_map/backward_part/pallas_call | solution.py:296
  51.3 6.5 %backward_part.6 = (bf16[2,1024,512]{2,1,0:T(8,128)(2,1)S(1)}, f32[128,1024]{1,0:T(8,128)S(1)}, f32[1024,1024]{1,0:T(8,128)S(1)}) custom-call(f32[200,512]{1,0:T(8,128)S(1)} %get-tuple-element.66.f_ref, f32[200,512]{1,0:T(8,128)S(1)} %collective-permute-done.9.fc_ref, ...), custom_call_target="tpu_custom_call", output_to_operand_aliasing={{2}: (11, {})} | custom-call | flops 2097152 | bytes 2097152 | tf_op jit(solution)/shard_map/backward_part/pallas_call | solution.py:296
  57.8 7.4 %backward_part.7 = (bf16[2,1024,512]{2,1,0:T(8,128)(2,1)S(1)}, f32[128,1024]{1,0:T(8,128)}, f32[1024,1024]{1,0:T(8,128)S(1)}, f32[2,2,4,72,256]{4,3,2,1,0:T(8,12...) custom-call(f32[200,512]{1,0:T(8,128)S(1)} %get-tuple-element.68.f_r, ...), custom_call_target="tpu_custom_call", output_to_operand_aliasing={{2}: (11, {})} | custom-call | flops 2097152 | bytes 2097152 | tf_op jit(solution)/shard_map/backward_part/pallas_call | solution.py:296
  65.2 0.3 collective-permute-start.12
  65.7 2.3 %collective-permute-done.12 = f32[2,2,4,72,256]{4,3,2,1,0:T(8,128)S(1)} collective-permute-done((f32[2,2,4,72,256]{4,3,2,1,0:T(8,128)S(1)}, f32[2,2,4,72,256]{4,3,2,1,0:T(8,128)S(1)}, u32[]{:S(2)}, u32[]{:S(2)}) %collective-permute-start.12) | collective-permute-done | bytes 1179680 | tf_op jit(solution)/shard_map/ppermute | solution.py:409
  68.2 1.3 collective-permute-start.14
  69.4 0.3 collective-permute-done.13
  69.8 1.3 %collective-permute-start.15 = (f32[2,4,72,256]{3,2,1,0:T(8,128)S(1)}, f32[2,4,72,256]{3,2,1,0:T(8,128)S(1)}, u32[]{:S(2)}, u32[]{:S(2)}) collective-permute-start(f32[2,4,72,256]{3,2,1,0:T(8,128)S(1)} %fusion.4), channel_id=1, source_target_pairs={{0,1},{1,0},{2,3},{3,2},{4,5},{5,4},{6,7},{7,6},{8,9},{9,8},{10,11... | collective-permute-start | bytes 1769480 | tf_op jit(solution)/shard_map/ppermute | solution.py:410
  71.1 3.5 %grad_hidden_part.4.refs_0_ = bf16[2,1024,2048]{2,1,0:T(8,128)(2,1)} custom-call(bf16[1024,1024]{1,0:T(8,128)(2,1)S(1)} %get-tuple-element.70.wt_ref, bf16[2,1024,512]{2,1,0:T(8,128)(2,1)S(1)} %get-tuple-element.98.gp_ref), custom_call_target="tpu_custom_call" | custom-call | flops 2097152 | bytes 2097152 | tf_op jit(solution)/shard_map/grad_hidden_part/pallas_call | solution.py:367
  74.6 3.5 %grad_hidden_part.5.refs_0_ = bf16[2,1024,2048]{2,1,0:T(8,128)(2,1)} custom-call(bf16[1024,1024]{1,0:T(8,128)(2,1)S(1)} %get-tuple-element.70.wt_ref, bf16[2,1024,512]{2,1,0:T(8,128)(2,1)S(1)} %get-tuple-element.97.gp_ref, bf16[2,1024,2048]{2,1,0:T(8,128)(2,1)} %grad_hidden_part.4.refs_0_), custom_call_target="tpu_custom_call", output_to_operand_aliasing={{}: (2, {})} | custom-call | flops 2097152 | bytes 2097152 | tf_op jit(solution)/shard_map/grad_hidden_part/pallas_call | solution.py:367
  78.1 4.7 %collective-permute-done.14 = f32[2,4,72,256]{3,2,1,0:T(8,128)S(1)} collective-permute-done((f32[2,4,72,256]{3,2,1,0:T(8,128)S(1)}, f32[2,4,72,256]{3,2,1,0:T(8,128)S(1)}, u32[]{:S(2)}, u32[]{:S(2)}) %collective-permute-start.14) | collective-permute-done | bytes 589856 | tf_op jit(solution)/shard_map/ppermute | solution.py:408
  83.0 1.3 %collective-permute-start.16 = (f32[4,72,256]{2,1,0:T(8,128)S(1)}, f32[4,72,256]{2,1,0:T(8,128)S(1)}, u32[]{:S(2)}, u32[]{:S(2)}) collective-permute-start(f32[4,72,256]{2,1,0:T(8,128)S(1)} %get-tuple-element.115), channel_id=1, source_target_pairs={{0,1},{1,0},{2,3},{3,2},{4,5},{5,4},{6,7},{7,6},{8,9},{9,8},{10,11... | collective-permute-start | bytes 884744 | tf_op jit(solution)/shard_map/ppermute | solution.py:410
  84.7 1.3 collective-permute-start.17
  85.9 3.5 %grad_hidden_part.6.refs_0_ = bf16[2,1024,2048]{2,1,0:T(8,128)(2,1)} custom-call(bf16[1024,1024]{1,0:T(8,128)(2,1)S(1)} %get-tuple-element.70.wt_ref, bf16[2,1024,512]{2,1,0:T(8,128)(2,1)S(1)} %get-tuple-element.104.gp_ref, bf16[2,1024,2048]{2,1,0:T(8,128)(2,1)} %grad_hidden_part.5.refs_0_), custom_call_target="tpu_custom_call", output_to_operand_aliasing={{}: (2, {})} | custom-call | flops 2097152 | bytes 2097152 | tf_op jit(solution)/shard_map/grad_hidden_part/pallas_call | solution.py:367
  89.4 1.0 collective-permute-done.16
  90.5 1.5 %collective-permute-done.17 = f32[4,72,256]{2,1,0:T(8,128)S(1)} collective-permute-done((f32[4,72,256]{2,1,0:T(8,128)S(1)}, f32[4,72,256]{2,1,0:T(8,128)S(1)}, u32[]{:S(2)}, u32[]{:S(2)}) %collective-permute-start.17) | collective-permute-done | bytes 294944 | tf_op jit(solution)/shard_map/ppermute | solution.py:408
  92.2 1.4 %collective-permute-start.18 = (f32[192,256]{1,0:T(8,128)S(1)}, f32[192,256]{1,0:T(8,128)S(1)}, u32[]{:S(2)}, u32[]{:S(2)}) collective-permute-start(f32[192,256]{1,0:T(8,128)S(1)} %get-tuple-element.136), channel_id=1, source_target_pairs={{0,2},{1,3},{2,4},{3,5},{4,6},{5,7},{6,0},{7,1},{8,10},{9,11},{10,... | collective-permute-start | bytes 589832 | tf_op jit(solution)/shard_map/ppermute | solution.py:411
  93.5 1.1 collective-permute-start.19
  94.6 1.4 %collective-permute-start.20 = (f32[192,256]{1,0:T(8,128)S(1)}, f32[192,256]{1,0:T(8,128)S(1)}, u32[]{:S(2)}, u32[]{:S(2)}) collective-permute-start(f32[192,256]{1,0:T(8,128)S(1)} %get-tuple-element.135), channel_id=1, source_target_pairs={{0,6},{1,7},{2,0},{3,1},{4,2},{5,3},{6,4},{7,5},{8,14},{9,15},{10,... | collective-permute-start | bytes 589832 | tf_op jit(solution)/shard_map/ppermute | solution.py:411
  96.0 3.5 %grad_hidden_part.7 = bf16[2,1024,2048]{2,1,0:T(8,128)(2,1)} custom-call(bf16[1024,1024]{1,0:T(8,128)(2,1)S(1)} %get-tuple-element.70.wt_ref, bf16[2,1024,512]{2,1,0:T(8,128)(2,1)S(1)} %get-tuple-element.108.gp_ref, bf16[2,1024,2048]{2,1,0:T(8,128)(2,1)} %grad_hidden_part.6.refs_0_), custom_call_target="tpu_custom_call", output_to_operand_aliasing={{}: (2, {})} | custom-call | flops 2097152 | bytes 2097152 | tf_op jit(solution)/shard_map/grad_hidden_part/pallas_call | solution.py:367
  99.5 9.0 %collective-permute-done.19 = f32[192,256]{1,0:T(8,128)S(1)} collective-permute-done((f32[192,256]{1,0:T(8,128)S(1)}, f32[192,256]{1,0:T(8,128)S(1)}, u32[]{:S(2)}, u32[]{:S(2)}) %collective-permute-start.19) | collective-permute-done | bytes 196640 | tf_op jit(solution)/shard_map/ppermute | solution.py:411
  108.5 4.0 %collective-permute-done.20 = f32[192,256]{1,0:T(8,128)S(1)} collective-permute-done((f32[192,256]{1,0:T(8,128)S(1)}, f32[192,256]{1,0:T(8,128)S(1)}, u32[]{:S(2)}, u32[]{:S(2)}) %collective-permute-start.20) | collective-permute-done | bytes 196640 | tf_op jit(solution)/shard_map/ppermute | solution.py:411
  112.6 1.4 %collective-permute-start.22 = (f32[1,64,256]{2,1,0:T(8,128)S(1)}, f32[1,64,256]{2,1,0:T(8,128)S(1)}, u32[]{:S(2)}, u32[]{:S(2)}) collective-permute-start(f32[1,64,256]{2,1,0:T(8,128)S(1)} %get-tuple-element.125), channel_id=1, source_target_pairs={{0,1},{1,0},{2,3},{3,2},{4,5},{5,4},{6,7},{7,6},{8,9},{9,8},{10,11... | collective-permute-start | bytes 196616 | tf_op jit(solution)/shard_map/ppermute | solution.py:496
  114.0 1.1 collective-permute-start.23
  115.4 0.5 collective-permute-done.22
  115.8 2.2 %collective-permute-done.23 = f32[1,64,256]{2,1,0:T(8,128)S(1)} collective-permute-done((f32[1,64,256]{2,1,0:T(8,128)S(1)}, f32[1,64,256]{2,1,0:T(8,128)S(1)}, u32[]{:S(2)}, u32[]{:S(2)}) %collective-permute-start.23) | collective-permute-done | bytes 65568 | tf_op jit(solution)/shard_map/ppermute | solution.py:498
  118.1 3.8 %collective-permute-done.21 = f32[192,256]{1,0:T(8,128)S(1)} collective-permute-done((f32[192,256]{1,0:T(8,128)S(1)}, f32[192,256]{1,0:T(8,128)S(1)}, u32[]{:S(2)}, u32[]{:S(2)}) %collective-permute-start.21) | collective-permute-done | bytes 196640 | tf_op jit(solution)/shard_map/ppermute | solution.py:408
  121.9 1.3 %collective-permute-start.24 = (f32[1,2,2,64,256]{4,3,2,1,0:T(8,128)S(1)}, f32[1,2,2,64,256]{4,3,2,1,0:T(8,128)S(1)}, u32[]{:S(2)}, u32[]{:S(2)}) collective-permute-start(f32[1,2,2,64,256]{4,3,2,1,0:T(8,128)S(1)} %maximum_select_fusion.3), channel_id=1, source_target_pairs={{0,8},{8,0},{16,24},{24,16},{1,9},{9,1},{17,25},{25,17},{2,10},{10... | collective-permute-start | bytes 786440 | tf_op jit(solution)/shard_map/ppermute | solution.py:457
  123.4 1.0 collective-permute-done.24
  124.5 0.6 slice_reduce_fusion
  125.8 0.8 slice_multiply_fusion
  126.6 0.8 maximum_select_fusion.1
  (54 shorter events, 2.0 us)
Async XLA Ops:
  0.6 8.2 %copy-start = (bf16[1024,1024]{1,0:T(8,128)(2,1)S(1)}, bf16[1024,1024]{1,0:T(8,128)(2,1)}, u32[]{:S(2)}) copy-start(bf16[1024,1024]{1,0:T(8,128)(2,1)} %w_ref.8) | copy-start | bytes 6291460
  7.6 10.4 %collective-permute-start.6 = (f32[200,512]{1,0:T(8,128)S(1)}, f32[200,512]{1,0:T(8,128)S(1)}, u32[]{:S(2)}, u32[]{:S(2)}) collective-permute-start(f32[200,512]{1,0:T(8,128)S(1)} %get-tuple-element.62.refs_0_), channel_id=1, source_target_pairs={{0,16},{8,24},{16,0},{24,8},{1,17},{9,25},{17,1},{25,9},{2,18},{10... | collective-permute-start | bytes 1228808 | tf_op jit(solution)/shard_map/ppermute | solution.py:408
  14.9 19.2 %collective-permute-start.3 = (f32[200,512]{1,0:T(8,128)S(1)}, f32[200,512]{1,0:T(8,128)S(1)}, u32[]{:S(2)}, u32[]{:S(2)}) collective-permute-start(f32[200,512]{1,0:T(8,128)S(1)} %get-tuple-element.64.f_ref), channel_id=1, source_target_pairs={{0,16},{8,24},{16,0},{24,8},{1,17},{9,25},{17,1},{25,9},{2,18},{10... | collective-permute-start | bytes 1228808 | tf_op jit(solution)/shard_map/ppermute | solution.py:408
  15.2 19.2 %collective-permute-start.5 = (f32[200,512]{1,0:T(8,128)S(1)}, f32[200,512]{1,0:T(8,128)S(1)}, u32[]{:S(2)}, u32[]{:S(2)}) collective-permute-start(f32[200,512]{1,0:T(8,128)S(1)} %get-tuple-element.62.refs_0_), channel_id=1, source_target_pairs={{0,8},{8,0},{16,24},{24,16},{1,9},{9,1},{17,25},{25,17},{2,10},{10... | collective-permute-start | bytes 1228808 | tf_op jit(solution)/shard_map/ppermute | solution.py:409
  16.4 27.9 %collective-permute-start.2 = (f32[200,512]{1,0:T(8,128)S(1)}, f32[200,512]{1,0:T(8,128)S(1)}, u32[]{:S(2)}, u32[]{:S(2)}) collective-permute-start(f32[200,512]{1,0:T(8,128)S(1)} %get-tuple-element.64.f_ref), channel_id=1, source_target_pairs={{0,8},{8,0},{16,24},{24,16},{1,9},{9,1},{17,25},{25,17},{2,10},{10... | collective-permute-start | bytes 1228808 | tf_op jit(solution)/shard_map/ppermute | solution.py:409
  18.0 18.9 %collective-permute-start.7 = (f32[200,512]{1,0:T(8,128)S(1)}, f32[200,512]{1,0:T(8,128)S(1)}, u32[]{:S(2)}, u32[]{:S(2)}) collective-permute-start(f32[200,512]{1,0:T(8,128)S(1)} %collective-permute-done.6.refs_2_), channel_id=1, source_target_pairs={{0,8},{8,0},{16,24},{24,16},{1,9},{9,1},{17,25},{25,17},{2,10},{10... | collective-permute-start | bytes 1228808 | tf_op jit(solution)/shard_map/ppermute | solution.py:409
  26.7 17.5 %collective-permute-start.10 = (f32[200,512]{1,0:T(8,128)S(1)}, f32[200,512]{1,0:T(8,128)S(1)}, u32[]{:S(2)}, u32[]{:S(2)}) collective-permute-start(f32[200,512]{1,0:T(8,128)S(1)} %get-tuple-element.66.f_ref), channel_id=1, source_target_pairs={{0,16},{8,24},{16,0},{24,8},{1,17},{9,25},{17,1},{25,9},{2,18},{10... | collective-permute-start | bytes 1228808 | tf_op jit(solution)/shard_map/ppermute | solution.py:408
  34.0 3.4 %copy-start.1 = (f32[100,2048]{1,0:T(8,128)S(1)}, f32[100,2048]{1,0:T(8,128)}, u32[]{:S(2)}) copy-start(f32[100,2048]{1,0:T(8,128)} %target_ref.5) | copy-start | bytes 2457604
  34.0 3.4 %copy-start.2 = (f32[2048]{0:T(1024)S(1)}, f32[2048]{0:T(1024)}, u32[]{:S(2)}) copy-start(f32[2048]{0:T(1024)} %param.10) | copy-start | bytes 24580
  34.0 3.4 %copy-start.3 = (f32[100]{0:T(128)S(1)}, f32[100]{0:T(128)}, u32[]{:S(2)}) copy-start(f32[100]{0:T(128)} %param.11) | copy-start | bytes 1204
  34.0 10.8 %collective-permute-start.4 = (f32[200,512]{1,0:T(8,128)S(1)}, f32[200,512]{1,0:T(8,128)S(1)}, u32[]{:S(2)}, u32[]{:S(2)}) collective-permute-start(f32[200,512]{1,0:T(8,128)S(1)} %collective-permute-done.3.fx_ref), channel_id=1, source_target_pairs={{0,8},{8,0},{16,24},{24,16},{1,9},{9,1},{17,25},{25,17},{2,10},{10... | collective-permute-start | bytes 1228808 | tf_op jit(solution)/shard_map/ppermute | solution.py:409
  34.4 16.7 %collective-permute-start.1 = (f32[200,512]{1,0:T(8,128)S(1)}, f32[200,512]{1,0:T(8,128)S(1)}, u32[]{:S(2)}, u32[]{:S(2)}) collective-permute-start(f32[200,512]{1,0:T(8,128)S(1)} %get-tuple-element.68.f_ref), channel_id=1, source_target_pairs={{0,16},{8,24},{16,0},{24,8},{1,17},{9,25},{17,1},{25,9},{2,18},{10... | collective-permute-start | bytes 1228808 | tf_op jit(solution)/shard_map/ppermute | solution.py:408
  36.9 14.4 %collective-permute-start.9 = (f32[200,512]{1,0:T(8,128)S(1)}, f32[200,512]{1,0:T(8,128)S(1)}, u32[]{:S(2)}, u32[]{:S(2)}) collective-permute-start(f32[200,512]{1,0:T(8,128)S(1)} %get-tuple-element.66.f_ref), channel_id=1, source_target_pairs={{0,8},{8,0},{16,24},{24,16},{1,9},{9,1},{17,25},{25,17},{2,10},{10... | collective-permute-start | bytes 1228808 | tf_op jit(solution)/shard_map/ppermute | solution.py:409
  44.2 13.6 %collective-permute-start = (f32[200,512]{1,0:T(8,128)S(1)}, f32[200,512]{1,0:T(8,128)S(1)}, u32[]{:S(2)}, u32[]{:S(2)}) collective-permute-start(f32[200,512]{1,0:T(8,128)S(1)} %get-tuple-element.68.f_ref), channel_id=1, source_target_pairs={{0,8},{8,0},{16,24},{24,16},{1,9},{9,1},{17,25},{25,17},{2,10},{10... | collective-permute-start | bytes 1228808 | tf_op jit(solution)/shard_map/ppermute | solution.py:409
  44.3 6.9 %collective-permute-start.11 = (f32[200,512]{1,0:T(8,128)S(1)}, f32[200,512]{1,0:T(8,128)S(1)}, u32[]{:S(2)}, u32[]{:S(2)}) collective-permute-start(f32[200,512]{1,0:T(8,128)S(1)} %collective-permute-done.10.fx_ref), channel_id=1, source_target_pairs={{0,8},{8,0},{16,24},{24,16},{1,9},{9,1},{17,25},{25,17},{2,10},{10... | collective-permute-start | bytes 1228808 | tf_op jit(solution)/shard_map/ppermute | solution.py:409
  51.1 6.7 %collective-permute-start.8 = (f32[200,512]{1,0:T(8,128)S(1)}, f32[200,512]{1,0:T(8,128)S(1)}, u32[]{:S(2)}, u32[]{:S(2)}) collective-permute-start(f32[200,512]{1,0:T(8,128)S(1)} %collective-permute-done.1.fx_ref), channel_id=1, source_target_pairs={{0,8},{8,0},{16,24},{24,16},{1,9},{9,1},{17,25},{25,17},{2,10},{10... | collective-permute-start | bytes 1228808 | tf_op jit(solution)/shard_map/ppermute | solution.py:409
  65.2 2.8 %collective-permute-start.12 = (f32[2,2,4,72,256]{4,3,2,1,0:T(8,128)S(1)}, f32[2,2,4,72,256]{4,3,2,1,0:T(8,128)S(1)}, u32[]{:S(2)}, u32[]{:S(2)}) collective-permute-start(f32[2,2,4,72,256]{4,3,2,1,0:T(8,128)S(1)} %get-tuple-element.94), channel_id=1, source_target_pairs={{0,8},{8,0},{16,24},{24,16},{1,9},{9,1},{17,25},{25,17},{2,10},{10... | collective-permute-start | bytes 3538952 | tf_op jit(solution)/shard_map/ppermute | solution.py:409
  65.5 4.2 %collective-permute-start.13 = (f32[2,2,4,72,256]{4,3,2,1,0:T(8,128)S(1)}, f32[2,2,4,72,256]{4,3,2,1,0:T(8,128)S(1)}, u32[]{:S(2)}, u32[]{:S(2)}) collective-permute-start(f32[2,2,4,72,256]{4,3,2,1,0:T(8,128)S(1)} %get-tuple-element.96), channel_id=1, source_target_pairs={{0,8},{8,0},{16,24},{24,16},{1,9},{9,1},{17,25},{25,17},{2,10},{10... | collective-permute-start | bytes 3538952 | tf_op jit(solution)/shard_map/ppermute | solution.py:409
  68.2 14.7 %collective-permute-start.14 = (f32[2,4,72,256]{3,2,1,0:T(8,128)S(1)}, f32[2,4,72,256]{3,2,1,0:T(8,128)S(1)}, u32[]{:S(2)}, u32[]{:S(2)}) collective-permute-start(f32[2,4,72,256]{3,2,1,0:T(8,128)S(1)} %fusion.5), channel_id=1, source_target_pairs={{0,16},{8,24},{16,0},{24,8},{1,17},{9,25},{17,1},{25,9},{2,18},{10... | collective-permute-start | bytes 1769480 | tf_op jit(solution)/shard_map/ppermute | solution.py:408
  69.8 14.7 %collective-permute-start.15 = (f32[2,4,72,256]{3,2,1,0:T(8,128)S(1)}, f32[2,4,72,256]{3,2,1,0:T(8,128)S(1)}, u32[]{:S(2)}, u32[]{:S(2)}) collective-permute-start(f32[2,4,72,256]{3,2,1,0:T(8,128)S(1)} %fusion.4), channel_id=1, source_target_pairs={{0,1},{1,0},{2,3},{3,2},{4,5},{5,4},{6,7},{7,6},{8,9},{9,8},{10,11... | collective-permute-start | bytes 1769480 | tf_op jit(solution)/shard_map/ppermute | solution.py:410
  83.0 7.4 %collective-permute-start.16 = (f32[4,72,256]{2,1,0:T(8,128)S(1)}, f32[4,72,256]{2,1,0:T(8,128)S(1)}, u32[]{:S(2)}, u32[]{:S(2)}) collective-permute-start(f32[4,72,256]{2,1,0:T(8,128)S(1)} %get-tuple-element.115), channel_id=1, source_target_pairs={{0,1},{1,0},{2,3},{3,2},{4,5},{5,4},{6,7},{7,6},{8,9},{9,8},{10,11... | collective-permute-start | bytes 884744 | tf_op jit(solution)/shard_map/ppermute | solution.py:410
  84.7 7.4 %collective-permute-start.17 = (f32[4,72,256]{2,1,0:T(8,128)S(1)}, f32[4,72,256]{2,1,0:T(8,128)S(1)}, u32[]{:S(2)}, u32[]{:S(2)}) collective-permute-start(f32[4,72,256]{2,1,0:T(8,128)S(1)} %get-tuple-element.113), channel_id=1, source_target_pairs={{0,16},{8,24},{16,0},{24,8},{1,17},{9,25},{17,1},{25,9},{2,18},{10... | collective-permute-start | bytes 884744 | tf_op jit(solution)/shard_map/ppermute | solution.py:408
  92.2 7.3 %collective-permute-start.18 = (f32[192,256]{1,0:T(8,128)S(1)}, f32[192,256]{1,0:T(8,128)S(1)}, u32[]{:S(2)}, u32[]{:S(2)}) collective-permute-start(f32[192,256]{1,0:T(8,128)S(1)} %get-tuple-element.136), channel_id=1, source_target_pairs={{0,2},{1,3},{2,4},{3,5},{4,6},{5,7},{6,0},{7,1},{8,10},{9,11},{10,... | collective-permute-start | bytes 589832 | tf_op jit(solution)/shard_map/ppermute | solution.py:411
  93.5 15.0 %collective-permute-start.19 = (f32[192,256]{1,0:T(8,128)S(1)}, f32[192,256]{1,0:T(8,128)S(1)}, u32[]{:S(2)}, u32[]{:S(2)}) collective-permute-start(f32[192,256]{1,0:T(8,128)S(1)} %get-tuple-element.134), channel_id=1, source_target_pairs={{0,4},{1,5},{2,6},{3,7},{4,0},{5,1},{6,2},{7,3},{8,12},{9,13},{10,... | collective-permute-start | bytes 589832 | tf_op jit(solution)/shard_map/ppermute | solution.py:411
  94.6 17.9 %collective-permute-start.20 = (f32[192,256]{1,0:T(8,128)S(1)}, f32[192,256]{1,0:T(8,128)S(1)}, u32[]{:S(2)}, u32[]{:S(2)}) collective-permute-start(f32[192,256]{1,0:T(8,128)S(1)} %get-tuple-element.135), channel_id=1, source_target_pairs={{0,6},{1,7},{2,0},{3,1},{4,2},{5,3},{6,4},{7,5},{8,14},{9,15},{10,... | collective-permute-start | bytes 589832 | tf_op jit(solution)/shard_map/ppermute | solution.py:411
  112.6 3.2 %collective-permute-start.22 = (f32[1,64,256]{2,1,0:T(8,128)S(1)}, f32[1,64,256]{2,1,0:T(8,128)S(1)}, u32[]{:S(2)}, u32[]{:S(2)}) collective-permute-start(f32[1,64,256]{2,1,0:T(8,128)S(1)} %get-tuple-element.125), channel_id=1, source_target_pairs={{0,1},{1,0},{2,3},{3,2},{4,5},{5,4},{6,7},{7,6},{8,9},{9,8},{10,11... | collective-permute-start | bytes 196616 | tf_op jit(solution)/shard_map/ppermute | solution.py:496
  114.0 4.0 %collective-permute-start.23 = (f32[1,64,256]{2,1,0:T(8,128)S(1)}, f32[1,64,256]{2,1,0:T(8,128)S(1)}, u32[]{:S(2)}, u32[]{:S(2)}) collective-permute-start(f32[1,64,256]{2,1,0:T(8,128)S(1)} %get-tuple-element.125), channel_id=1, source_target_pairs={{0,17},{1,16},{2,19},{3,18},{4,21},{5,20},{6,23},{7,22},{8,25},{9,... | collective-permute-start | bytes 196616 | tf_op jit(solution)/shard_map/ppermute | solution.py:498
  115.1 6.7 %collective-permute-start.21 = (f32[192,256]{1,0:T(8,128)S(1)}, f32[192,256]{1,0:T(8,128)S(1)}, u32[]{:S(2)}, u32[]{:S(2)}) collective-permute-start(f32[192,256]{1,0:T(8,128)S(1)} %add_add_fusion), channel_id=1, source_target_pairs={{0,16},{8,24},{16,0},{24,8},{1,17},{9,25},{17,1},{25,9},{2,18},{10... | collective-permute-start | bytes 589832 | tf_op jit(solution)/shard_map/ppermute | solution.py:408
  121.9 2.5 %collective-permute-start.24 = (f32[1,2,2,64,256]{4,3,2,1,0:T(8,128)S(1)}, f32[1,2,2,64,256]{4,3,2,1,0:T(8,128)S(1)}, u32[]{:S(2)}, u32[]{:S(2)}) collective-permute-start(f32[1,2,2,64,256]{4,3,2,1,0:T(8,128)S(1)} %maximum_select_fusion.3), channel_id=1, source_target_pairs={{0,8},{8,0},{16,24},{24,16},{1,9},{9,1},{17,25},{25,17},{2,10},{10... | collective-permute-start | bytes 786440 | tf_op jit(solution)/shard_map/ppermute | solution.py:457
  123.3 3.3 %collective-permute-start.25 = (f32[64,1024]{1,0:T(8,128)S(1)}, f32[64,1024]{1,0:T(8,128)S(1)}, u32[]{:S(2)}, u32[]{:S(2)}) collective-permute-start(f32[64,1024]{1,0:T(8,128)S(1)} %maximum_multiply_fusion), channel_id=1, source_target_pairs={{0,8},{8,0},{16,24},{24,16},{1,9},{9,1},{17,25},{25,17},{2,10},{10... | collective-permute-start | bytes 786440 | tf_op jit(solution)/shard_map/ppermute | solution.py:457

commit v2 on v1

--- a/solution.py
+++ b/solution.py
@@ -13,7 +13,7 @@
 EPS = 0.0004
 K0 = math.sqrt(2.0 / math.pi)
 K1 = K0 * 0.044715
-SLAB = 512
+SLAB = 256
 EXTRA_ROWS = 8
 VMEM = 8 * 1024 * 1024
 NT = (((1,), (1,)), ((), ()))
@@ -47,13 +47,16 @@
         half[...] = wo_ref[...] * jnp.bfloat16(0.5)
 
     hid = jnp.concatenate([hid_ref[m] for m in range(mloc)], axis=1)
-    for k, slab in enumerate(slabs):
-        rows = pl.ds(k * size, size)
-        slab[...] = jnp.dot(w_ref[rows, :], hid, preferred_element_type=jnp.float32)
     out = jnp.broadcast_to(column(bo_ref[...], v), (v, mloc * t))
-    for k, slab in enumerate(slabs):
+    for k in range(len(slabs) + 1):
+        if k < len(slabs):
+            rows = pl.ds(k * size, size)
+            slabs[k][...] = jnp.dot(w_ref[rows, :], hid, preferred_element_type=jnp.float32)
+        if k == 0:
+            continue
+        slab, start = slabs[k - 1], (k - 1) * size
         for r in range(0, size, 16):
-            rows = pl.ds(k * size + r, 16)
+            rows = pl.ds(start + r, 16)
             b = jnp.concatenate([bias[rows, :]] * (t // 128), axis=1)
             for m in range(mloc):
                 x = slab[pl.ds(r, 16), pl.ds(m * t, t)] + b
@@ -63,7 +66,7 @@
                 act = x * up
                 act_ref[step, m, rows, :] = act.astype(jnp.bfloat16)
                 slope_ref[step, m, rows, :] = up + act * ((1.0 - th) * (K0 + 3.0 * q))
-        rows = pl.ds(k * size, size)
+        rows = pl.ds(start, size)
         act = jnp.concatenate([act_ref[step, m, rows, :] for m in range(mloc)], axis=1)
         out = out + jnp.dot(half[:, rows], act, preferred_element_type=jnp.float32)
     for m in range(mloc):
@@ -103,9 +106,8 @@
         scratch_shapes=[
             pltpu.VMEM((h, 128), jnp.float32),
             pltpu.VMEM((v, h), jnp.bfloat16),
-            pltpu.VMEM((h // 2, mloc * t), jnp.float32),
-            pltpu.VMEM((h // 2, mloc * t), jnp.float32),
-        ],
+        ]
+        + [pltpu.VMEM((SLAB, mloc * t), jnp.float32)] * (h // SLAB),
         compiler_params=pltpu.CompilerParams(vmem_limit_bytes=vmem),
         cost_estimate=pl.CostEstimate(
             flops=2 * h * h, bytes_accessed=2 * h * h, transcendentals=0
@@ -351,6 +353,40 @@
             refs[-1][m, rows, :] = out[:, m * t : (m + 1) * t].astype(jnp.bfloat16)
 
 
+def last_kernel(n_hi, n_lo, scale, npoints, own_ref, other_ref, e_ref, f_ref, inner_ref, out_ref, loss_ref):
+    core = lax.axis_index("mem") % 2
+    r = own_ref.shape[0]
+    inner_ref[pl.ds(pl.multiple_of(core * r, r), r), :] = own_ref[...] * scale
+    inner_ref[pl.ds(pl.multiple_of((1 - core) * r, r), r), :] = other_ref[...] * scale
+    v = out_ref.shape[0]
+    cx = e_ref.shape[-1]
+    for row in range(0, v + 1, EXTRA_ROWS):
+        c, g = divmod(row // EXTRA_ROWS, n_hi * n_lo)
+        hi, lo = divmod(g, n_lo)
+        count = min(EXTRA_ROWS, v - row)
+        total = 0.0
+        for part in range(2):
+            for x in range(2):
+                piece = jnp.where(core == c, e_ref[lo, x, part, hi], f_ref[lo, x, part, hi])
+                columns = pl.ds((2 * part + x) * cx, cx)
+                out_ref[pl.ds(row, count), columns] = piece[:count] * (0.5 * scale)
+                if row + EXTRA_ROWS > v:
+                    total = total + jnp.sum(piece[count : count + 1], axis=1, keepdims=True)
+        if row + EXTRA_ROWS > v:
+            loss_ref[...] = total * (1.0 / npoints)
+
+
+def finished(dims, scale, npoints, v, own, other, e_own, e_other):
+    r, h = own.shape
+    shapes = [(2 * r, h), (v, h), (1, 1)]
+    return pl.pallas_call(
+        functools.partial(last_kernel, *dims, scale, npoints),
+        out_shape=[jax.ShapeDtypeStruct(shape, jnp.float32) for shape in shapes],
+        compiler_params=pltpu.CompilerParams(vmem_limit_bytes=VMEM),
+        name="last",
+    )(own, other, e_own, e_other)
+
+
 def input_gradient(start, p, n, wt, gp, gh):
     steps, h, width = gp.shape
     t = TILE
@@ -427,6 +463,9 @@
     parts, far = [], []
     for start, p in spans:
         w, vmem = w_inner, VMEM
+        if len(parts) == 2:
+            wt, wot = transposes(after(w_inner, parts[1][2]), w_out, vp)
+            b_out = after(b_out, wt)
         if parts:
             b_out = after(b_out, parts[-1][2])
         else:
@@ -435,7 +474,6 @@
         parts.append(forward(start, p, hidden, w, b_inner, w_out, b_out, vmem))
         far.append(to_x(parts[-1][2]))
     near = [to_core(fields) for _, _, fields in parts]
-    wt, wot = transposes(after(w_inner, parts[-1][2]), w_out, vp)
     vw, area = var_weight.reshape(1, v), area.reshape(1, n)
     acc = extra = gh = None
     grad_pre = []
@@ -499,7 +537,8 @@
 
     scale = 1.0 / math.sqrt(members * npoints)
     halves = [ordered(total[k : k + r], far[k : k + r], 1, "mem", n_mem // 2) for k in (0, r)]
-    grad_inner = gathered(jnp.concatenate(halves, 1) * scale, 0, "mem", 1)
+    own = jnp.concatenate(halves, 1)
+    other = to_core(own)
 
     sides = [ordered(mine, far[2 * r :][None], 0, "mem", n_mem // 2)]
     sides.append(ordered(beyond, across, 0, "mem", n_mem // 2))
@@ -508,11 +547,11 @@
     while bit < n_lo:
         extra = gathered(extra, 0, "grid", bit)
         bit *= 2
-    extra = gathered(extra[None], 0, "mem", 1)
-    extra = extra.reshape(2, n_lo, 2, 2, n_hi, EXTRA_ROWS, cx)
-    extra = extra.transpose(0, 4, 1, 5, 3, 2, 6).reshape(2 * n_grid * EXTRA_ROWS, h)
-    loss = jnp.sum(extra[v]) / npoints
-    return (loss, gh, grad_inner, extra[:v] * (0.5 * scale))
+    extra = extra.reshape(n_lo, 2, 2, n_hi, EXTRA_ROWS, cx)
+    grad_inner, grad_out, loss = finished(
+        (n_hi, n_lo), scale, npoints, v, own, other, extra, to_core(extra)
+    )
+    return (loss.reshape(()), gh, grad_inner, grad_out)
 
 
 def solution(mesh):

time: 129 us -> 124 us (0.961)
  other arithmetic: 3 us -> 0.66 us
  waiting for transfers between devices: 32.2 us -> 30 us
  between operations: 2.76 us -> 0.94 us
  Pallas kernels: 68 us -> 69.7 us
    ppermute x7, waiting for transfers between devices: 11.6 us -> 6.23 us  [shards(): to_x = lambda a: lax.ppermute(a, 'mem', swap_x)]
    ppermute x10 -> x12, waiting for transfers between devices: 2.71 us -> 4.2 us  [shards(): to_core = lambda a: lax.ppermute(a, 'mem', swap_core)]
    ppermute x1, waiting for transfers between devices: 0.47 us -> 1.95 us  [shards(): beyond = lax.ppermute(mine, 'grid', [(g, g ^ 1) for g in range(n_grid)])]
    ppermute x2 -> x0, starting transfers between devices: 1.42 us -> none  [gathered(): other = lax.ppermute(block, name, [(i, i ^ bit) for i in range(n)])]
    ppermute x10 -> x12, starting transfers between devices: 6.09 us -> 7.03 us  [shards(): to_core = lambda a: lax.ppermute(a, 'mem', swap_core)]
  transfers between devices with their start and end apart: 26 -> 26, of which waited for: 13 -> 12; matrix products, arithmetic and copies ran while one was open for 2% -> 0% of each run, Pallas kernels for 42% -> 44%
where the time goes in v2:
time: 124 us; the launch traced here: 123 us
  Pallas kernels  69.7 us (56%)
  waiting for transfers between devices  30 us (24%)
  starting transfers between devices  22 us (18%)
    pallas_call x4, Pallas kernels, backward(): pl.pallas_call(kernel_fn, grid=(steps + 1,), in_specs=in_specs, out_specs...  27.2 us
    pallas_call x4, Pallas kernels, forward(): pl.pallas_call(forward_kernel, grid=(tiles,), in_specs=[pl.BlockSpec((mlo...  25.4 us
    pallas_call x4, Pallas kernels, input_gradient(): pl.pallas_call(input_kernel, grid=(steps,), in_specs=in_specs, out_specs=...  13.9 us
    ppermute x3, waiting for transfers between devices, shards(): to_hi = lambda a, k: lax.ppermute(a, 'grid', shift_hi(k))  13.1 us
    ppermute x12, starting transfers between devices, shards(): to_core = lambda a: lax.ppermute(a, 'mem', swap_core)  7.03 us
    ppermute x7, starting transfers between devices, shards(): to_x = lambda a: lax.ppermute(a, 'mem', swap_x)  6.94 us
    ppermute x7, waiting for transfers between devices, shards(): to_x = lambda a: lax.ppermute(a, 'mem', swap_x)  6.23 us
    ppermute x12, waiting for transfers between devices, shards(): to_core = lambda a: lax.ppermute(a, 'mem', swap_core)  4.2 us
  transfers between devices with their start and end apart: 26, of which 12 were waited for; matrix products, arithmetic and copies ran while one was open for 0% of the time, Pallas kernels for 44%

profile of v2, /device:TPU:9, one launch (start us, length us, event | category | flops | bytes accessed | tf_op | source)
XLA Modules:
  0.0 123.5 jit_solution(7224089325634629904)
XLA Ops:
  0.7 7.1 %forward_part.4 = (bf16[2,2,1024,256]{3,2,1,0:T(8,128)(2,1)S(1)}, f32[2,2,1024,256]{3,2,1,0:T(8,128)S(1)}, f32[200,512]{1,0:T(8,128)S(1)}) custom-call(bf16[2,1024,2048]{2,1,0:T(8,128)(2,1)} %hid_ref.6, bf16[1024,1024]{1,0:T(8,128)(2,1)} %w_ref.8, f32[1,1024]{1,0:T(1,128)} %bitcast.61, bf16[100,1024]{1,0:T(8,128)(2,1)} %wo_ref.9, f32[1,100]{1,0:T(1,128)} %bitcast.67), custom_call_target="tpu_custom_call" | custom-call | flops 2097152 | bytes 2097152 | tf_op jit(solution)/shard_map/forward_part/pallas_call | solution.py:86
  7.7 1.3 %collective-permute-start.6 = (f32[200,512]{1,0:T(8,128)S(1)}, f32[200,512]{1,0:T(8,128)S(1)}, u32[]{:S(2)}, u32[]{:S(2)}) collective-permute-start(f32[200,512]{1,0:T(8,128)S(1)} %get-tuple-element.63.refs_0_), channel_id=1, source_target_pairs={{0,16},{8,24},{16,0},{24,8},{1,17},{9,25},{17,1},{25,9},{2,18},{10... | collective-permute-start | bytes 1228808 | tf_op jit(solution)/shard_map/ppermute | solution.py:444
  9.0 6.1 %forward_part.5 = (bf16[2,2,1024,256]{3,2,1,0:T(8,128)(2,1)S(1)}, f32[2,2,1024,256]{3,2,1,0:T(8,128)S(1)}, f32[200,512]{1,0:T(8,128)S(1)}) custom-call(bf16[2,1024,2048]{2,1,0:T(8,128)(2,1)} %hid_ref.6, bf16[1024,1024]{1,0:T(8,128)(2,1)S(1)} %copy-done, f32[1,1024]{1,0:T(1,128)} %bitcast.62, bf16[100,1024]{1,0:T(8,128)(2,1)} %wo_ref.9, f32[1,100]{1,0:T(1,128)} %bitcast.68), custom_call_target="tpu_custom_call" | custom-call | flops 2097152 | bytes 2097152 | tf_op jit(solution)/shard_map/forward_part/pallas_call | solution.py:86
  15.1 0.3 collective-permute-start.3
  15.4 1.2 collective-permute-start.5
  16.7 2.2 %transposes.1 = (bf16[1024,1024]{1,0:T(8,128)(2,1)S(1)}, bf16[1024,128]{1,0:T(8,128)(2,1)S(1)}) custom-call(bf16[1024,1024]{1,0:T(8,128)(2,1)S(1)} %copy-done, bf16[100,1024]{1,0:T(8,128)(2,1)} %wo_ref.9), custom_call_target="tpu_custom_call" | custom-call | flops 2048 | bytes 2048 | tf_op jit(solution)/shard_map/transposes/pallas_call | solution.py:329
  18.9 1.9 %collective-permute-start.7 = (f32[200,512]{1,0:T(8,128)S(1)}, f32[200,512]{1,0:T(8,128)S(1)}, u32[]{:S(2)}, u32[]{:S(2)}) collective-permute-start(f32[200,512]{1,0:T(8,128)S(1)} %collective-permute-done.6.refs_2_), channel_id=1, source_target_pairs={{0,8},{8,0},{16,24},{24,16},{1,9},{9,1},{17,25},{25,17},{2,10},{10... | collective-permute-start | bytes 1228808 | tf_op jit(solution)/shard_map/ppermute | solution.py:445
  20.8 6.1 %forward_part.6 = (bf16[2,2,1024,256]{3,2,1,0:T(8,128)(2,1)S(1)}, f32[2,2,1024,256]{3,2,1,0:T(8,128)S(1)}, f32[200,512]{1,0:T(8,128)S(1)}) custom-call(bf16[2,1024,2048]{2,1,0:T(8,128)(2,1)} %hid_ref.6, bf16[1024,1024]{1,0:T(8,128)(2,1)S(1)} %copy-done, f32[1,1024]{1,0:T(1,128)} %bitcast.63, bf16[100,1024]{1,0:T(8,128)(2,1)} %wo_ref.9, f32[1,100]{1,0:T(1,128)} %bitcast.69), custom_call_target="tpu_custom_call" | custom-call | flops 2097152 | bytes 2097152 | tf_op jit(solution)/shard_map/forward_part/pallas_call | solution.py:86
  27.0 1.3 %collective-permute-start.10 = (f32[200,512]{1,0:T(8,128)S(1)}, f32[200,512]{1,0:T(8,128)S(1)}, u32[]{:S(2)}, u32[]{:S(2)}) collective-permute-start(f32[200,512]{1,0:T(8,128)S(1)} %get-tuple-element.70.f_ref), channel_id=1, source_target_pairs={{0,16},{8,24},{16,0},{24,8},{1,17},{9,25},{17,1},{25,9},{2,18},{10... | collective-permute-start | bytes 1228808 | tf_op jit(solution)/shard_map/ppermute | solution.py:444
  28.3 6.1 %forward_part.7 = (bf16[2,2,1024,256]{3,2,1,0:T(8,128)(2,1)S(1)}, f32[2,2,1024,256]{3,2,1,0:T(8,128)S(1)}, f32[200,512]{1,0:T(8,128)S(1)}) custom-call(bf16[2,1024,2048]{2,1,0:T(8,128)(2,1)} %hid_ref.6, bf16[1024,1024]{1,0:T(8,128)(2,1)S(1)} %copy-done, f32[1,1024]{1,0:T(1,128)} %bitcast.64, bf16[100,1024]{1,0:T(8,128)(2,1)} %wo_ref.9, f32[1,100]{1,0:T(1,128)} %bitcast.70), custom_call_target="tpu_custom_call" | custom-call | flops 2097152 | bytes 2097152 | tf_op jit(solution)/shard_map/forward_part/pallas_call | solution.py:86
  34.4 0.4 collective-permute-start.4
  34.7 0.2 collective-permute-start.1
  35.0 0.5 collective-permute-start.9
  35.5 6.8 %backward_part.4 = (bf16[2,1024,512]{2,1,0:T(8,128)(2,1)S(1)}, f32[128,1024]{1,0:T(8,128)S(1)}, f32[1024,1024]{1,0:T(8,128)S(1)}) custom-call(f32[200,512]{1,0:T(8,128)S(1)} %get-tuple-element.63.refs_0_, f32[200,512]{1,0:T(8,128)S(1)} %collective-permute-done.5.refs_1_, f32[200,512]{1,0:T(8,128)S(1)} %collective-permute-done.6.refs_2_, ...), custom_call_target="tpu_custom_call" | custom-call | flops 2097152 | bytes 2097152 | tf_op jit(solution)/shard_map/backward_part/pallas_call | solution.py:298
  42.4 0.5 collective-permute-start.11
  42.9 6.3 %backward_part.5 = (bf16[2,1024,512]{2,1,0:T(8,128)(2,1)S(1)}, f32[128,1024]{1,0:T(8,128)S(1)}, f32[1024,1024]{1,0:T(8,128)S(1)}) custom-call(f32[200,512]{1,0:T(8,128)S(1)} %get-tuple-element.65.f_ref, f32[200,512]{1,0:T(8,128)S(1)} %collective-permute-done.2.fc_ref, ...), custom_call_target="tpu_custom_call", output_to_operand_aliasing={{2}: (11, {})} | custom-call | flops 2097152 | bytes 2097152 | tf_op jit(solution)/shard_map/backward_part/pallas_call | solution.py:298
  49.3 0.1 collective-permute-start.8
  49.4 6.6 %backward_part.6 = (bf16[2,1024,512]{2,1,0:T(8,128)(2,1)S(1)}, f32[128,1024]{1,0:T(8,128)S(1)}, f32[1024,1024]{1,0:T(8,128)S(1)}) custom-call(f32[200,512]{1,0:T(8,128)S(1)} %get-tuple-element.70.f_ref, f32[200,512]{1,0:T(8,128)S(1)} %collective-permute-done.9.fc_ref, ...), custom_call_target="tpu_custom_call", output_to_operand_aliasing={{2}: (11, {})} | custom-call | flops 2097152 | bytes 2097152 | tf_op jit(solution)/shard_map/backward_part/pallas_call | solution.py:298
  56.0 7.5 %backward_part.7 = (bf16[2,1024,512]{2,1,0:T(8,128)(2,1)S(1)}, f32[128,1024]{1,0:T(8,128)}, f32[1024,1024]{1,0:T(8,128)S(1)}, f32[2,2,4,72,256]{4,3,2,1,0:T(8,12...) custom-call(f32[200,512]{1,0:T(8,128)S(1)} %get-tuple-element.72.f_r, ...), custom_call_target="tpu_custom_call", output_to_operand_aliasing={{2}: (11, {})} | custom-call | flops 2097152 | bytes 2097152 | tf_op jit(solution)/shard_map/backward_part/pallas_call | solution.py:298
  63.5 0.3 collective-permute-start.12
  63.8 0.2 collective-permute-start.13
  64.0 2.3 %collective-permute-done.12 = f32[2,2,4,72,256]{4,3,2,1,0:T(8,128)S(1)} collective-permute-done((f32[2,2,4,72,256]{4,3,2,1,0:T(8,128)S(1)}, f32[2,2,4,72,256]{4,3,2,1,0:T(8,128)S(1)}, u32[]{:S(2)}, u32[]{:S(2)}) %collective-permute-start.12) | collective-permute-done | bytes 1179680 | tf_op jit(solution)/shard_map/ppermute | solution.py:445
  66.4 1.3 %collective-permute-start.14 = (f32[2,4,72,256]{3,2,1,0:T(8,128)S(1)}, f32[2,4,72,256]{3,2,1,0:T(8,128)S(1)}, u32[]{:S(2)}, u32[]{:S(2)}) collective-permute-start(f32[2,4,72,256]{3,2,1,0:T(8,128)S(1)} %fusion.5), channel_id=1, source_target_pairs={{0,16},{8,24},{16,0},{24,8},{1,17},{9,25},{17,1},{25,9},{2,18},{10... | collective-permute-start | bytes 1769480 | tf_op jit(solution)/shard_map/ppermute | solution.py:444
  67.7 0.3 collective-permute-done.13
  68.1 1.3 %collective-permute-start.15 = (f32[2,4,72,256]{3,2,1,0:T(8,128)S(1)}, f32[2,4,72,256]{3,2,1,0:T(8,128)S(1)}, u32[]{:S(2)}, u32[]{:S(2)}) collective-permute-start(f32[2,4,72,256]{3,2,1,0:T(8,128)S(1)} %fusion.4), channel_id=1, source_target_pairs={{0,1},{1,0},{2,3},{3,2},{4,5},{5,4},{6,7},{7,6},{8,9},{9,8},{10,11... | collective-permute-start | bytes 1769480 | tf_op jit(solution)/shard_map/ppermute | solution.py:446
  69.4 3.5 %grad_hidden_part.4.refs_0_ = bf16[2,1024,2048]{2,1,0:T(8,128)(2,1)} custom-call(bf16[1024,1024]{1,0:T(8,128)(2,1)S(1)} %get-tuple-element.67.wt_ref, bf16[2,1024,512]{2,1,0:T(8,128)(2,1)S(1)} %get-tuple-element.100.gp_ref), custom_call_target="tpu_custom_call" | custom-call | flops 2097152 | bytes 2097152 | tf_op jit(solution)/shard_map/grad_hidden_part/pallas_call | solution.py:403
  72.9 3.5 %grad_hidden_part.5.refs_0_ = bf16[2,1024,2048]{2,1,0:T(8,128)(2,1)} custom-call(bf16[1024,1024]{1,0:T(8,128)(2,1)S(1)} %get-tuple-element.67.wt_ref, bf16[2,1024,512]{2,1,0:T(8,128)(2,1)S(1)} %get-tuple-element.99.gp_ref, bf16[2,1024,2048]{2,1,0:T(8,128)(2,1)} %grad_hidden_part.4.refs_0_), custom_call_target="tpu_custom_call", output_to_operand_aliasing={{}: (2, {})} | custom-call | flops 2097152 | bytes 2097152 | tf_op jit(solution)/shard_map/grad_hidden_part/pallas_call | solution.py:403
  76.4 4.7 %collective-permute-done.14 = f32[2,4,72,256]{3,2,1,0:T(8,128)S(1)} collective-permute-done((f32[2,4,72,256]{3,2,1,0:T(8,128)S(1)}, f32[2,4,72,256]{3,2,1,0:T(8,128)S(1)}, u32[]{:S(2)}, u32[]{:S(2)}) %collective-permute-start.14) | collective-permute-done | bytes 589856 | tf_op jit(solution)/shard_map/ppermute | solution.py:444
  81.2 1.3 %collective-permute-start.16 = (f32[4,72,256]{2,1,0:T(8,128)S(1)}, f32[4,72,256]{2,1,0:T(8,128)S(1)}, u32[]{:S(2)}, u32[]{:S(2)}) collective-permute-start(f32[4,72,256]{2,1,0:T(8,128)S(1)} %get-tuple-element.121), channel_id=1, source_target_pairs={{0,1},{1,0},{2,3},{3,2},{4,5},{5,4},{6,7},{7,6},{8,9},{9,8},{10,11... | collective-permute-start | bytes 884744 | tf_op jit(solution)/shard_map/ppermute | solution.py:446
  82.6 0.2 collective-permute-done.15
  82.9 1.3 %collective-permute-start.17 = (f32[4,72,256]{2,1,0:T(8,128)S(1)}, f32[4,72,256]{2,1,0:T(8,128)S(1)}, u32[]{:S(2)}, u32[]{:S(2)}) collective-permute-start(f32[4,72,256]{2,1,0:T(8,128)S(1)} %get-tuple-element.119), channel_id=1, source_target_pairs={{0,16},{8,24},{16,0},{24,8},{1,17},{9,25},{17,1},{25,9},{2,18},{10... | collective-permute-start | bytes 884744 | tf_op jit(solution)/shard_map/ppermute | solution.py:444
  84.2 3.5 %grad_hidden_part.6.refs_0_ = bf16[2,1024,2048]{2,1,0:T(8,128)(2,1)} custom-call(bf16[1024,1024]{1,0:T(8,128)(2,1)S(1)} %get-tuple-element.67.wt_ref, bf16[2,1024,512]{2,1,0:T(8,128)(2,1)S(1)} %get-tuple-element.106.gp_ref, bf16[2,1024,2048]{2,1,0:T(8,128)(2,1)} %grad_hidden_part.5.refs_0_), custom_call_target="tpu_custom_call", output_to_operand_aliasing={{}: (2, {})} | custom-call | flops 2097152 | bytes 2097152 | tf_op jit(solution)/shard_map/grad_hidden_part/pallas_call | solution.py:403
  87.7 1.0 collective-permute-done.16
  88.7 1.5 %collective-permute-done.17 = f32[4,72,256]{2,1,0:T(8,128)S(1)} collective-permute-done((f32[4,72,256]{2,1,0:T(8,128)S(1)}, f32[4,72,256]{2,1,0:T(8,128)S(1)}, u32[]{:S(2)}, u32[]{:S(2)}) %collective-permute-start.17) | collective-permute-done | bytes 294944 | tf_op jit(solution)/shard_map/ppermute | solution.py:444
  90.4 1.4 %collective-permute-start.18 = (f32[192,256]{1,0:T(8,128)S(1)}, f32[192,256]{1,0:T(8,128)S(1)}, u32[]{:S(2)}, u32[]{:S(2)}) collective-permute-start(f32[192,256]{1,0:T(8,128)S(1)} %get-tuple-element.140), channel_id=1, source_target_pairs={{0,2},{1,3},{2,4},{3,5},{4,6},{5,7},{6,0},{7,1},{8,10},{9,11},{10,... | collective-permute-start | bytes 589832 | tf_op jit(solution)/shard_map/ppermute | solution.py:447
  91.8 1.1 collective-permute-start.19
  92.9 1.4 %collective-permute-start.20 = (f32[192,256]{1,0:T(8,128)S(1)}, f32[192,256]{1,0:T(8,128)S(1)}, u32[]{:S(2)}, u32[]{:S(2)}) collective-permute-start(f32[192,256]{1,0:T(8,128)S(1)} %get-tuple-element.139), channel_id=1, source_target_pairs={{0,6},{1,7},{2,0},{3,1},{4,2},{5,3},{6,4},{7,5},{8,14},{9,15},{10,... | collective-permute-start | bytes 589832 | tf_op jit(solution)/shard_map/ppermute | solution.py:447
  94.3 3.5 %grad_hidden_part.7 = bf16[2,1024,2048]{2,1,0:T(8,128)(2,1)} custom-call(bf16[1024,1024]{1,0:T(8,128)(2,1)S(1)} %get-tuple-element.67.wt_ref, bf16[2,1024,512]{2,1,0:T(8,128)(2,1)S(1)} %get-tuple-element.110.gp_ref, bf16[2,1024,2048]{2,1,0:T(8,128)(2,1)} %grad_hidden_part.6.refs_0_), custom_call_target="tpu_custom_call", output_to_operand_aliasing={{}: (2, {})} | custom-call | flops 2097152 | bytes 2097152 | tf_op jit(solution)/shard_map/grad_hidden_part/pallas_call | solution.py:403
  97.7 9.0 %collective-permute-done.19 = f32[192,256]{1,0:T(8,128)S(1)} collective-permute-done((f32[192,256]{1,0:T(8,128)S(1)}, f32[192,256]{1,0:T(8,128)S(1)}, u32[]{:S(2)}, u32[]{:S(2)}) %collective-permute-start.19) | collective-permute-done | bytes 196640 | tf_op jit(solution)/shard_map/ppermute | solution.py:447
  106.8 4.0 %collective-permute-done.20 = f32[192,256]{1,0:T(8,128)S(1)} collective-permute-done((f32[192,256]{1,0:T(8,128)S(1)}, f32[192,256]{1,0:T(8,128)S(1)}, u32[]{:S(2)}, u32[]{:S(2)}) %collective-permute-start.20) | collective-permute-done | bytes 196640 | tf_op jit(solution)/shard_map/ppermute | solution.py:447
  110.9 1.2 %collective-permute-start.21 = (f32[192,256]{1,0:T(8,128)S(1)}, f32[192,256]{1,0:T(8,128)S(1)}, u32[]{:S(2)}, u32[]{:S(2)}) collective-permute-start(f32[192,256]{1,0:T(8,128)S(1)} %add_add_fusion), channel_id=1, source_target_pairs={{0,16},{8,24},{16,0},{24,8},{1,17},{9,25},{17,1},{25,9},{2,18},{10... | collective-permute-start | bytes 589832 | tf_op jit(solution)/shard_map/ppermute | solution.py:444
  112.1 1.4 %collective-permute-start.23 = (f32[1,64,256]{2,1,0:T(8,128)S(1)}, f32[1,64,256]{2,1,0:T(8,128)S(1)}, u32[]{:S(2)}, u32[]{:S(2)}) collective-permute-start(f32[1,64,256]{2,1,0:T(8,128)S(1)} %get-tuple-element.131), channel_id=1, source_target_pairs={{0,1},{1,0},{2,3},{3,2},{4,5},{5,4},{6,7},{7,6},{8,9},{9,8},{10,11... | collective-permute-start | bytes 196616 | tf_op jit(solution)/shard_map/ppermute | solution.py:534
  113.7 1.9 %collective-permute-done.23 = f32[1,64,256]{2,1,0:T(8,128)S(1)} collective-permute-done((f32[1,64,256]{2,1,0:T(8,128)S(1)}, f32[1,64,256]{2,1,0:T(8,128)S(1)}, u32[]{:S(2)}, u32[]{:S(2)}) %collective-permute-start.23) | collective-permute-done | bytes 65568 | tf_op jit(solution)/shard_map/ppermute | solution.py:534
  115.6 3.4 %collective-permute-done.24 = f32[1,64,256]{2,1,0:T(8,128)S(1)} collective-permute-done((f32[1,64,256]{2,1,0:T(8,128)S(1)}, f32[1,64,256]{2,1,0:T(8,128)S(1)}, u32[]{:S(2)}, u32[]{:S(2)}) %collective-permute-start.24) | collective-permute-done | bytes 65568 | tf_op jit(solution)/shard_map/ppermute | solution.py:536
  119.1 1.7 %collective-permute-start.25 = (f32[2,2,2,4,8,256]{5,4,3,2,1,0:T(8,128)S(1)}, f32[2,2,2,4,8,256]{5,4,3,2,1,0:T(8,128)S(1)}, u32[]{:S(2)}, u32[]{:S(2)}) collective-permute-start(f32[2,2,2,4,8,256]{5,4,3,2,1,0:T(8,128)S(1)} %maximum_select_fusion.e_ref), channel_id=1, source_target_pairs={{0,8},{8,0},{16,24},{24,16},{1,9},{9,1},{17,25},{25,17},{2,10},{10... | collective-permute-start | bytes 786440 | tf_op jit(solution)/shard_map/ppermute | solution.py:445
  121.0 1.0 collective-permute-done.25.f_ref
  122.0 0.5 collective-permute-done.22.other_ref
  122.5 1.0 last.1
  (47 shorter events, 1.2 us)
Async XLA Ops:
  0.6 8.4 %copy-start = (bf16[1024,1024]{1,0:T(8,128)(2,1)S(1)}, bf16[1024,1024]{1,0:T(8,128)(2,1)}, u32[]{:S(2)}) copy-start(bf16[1024,1024]{1,0:T(8,128)(2,1)} %w_ref.8) | copy-start | bytes 6291460
  7.7 11.2 %collective-permute-start.6 = (f32[200,512]{1,0:T(8,128)S(1)}, f32[200,512]{1,0:T(8,128)S(1)}, u32[]{:S(2)}, u32[]{:S(2)}) collective-permute-start(f32[200,512]{1,0:T(8,128)S(1)} %get-tuple-element.63.refs_0_), channel_id=1, source_target_pairs={{0,16},{8,24},{16,0},{24,8},{1,17},{9,25},{17,1},{25,9},{2,18},{10... | collective-permute-start | bytes 1228808 | tf_op jit(solution)/shard_map/ppermute | solution.py:444
  15.1 19.3 %collective-permute-start.3 = (f32[200,512]{1,0:T(8,128)S(1)}, f32[200,512]{1,0:T(8,128)S(1)}, u32[]{:S(2)}, u32[]{:S(2)}) collective-permute-start(f32[200,512]{1,0:T(8,128)S(1)} %get-tuple-element.65.f_ref), channel_id=1, source_target_pairs={{0,16},{8,24},{16,0},{24,8},{1,17},{9,25},{17,1},{25,9},{2,18},{10... | collective-permute-start | bytes 1228808 | tf_op jit(solution)/shard_map/ppermute | solution.py:444
  15.4 19.3 %collective-permute-start.5 = (f32[200,512]{1,0:T(8,128)S(1)}, f32[200,512]{1,0:T(8,128)S(1)}, u32[]{:S(2)}, u32[]{:S(2)}) collective-permute-start(f32[200,512]{1,0:T(8,128)S(1)} %get-tuple-element.63.refs_0_), channel_id=1, source_target_pairs={{0,8},{8,0},{16,24},{24,16},{1,9},{9,1},{17,25},{25,17},{2,10},{10... | collective-permute-start | bytes 1228808 | tf_op jit(solution)/shard_map/ppermute | solution.py:445
  16.7 25.7 %collective-permute-start.2 = (f32[200,512]{1,0:T(8,128)S(1)}, f32[200,512]{1,0:T(8,128)S(1)}, u32[]{:S(2)}, u32[]{:S(2)}) collective-permute-start(f32[200,512]{1,0:T(8,128)S(1)} %get-tuple-element.65.f_ref), channel_id=1, source_target_pairs={{0,8},{8,0},{16,24},{24,16},{1,9},{9,1},{17,25},{25,17},{2,10},{10... | collective-permute-start | bytes 1228808 | tf_op jit(solution)/shard_map/ppermute | solution.py:445
  18.9 16.1 %collective-permute-start.7 = (f32[200,512]{1,0:T(8,128)S(1)}, f32[200,512]{1,0:T(8,128)S(1)}, u32[]{:S(2)}, u32[]{:S(2)}) collective-permute-start(f32[200,512]{1,0:T(8,128)S(1)} %collective-permute-done.6.refs_2_), channel_id=1, source_target_pairs={{0,8},{8,0},{16,24},{24,16},{1,9},{9,1},{17,25},{25,17},{2,10},{10... | collective-permute-start | bytes 1228808 | tf_op jit(solution)/shard_map/ppermute | solution.py:445
  26.9 8.6 %copy-start.1 = (f32[100,2048]{1,0:T(8,128)S(1)}, f32[100,2048]{1,0:T(8,128)}, u32[]{:S(2)}) copy-start(f32[100,2048]{1,0:T(8,128)} %target_ref.5) | copy-start | bytes 2457604
  26.9 8.6 %copy-start.2 = (f32[2048]{0:T(1024)S(1)}, f32[2048]{0:T(1024)}, u32[]{:S(2)}) copy-start(f32[2048]{0:T(1024)} %param.10) | copy-start | bytes 24580
  27.0 8.6 %copy-start.3 = (f32[100]{0:T(128)S(1)}, f32[100]{0:T(128)}, u32[]{:S(2)}) copy-start(f32[100]{0:T(128)} %param.11) | copy-start | bytes 1204
  27.0 15.3 %collective-permute-start.10 = (f32[200,512]{1,0:T(8,128)S(1)}, f32[200,512]{1,0:T(8,128)S(1)}, u32[]{:S(2)}, u32[]{:S(2)}) collective-permute-start(f32[200,512]{1,0:T(8,128)S(1)} %get-tuple-element.70.f_ref), channel_id=1, source_target_pairs={{0,16},{8,24},{16,0},{24,8},{1,17},{9,25},{17,1},{25,9},{2,18},{10... | collective-permute-start | bytes 1228808 | tf_op jit(solution)/shard_map/ppermute | solution.py:444
  34.4 8.5 %collective-permute-start.4 = (f32[200,512]{1,0:T(8,128)S(1)}, f32[200,512]{1,0:T(8,128)S(1)}, u32[]{:S(2)}, u32[]{:S(2)}) collective-permute-start(f32[200,512]{1,0:T(8,128)S(1)} %collective-permute-done.3.fx_ref), channel_id=1, source_target_pairs={{0,8},{8,0},{16,24},{24,16},{1,9},{9,1},{17,25},{25,17},{2,10},{10... | collective-permute-start | bytes 1228808 | tf_op jit(solution)/shard_map/ppermute | solution.py:445
  34.7 14.5 %collective-permute-start.1 = (f32[200,512]{1,0:T(8,128)S(1)}, f32[200,512]{1,0:T(8,128)S(1)}, u32[]{:S(2)}, u32[]{:S(2)}) collective-permute-start(f32[200,512]{1,0:T(8,128)S(1)} %get-tuple-element.72.f_ref), channel_id=1, source_target_pairs={{0,16},{8,24},{16,0},{24,8},{1,17},{9,25},{17,1},{25,9},{2,18},{10... | collective-permute-start | bytes 1228808 | tf_op jit(solution)/shard_map/ppermute | solution.py:444
  35.0 14.4 %collective-permute-start.9 = (f32[200,512]{1,0:T(8,128)S(1)}, f32[200,512]{1,0:T(8,128)S(1)}, u32[]{:S(2)}, u32[]{:S(2)}) collective-permute-start(f32[200,512]{1,0:T(8,128)S(1)} %get-tuple-element.70.f_ref), channel_id=1, source_target_pairs={{0,8},{8,0},{16,24},{24,16},{1,9},{9,1},{17,25},{25,17},{2,10},{10... | collective-permute-start | bytes 1228808 | tf_op jit(solution)/shard_map/ppermute | solution.py:445
  42.3 13.7 %collective-permute-start = (f32[200,512]{1,0:T(8,128)S(1)}, f32[200,512]{1,0:T(8,128)S(1)}, u32[]{:S(2)}, u32[]{:S(2)}) collective-permute-start(f32[200,512]{1,0:T(8,128)S(1)} %get-tuple-element.72.f_ref), channel_id=1, source_target_pairs={{0,8},{8,0},{16,24},{24,16},{1,9},{9,1},{17,25},{25,17},{2,10},{10... | collective-permute-start | bytes 1228808 | tf_op jit(solution)/shard_map/ppermute | solution.py:445
  42.4 7.0 %collective-permute-start.11 = (f32[200,512]{1,0:T(8,128)S(1)}, f32[200,512]{1,0:T(8,128)S(1)}, u32[]{:S(2)}, u32[]{:S(2)}) collective-permute-start(f32[200,512]{1,0:T(8,128)S(1)} %collective-permute-done.10.fx_ref), channel_id=1, source_target_pairs={{0,8},{8,0},{16,24},{24,16},{1,9},{9,1},{17,25},{25,17},{2,10},{10... | collective-permute-start | bytes 1228808 | tf_op jit(solution)/shard_map/ppermute | solution.py:445
  49.3 6.7 %collective-permute-start.8 = (f32[200,512]{1,0:T(8,128)S(1)}, f32[200,512]{1,0:T(8,128)S(1)}, u32[]{:S(2)}, u32[]{:S(2)}) collective-permute-start(f32[200,512]{1,0:T(8,128)S(1)} %collective-permute-done.1.fx_ref), channel_id=1, source_target_pairs={{0,8},{8,0},{16,24},{24,16},{1,9},{9,1},{17,25},{25,17},{2,10},{10... | collective-permute-start | bytes 1228808 | tf_op jit(solution)/shard_map/ppermute | solution.py:445
  63.5 2.8 %collective-permute-start.12 = (f32[2,2,4,72,256]{4,3,2,1,0:T(8,128)S(1)}, f32[2,2,4,72,256]{4,3,2,1,0:T(8,128)S(1)}, u32[]{:S(2)}, u32[]{:S(2)}) collective-permute-start(f32[2,2,4,72,256]{4,3,2,1,0:T(8,128)S(1)} %get-tuple-element.96), channel_id=1, source_target_pairs={{0,8},{8,0},{16,24},{24,16},{1,9},{9,1},{17,25},{25,17},{2,10},{10... | collective-permute-start | bytes 3538952 | tf_op jit(solution)/shard_map/ppermute | solution.py:445
  63.8 4.2 %collective-permute-start.13 = (f32[2,2,4,72,256]{4,3,2,1,0:T(8,128)S(1)}, f32[2,2,4,72,256]{4,3,2,1,0:T(8,128)S(1)}, u32[]{:S(2)}, u32[]{:S(2)}) collective-permute-start(f32[2,2,4,72,256]{4,3,2,1,0:T(8,128)S(1)} %get-tuple-element.98), channel_id=1, source_target_pairs={{0,8},{8,0},{16,24},{24,16},{1,9},{9,1},{17,25},{25,17},{2,10},{10... | collective-permute-start | bytes 3538952 | tf_op jit(solution)/shard_map/ppermute | solution.py:445
  66.4 14.7 %collective-permute-start.14 = (f32[2,4,72,256]{3,2,1,0:T(8,128)S(1)}, f32[2,4,72,256]{3,2,1,0:T(8,128)S(1)}, u32[]{:S(2)}, u32[]{:S(2)}) collective-permute-start(f32[2,4,72,256]{3,2,1,0:T(8,128)S(1)} %fusion.5), channel_id=1, source_target_pairs={{0,16},{8,24},{16,0},{24,8},{1,17},{9,25},{17,1},{25,9},{2,18},{10... | collective-permute-start | bytes 1769480 | tf_op jit(solution)/shard_map/ppermute | solution.py:444
  68.1 14.7 %collective-permute-start.15 = (f32[2,4,72,256]{3,2,1,0:T(8,128)S(1)}, f32[2,4,72,256]{3,2,1,0:T(8,128)S(1)}, u32[]{:S(2)}, u32[]{:S(2)}) collective-permute-start(f32[2,4,72,256]{3,2,1,0:T(8,128)S(1)} %fusion.4), channel_id=1, source_target_pairs={{0,1},{1,0},{2,3},{3,2},{4,5},{5,4},{6,7},{7,6},{8,9},{9,8},{10,11... | collective-permute-start | bytes 1769480 | tf_op jit(solution)/shard_map/ppermute | solution.py:446
  81.2 7.4 %collective-permute-start.16 = (f32[4,72,256]{2,1,0:T(8,128)S(1)}, f32[4,72,256]{2,1,0:T(8,128)S(1)}, u32[]{:S(2)}, u32[]{:S(2)}) collective-permute-start(f32[4,72,256]{2,1,0:T(8,128)S(1)} %get-tuple-element.121), channel_id=1, source_target_pairs={{0,1},{1,0},{2,3},{3,2},{4,5},{5,4},{6,7},{7,6},{8,9},{9,8},{10,11... | collective-permute-start | bytes 884744 | tf_op jit(solution)/shard_map/ppermute | solution.py:446
  82.9 7.3 %collective-permute-start.17 = (f32[4,72,256]{2,1,0:T(8,128)S(1)}, f32[4,72,256]{2,1,0:T(8,128)S(1)}, u32[]{:S(2)}, u32[]{:S(2)}) collective-permute-start(f32[4,72,256]{2,1,0:T(8,128)S(1)} %get-tuple-element.119), channel_id=1, source_target_pairs={{0,16},{8,24},{16,0},{24,8},{1,17},{9,25},{17,1},{25,9},{2,18},{10... | collective-permute-start | bytes 884744 | tf_op jit(solution)/shard_map/ppermute | solution.py:444
  90.4 7.3 %collective-permute-start.18 = (f32[192,256]{1,0:T(8,128)S(1)}, f32[192,256]{1,0:T(8,128)S(1)}, u32[]{:S(2)}, u32[]{:S(2)}) collective-permute-start(f32[192,256]{1,0:T(8,128)S(1)} %get-tuple-element.140), channel_id=1, source_target_pairs={{0,2},{1,3},{2,4},{3,5},{4,6},{5,7},{6,0},{7,1},{8,10},{9,11},{10,... | collective-permute-start | bytes 589832 | tf_op jit(solution)/shard_map/ppermute | solution.py:447
  91.8 15.0 %collective-permute-start.19 = (f32[192,256]{1,0:T(8,128)S(1)}, f32[192,256]{1,0:T(8,128)S(1)}, u32[]{:S(2)}, u32[]{:S(2)}) collective-permute-start(f32[192,256]{1,0:T(8,128)S(1)} %get-tuple-element.138), channel_id=1, source_target_pairs={{0,4},{1,5},{2,6},{3,7},{4,0},{5,1},{6,2},{7,3},{8,12},{9,13},{10,... | collective-permute-start | bytes 589832 | tf_op jit(solution)/shard_map/ppermute | solution.py:447
  92.9 17.9 %collective-permute-start.20 = (f32[192,256]{1,0:T(8,128)S(1)}, f32[192,256]{1,0:T(8,128)S(1)}, u32[]{:S(2)}, u32[]{:S(2)}) collective-permute-start(f32[192,256]{1,0:T(8,128)S(1)} %get-tuple-element.139), channel_id=1, source_target_pairs={{0,6},{1,7},{2,0},{3,1},{4,2},{5,3},{6,4},{7,5},{8,14},{9,15},{10,... | collective-permute-start | bytes 589832 | tf_op jit(solution)/shard_map/ppermute | solution.py:447
  110.9 8.2 %collective-permute-start.21 = (f32[192,256]{1,0:T(8,128)S(1)}, f32[192,256]{1,0:T(8,128)S(1)}, u32[]{:S(2)}, u32[]{:S(2)}) collective-permute-start(f32[192,256]{1,0:T(8,128)S(1)} %add_add_fusion), channel_id=1, source_target_pairs={{0,16},{8,24},{16,0},{24,8},{1,17},{9,25},{17,1},{25,9},{2,18},{10... | collective-permute-start | bytes 589832 | tf_op jit(solution)/shard_map/ppermute | solution.py:444
  112.1 3.5 %collective-permute-start.23 = (f32[1,64,256]{2,1,0:T(8,128)S(1)}, f32[1,64,256]{2,1,0:T(8,128)S(1)}, u32[]{:S(2)}, u32[]{:S(2)}) collective-permute-start(f32[1,64,256]{2,1,0:T(8,128)S(1)} %get-tuple-element.131), channel_id=1, source_target_pairs={{0,1},{1,0},{2,3},{3,2},{4,5},{5,4},{6,7},{7,6},{8,9},{9,8},{10,11... | collective-permute-start | bytes 196616 | tf_op jit(solution)/shard_map/ppermute | solution.py:534
  113.5 5.5 %collective-permute-start.24 = (f32[1,64,256]{2,1,0:T(8,128)S(1)}, f32[1,64,256]{2,1,0:T(8,128)S(1)}, u32[]{:S(2)}, u32[]{:S(2)}) collective-permute-start(f32[1,64,256]{2,1,0:T(8,128)S(1)} %get-tuple-element.131), channel_id=1, source_target_pairs={{0,17},{1,16},{2,19},{3,18},{4,21},{5,20},{6,23},{7,22},{8,25},{9,... | collective-permute-start | bytes 196616 | tf_op jit(solution)/shard_map/ppermute | solution.py:536
  119.1 2.9 %collective-permute-start.25 = (f32[2,2,2,4,8,256]{5,4,3,2,1,0:T(8,128)S(1)}, f32[2,2,2,4,8,256]{5,4,3,2,1,0:T(8,128)S(1)}, u32[]{:S(2)}, u32[]{:S(2)}) collective-permute-start(f32[2,2,2,4,8,256]{5,4,3,2,1,0:T(8,128)S(1)} %maximum_select_fusion.e_ref), channel_id=1, source_target_pairs={{0,8},{8,0},{16,24},{24,16},{1,9},{9,1},{17,25},{25,17},{2,10},{10... | collective-permute-start | bytes 786440 | tf_op jit(solution)/shard_map/ppermute | solution.py:445
  120.9 1.6 %collective-permute-start.22 = (f32[64,1024]{1,0:T(8,128)S(1)}, f32[64,1024]{1,0:T(8,128)S(1)}, u32[]{:S(2)}, u32[]{:S(2)}) collective-permute-start(f32[64,1024]{1,0:T(8,128)S(1)} %pad_maximum_fusion.8.own_ref), channel_id=1, source_target_pairs={{0,8},{8,0},{16,24},{24,16},{1,9},{9,1},{17,25},{25,17},{2,10},{10... | collective-permute-start | bytes 786440 | tf_op jit(solution)/shard_map/ppermute | solution.py:445

commit v3 on v2

--- a/solution.py
+++ b/solution.py
@@ -152,11 +152,15 @@
             sl, ph = pair(own[i], target)
             obs.append(sl)
             near = near + ph
-            for b in others:
+            for k, b in enumerate(others):
                 sl, ph = pair(own[i], b)
                 dsum[i] = dsum[i] + sl
-                cross = cross + ph
-                n_cross += 1
+                if k % mloc == i:
+                    cross = cross + ph
+                    n_cross += 1
+                elif k % mloc > i:
+                    inner = inner + ph
+                    n_inner += 1
             for j in range(i + 1, mloc):
                 sl, ph = pair(own[i], own[j])
                 dsum[i] = dsum[i] + sl
@@ -205,8 +209,6 @@
         if first:
             acc[...] = jnp.zeros_like(acc)
             extra_ref[...] = jnp.zeros_like(extra_ref)
-        else:
-            extra_ref[...] = extra_in[...]
         work(False)
 
     @pl.when((step > 0) & (step < end))
@@ -280,12 +282,12 @@
         aliases = {}
     else:
         kernel_fn = kernel
-        in_specs += [held(acc), const(extra)]
+        in_specs += [held(acc), held(extra)]
         args += [acc, extra]
-        aliases = {11: 2}
+        aliases = {11: 2, 12: 1}
     out_shape = [
         pltpu.VMEM((p // t, h, mloc * t), jnp.bfloat16),
-        jax.ShapeDtypeStruct((vp, h), jnp.float32),
+        pltpu.VMEM((vp, h), jnp.float32),
         pltpu.VMEM((h, h), jnp.float32),
     ]
     if last:

time: 124 us -> 123 us (level)
  no operation moved by 1% of the time
where the time goes in v3:
time: 123 us
  Pallas kernels  68.8 us (56%)
  waiting for transfers between devices  30 us (24%)
  starting transfers between devices  22.1 us (18%)
    pallas_call x4, Pallas kernels, backward(): pl.pallas_call(kernel_fn, grid=(steps + 1,), in_specs=in_specs, out_specs...  26.2 us
    pallas_call x4, Pallas kernels, forward(): pl.pallas_call(forward_kernel, grid=(tiles,), in_specs=[pl.BlockSpec((mlo...  25.4 us
    pallas_call x4, Pallas kernels, input_gradient(): pl.pallas_call(input_kernel, grid=(steps,), in_specs=in_specs, out_specs=...  13.9 us
    ppermute x3, waiting for transfers between devices, shards(): to_hi = lambda a, k: lax.ppermute(a, 'grid', shift_hi(k))  13.1 us
    ppermute x12, starting transfers between devices, shards(): to_core = lambda a: lax.ppermute(a, 'mem', swap_core)  7.1 us
    ppermute x7, starting transfers between devices, shards(): to_x = lambda a: lax.ppermute(a, 'mem', swap_x)  6.97 us
    ppermute x7, waiting for transfers between devices, shards(): to_x = lambda a: lax.ppermute(a, 'mem', swap_x)  6.23 us
    ppermute x12, waiting for transfers between devices, shards(): to_core = lambda a: lax.ppermute(a, 'mem', swap_core)  4.19 us
  transfers between devices with their start and end apart: 26, of which 12 were waited for; matrix products, arithmetic and copies ran while one was open for 0% of the time, Pallas kernels for 44%

profile of v3, /device:TPU:9, one launch (start us, length us, event | category | flops | bytes accessed | tf_op | source)
XLA Modules:
  0.0 122.6 jit_solution(4826049529199912641)
XLA Ops:
  0.7 7.1 %forward_part.4 = (bf16[2,2,1024,256]{3,2,1,0:T(8,128)(2,1)S(1)}, f32[2,2,1024,256]{3,2,1,0:T(8,128)S(1)}, f32[200,512]{1,0:T(8,128)S(1)}) custom-call(bf16[2,1024,2048]{2,1,0:T(8,128)(2,1)} %hid_ref.6, bf16[1024,1024]{1,0:T(8,128)(2,1)} %w_ref.8, f32[1,1024]{1,0:T(1,128)} %bitcast.61, bf16[100,1024]{1,0:T(8,128)(2,1)} %wo_ref.9, f32[1,100]{1,0:T(1,128)} %bitcast.67), custom_call_target="tpu_custom_call" | custom-call | flops 2097152 | bytes 2097152 | tf_op jit(solution)/shard_map/forward_part/pallas_call | solution.py:86
  7.7 1.3 %collective-permute-start.6 = (f32[200,512]{1,0:T(8,128)S(1)}, f32[200,512]{1,0:T(8,128)S(1)}, u32[]{:S(2)}, u32[]{:S(2)}) collective-permute-start(f32[200,512]{1,0:T(8,128)S(1)} %get-tuple-element.63.refs_0_), channel_id=1, source_target_pairs={{0,16},{8,24},{16,0},{24,8},{1,17},{9,25},{17,1},{25,9},{2,18},{10... | collective-permute-start | bytes 1228808 | tf_op jit(solution)/shard_map/ppermute | solution.py:446
  9.0 6.1 %forward_part.5 = (bf16[2,2,1024,256]{3,2,1,0:T(8,128)(2,1)S(1)}, f32[2,2,1024,256]{3,2,1,0:T(8,128)S(1)}, f32[200,512]{1,0:T(8,128)S(1)}) custom-call(bf16[2,1024,2048]{2,1,0:T(8,128)(2,1)} %hid_ref.6, bf16[1024,1024]{1,0:T(8,128)(2,1)S(1)} %copy-done, f32[1,1024]{1,0:T(1,128)} %bitcast.62, bf16[100,1024]{1,0:T(8,128)(2,1)} %wo_ref.9, f32[1,100]{1,0:T(1,128)} %bitcast.68), custom_call_target="tpu_custom_call" | custom-call | flops 2097152 | bytes 2097152 | tf_op jit(solution)/shard_map/forward_part/pallas_call | solution.py:86
  15.1 0.3 collective-permute-start.3
  15.4 1.2 %collective-permute-start.5 = (f32[200,512]{1,0:T(8,128)S(1)}, f32[200,512]{1,0:T(8,128)S(1)}, u32[]{:S(2)}, u32[]{:S(2)}) collective-permute-start(f32[200,512]{1,0:T(8,128)S(1)} %get-tuple-element.63.refs_0_), channel_id=1, source_target_pairs={{0,8},{8,0},{16,24},{24,16},{1,9},{9,1},{17,25},{25,17},{2,10},{10... | collective-permute-start | bytes 1228808 | tf_op jit(solution)/shard_map/ppermute | solution.py:447
  16.7 2.2 %transposes.1 = (bf16[1024,1024]{1,0:T(8,128)(2,1)S(1)}, bf16[1024,128]{1,0:T(8,128)(2,1)S(1)}) custom-call(bf16[1024,1024]{1,0:T(8,128)(2,1)S(1)} %copy-done, bf16[100,1024]{1,0:T(8,128)(2,1)} %wo_ref.9), custom_call_target="tpu_custom_call" | custom-call | flops 2048 | bytes 2048 | tf_op jit(solution)/shard_map/transposes/pallas_call | solution.py:331
  18.9 1.9 %collective-permute-start.7 = (f32[200,512]{1,0:T(8,128)S(1)}, f32[200,512]{1,0:T(8,128)S(1)}, u32[]{:S(2)}, u32[]{:S(2)}) collective-permute-start(f32[200,512]{1,0:T(8,128)S(1)} %collective-permute-done.6.refs_2_), channel_id=1, source_target_pairs={{0,8},{8,0},{16,24},{24,16},{1,9},{9,1},{17,25},{25,17},{2,10},{10... | collective-permute-start | bytes 1228808 | tf_op jit(solution)/shard_map/ppermute | solution.py:447
  20.8 6.1 %forward_part.6 = (bf16[2,2,1024,256]{3,2,1,0:T(8,128)(2,1)S(1)}, f32[2,2,1024,256]{3,2,1,0:T(8,128)S(1)}, f32[200,512]{1,0:T(8,128)S(1)}) custom-call(bf16[2,1024,2048]{2,1,0:T(8,128)(2,1)} %hid_ref.6, bf16[1024,1024]{1,0:T(8,128)(2,1)S(1)} %copy-done, f32[1,1024]{1,0:T(1,128)} %bitcast.63, bf16[100,1024]{1,0:T(8,128)(2,1)} %wo_ref.9, f32[1,100]{1,0:T(1,128)} %bitcast.69), custom_call_target="tpu_custom_call" | custom-call | flops 2097152 | bytes 2097152 | tf_op jit(solution)/shard_map/forward_part/pallas_call | solution.py:86
  27.0 1.3 %collective-permute-start.10 = (f32[200,512]{1,0:T(8,128)S(1)}, f32[200,512]{1,0:T(8,128)S(1)}, u32[]{:S(2)}, u32[]{:S(2)}) collective-permute-start(f32[200,512]{1,0:T(8,128)S(1)} %get-tuple-element.70.f_ref), channel_id=1, source_target_pairs={{0,16},{8,24},{16,0},{24,8},{1,17},{9,25},{17,1},{25,9},{2,18},{10... | collective-permute-start | bytes 1228808 | tf_op jit(solution)/shard_map/ppermute | solution.py:446
  28.3 6.1 %forward_part.7 = (bf16[2,2,1024,256]{3,2,1,0:T(8,128)(2,1)S(1)}, f32[2,2,1024,256]{3,2,1,0:T(8,128)S(1)}, f32[200,512]{1,0:T(8,128)S(1)}) custom-call(bf16[2,1024,2048]{2,1,0:T(8,128)(2,1)} %hid_ref.6, bf16[1024,1024]{1,0:T(8,128)(2,1)S(1)} %copy-done, f32[1,1024]{1,0:T(1,128)} %bitcast.64, bf16[100,1024]{1,0:T(8,128)(2,1)} %wo_ref.9, f32[1,100]{1,0:T(1,128)} %bitcast.70), custom_call_target="tpu_custom_call" | custom-call | flops 2097152 | bytes 2097152 | tf_op jit(solution)/shard_map/forward_part/pallas_call | solution.py:86
  34.4 0.4 collective-permute-start.4
  34.7 0.2 collective-permute-start.1
  35.0 0.5 collective-permute-start.9
  35.5 6.7 %backward_part.4 = (bf16[2,1024,512]{2,1,0:T(8,128)(2,1)S(1)}, f32[128,1024]{1,0:T(8,128)S(1)}, f32[1024,1024]{1,0:T(8,128)S(1)}) custom-call(f32[200,512]{1,0:T(8,128)S(1)} %get-tuple-element.63.refs_0_, f32[200,512]{1,0:T(8,128)S(1)} %collective-permute-done.5.refs_1_, f32[200,512]{1,0:T(8,128)S(1)} %collective-permute-done.6.refs_2_, ...), custom_call_target="tpu_custom_call" | custom-call | flops 2097152 | bytes 2097152 | tf_op jit(solution)/shard_map/backward_part/pallas_call | solution.py:300
  42.3 0.5 collective-permute-start.11
  42.8 6.3 %backward_part.5 = (bf16[2,1024,512]{2,1,0:T(8,128)(2,1)S(1)}, f32[128,1024]{1,0:T(8,128)S(1)}, f32[1024,1024]{1,0:T(8,128)S(1)}) custom-call(f32[200,512]{1,0:T(8,128)S(1)} %get-tuple-element.65.f_ref, f32[200,512]{1,0:T(8,128)S(1)} %collective-permute-done.2.fc_ref, ...), custom_call_target="tpu_custom_call", output_to_operand_aliasing={{2}: (11, {}), {1}: (12, {})} | custom-call | flops 2097152 | bytes 2097152 | tf_op jit(solution)/shard_map/backward_part/pallas_call | solution.py:300
  49.2 0.1 collective-permute-start.8
  49.3 6.5 %backward_part.6 = (bf16[2,1024,512]{2,1,0:T(8,128)(2,1)S(1)}, f32[128,1024]{1,0:T(8,128)S(1)}, f32[1024,1024]{1,0:T(8,128)S(1)}) custom-call(f32[200,512]{1,0:T(8,128)S(1)} %get-tuple-element.70.f_ref, f32[200,512]{1,0:T(8,128)S(1)} %collective-permute-done.9.fc_ref, ...), custom_call_target="tpu_custom_call", output_to_operand_aliasing={{2}: (11, {}), {1}: (12, {})} | custom-call | flops 2097152 | bytes 2097152 | tf_op jit(solution)/shard_map/backward_part/pallas_call | solution.py:300
  55.9 6.7 %backward_part.7 = (bf16[2,1024,512]{2,1,0:T(8,128)(2,1)S(1)}, f32[128,1024]{1,0:T(8,128)S(1)}, f32[1024,1024]{1,0:T(8,128)S(1)}, f32[2,2,4,72,256]{4,3,2,1,0:T(...) custom-call(f32[200,512]{1,0:T(8,128)S(1)} %get-tuple-element.72.f_r, ...), custom_call_target="tpu_custom_call", output_to_operand_aliasing={{2}: (11, {}), {1}: (12, {})} | custom-call | flops 2097152 | bytes 2097152 | tf_op jit(solution)/shard_map/backward_part/pallas_call | solution.py:300
  62.6 0.4 collective-permute-start.12
  62.9 0.2 collective-permute-start.13
  63.1 2.3 %collective-permute-done.12 = f32[2,2,4,72,256]{4,3,2,1,0:T(8,128)S(1)} collective-permute-done((f32[2,2,4,72,256]{4,3,2,1,0:T(8,128)S(1)}, f32[2,2,4,72,256]{4,3,2,1,0:T(8,128)S(1)}, u32[]{:S(2)}, u32[]{:S(2)}) %collective-permute-start.12) | collective-permute-done | bytes 1179680 | tf_op jit(solution)/shard_map/ppermute | solution.py:447
  65.6 1.3 %collective-permute-start.14 = (f32[2,4,72,256]{3,2,1,0:T(8,128)S(1)}, f32[2,4,72,256]{3,2,1,0:T(8,128)S(1)}, u32[]{:S(2)}, u32[]{:S(2)}) collective-permute-start(f32[2,4,72,256]{3,2,1,0:T(8,128)S(1)} %fusion.5), channel_id=1, source_target_pairs={{0,16},{8,24},{16,0},{24,8},{1,17},{9,25},{17,1},{25,9},{2,18},{10... | collective-permute-start | bytes 1769480 | tf_op jit(solution)/shard_map/ppermute | solution.py:446
  66.8 0.3 collective-permute-done.13
  67.2 1.3 %collective-permute-start.15 = (f32[2,4,72,256]{3,2,1,0:T(8,128)S(1)}, f32[2,4,72,256]{3,2,1,0:T(8,128)S(1)}, u32[]{:S(2)}, u32[]{:S(2)}) collective-permute-start(f32[2,4,72,256]{3,2,1,0:T(8,128)S(1)} %fusion.4), channel_id=1, source_target_pairs={{0,1},{1,0},{2,3},{3,2},{4,5},{5,4},{6,7},{7,6},{8,9},{9,8},{10,11... | collective-permute-start | bytes 1769480 | tf_op jit(solution)/shard_map/ppermute | solution.py:448
  68.6 3.5 %grad_hidden_part.4.refs_0_ = bf16[2,1024,2048]{2,1,0:T(8,128)(2,1)} custom-call(bf16[1024,1024]{1,0:T(8,128)(2,1)S(1)} %get-tuple-element.67.wt_ref, bf16[2,1024,512]{2,1,0:T(8,128)(2,1)S(1)} %get-tuple-element.100.gp_ref), custom_call_target="tpu_custom_call" | custom-call | flops 2097152 | bytes 2097152 | tf_op jit(solution)/shard_map/grad_hidden_part/pallas_call | solution.py:405
  72.0 3.5 %grad_hidden_part.5.refs_0_ = bf16[2,1024,2048]{2,1,0:T(8,128)(2,1)} custom-call(bf16[1024,1024]{1,0:T(8,128)(2,1)S(1)} %get-tuple-element.67.wt_ref, bf16[2,1024,512]{2,1,0:T(8,128)(2,1)S(1)} %get-tuple-element.99.gp_ref, bf16[2,1024,2048]{2,1,0:T(8,128)(2,1)} %grad_hidden_part.4.refs_0_), custom_call_target="tpu_custom_call", output_to_operand_aliasing={{}: (2, {})} | custom-call | flops 2097152 | bytes 2097152 | tf_op jit(solution)/shard_map/grad_hidden_part/pallas_call | solution.py:405
  75.5 4.7 %collective-permute-done.14 = f32[2,4,72,256]{3,2,1,0:T(8,128)S(1)} collective-permute-done((f32[2,4,72,256]{3,2,1,0:T(8,128)S(1)}, f32[2,4,72,256]{3,2,1,0:T(8,128)S(1)}, u32[]{:S(2)}, u32[]{:S(2)}) %collective-permute-start.14) | collective-permute-done | bytes 589856 | tf_op jit(solution)/shard_map/ppermute | solution.py:446
  80.4 1.3 %collective-permute-start.16 = (f32[4,72,256]{2,1,0:T(8,128)S(1)}, f32[4,72,256]{2,1,0:T(8,128)S(1)}, u32[]{:S(2)}, u32[]{:S(2)}) collective-permute-start(f32[4,72,256]{2,1,0:T(8,128)S(1)} %get-tuple-element.121), channel_id=1, source_target_pairs={{0,1},{1,0},{2,3},{3,2},{4,5},{5,4},{6,7},{7,6},{8,9},{9,8},{10,11... | collective-permute-start | bytes 884744 | tf_op jit(solution)/shard_map/ppermute | solution.py:448
  81.7 0.2 collective-permute-done.15
  82.1 1.3 %collective-permute-start.17 = (f32[4,72,256]{2,1,0:T(8,128)S(1)}, f32[4,72,256]{2,1,0:T(8,128)S(1)}, u32[]{:S(2)}, u32[]{:S(2)}) collective-permute-start(f32[4,72,256]{2,1,0:T(8,128)S(1)} %get-tuple-element.119), channel_id=1, source_target_pairs={{0,16},{8,24},{16,0},{24,8},{1,17},{9,25},{17,1},{25,9},{2,18},{10... | collective-permute-start | bytes 884744 | tf_op jit(solution)/shard_map/ppermute | solution.py:446
  83.4 3.5 %grad_hidden_part.6.refs_0_ = bf16[2,1024,2048]{2,1,0:T(8,128)(2,1)} custom-call(bf16[1024,1024]{1,0:T(8,128)(2,1)S(1)} %get-tuple-element.67.wt_ref, bf16[2,1024,512]{2,1,0:T(8,128)(2,1)S(1)} %get-tuple-element.106.gp_ref, bf16[2,1024,2048]{2,1,0:T(8,128)(2,1)} %grad_hidden_part.5.refs_0_), custom_call_target="tpu_custom_call", output_to_operand_aliasing={{}: (2, {})} | custom-call | flops 2097152 | bytes 2097152 | tf_op jit(solution)/shard_map/grad_hidden_part/pallas_call | solution.py:405
  86.8 1.0 collective-permute-done.16
  87.9 1.5 %collective-permute-done.17 = f32[4,72,256]{2,1,0:T(8,128)S(1)} collective-permute-done((f32[4,72,256]{2,1,0:T(8,128)S(1)}, f32[4,72,256]{2,1,0:T(8,128)S(1)}, u32[]{:S(2)}, u32[]{:S(2)}) %collective-permute-start.17) | collective-permute-done | bytes 294944 | tf_op jit(solution)/shard_map/ppermute | solution.py:446
  89.6 1.4 %collective-permute-start.18 = (f32[192,256]{1,0:T(8,128)S(1)}, f32[192,256]{1,0:T(8,128)S(1)}, u32[]{:S(2)}, u32[]{:S(2)}) collective-permute-start(f32[192,256]{1,0:T(8,128)S(1)} %get-tuple-element.140), channel_id=1, source_target_pairs={{0,2},{1,3},{2,4},{3,5},{4,6},{5,7},{6,0},{7,1},{8,10},{9,11},{10,... | collective-permute-start | bytes 589832 | tf_op jit(solution)/shard_map/ppermute | solution.py:449
  90.9 1.1 collective-permute-start.19
  92.0 1.4 %collective-permute-start.20 = (f32[192,256]{1,0:T(8,128)S(1)}, f32[192,256]{1,0:T(8,128)S(1)}, u32[]{:S(2)}, u32[]{:S(2)}) collective-permute-start(f32[192,256]{1,0:T(8,128)S(1)} %get-tuple-element.139), channel_id=1, source_target_pairs={{0,6},{1,7},{2,0},{3,1},{4,2},{5,3},{6,4},{7,5},{8,14},{9,15},{10,... | collective-permute-start | bytes 589832 | tf_op jit(solution)/shard_map/ppermute | solution.py:449
  93.4 3.5 %grad_hidden_part.7 = bf16[2,1024,2048]{2,1,0:T(8,128)(2,1)} custom-call(bf16[1024,1024]{1,0:T(8,128)(2,1)S(1)} %get-tuple-element.67.wt_ref, bf16[2,1024,512]{2,1,0:T(8,128)(2,1)S(1)} %get-tuple-element.110.gp_ref, bf16[2,1024,2048]{2,1,0:T(8,128)(2,1)} %grad_hidden_part.6.refs_0_), custom_call_target="tpu_custom_call", output_to_operand_aliasing={{}: (2, {})} | custom-call | flops 2097152 | bytes 2097152 | tf_op jit(solution)/shard_map/grad_hidden_part/pallas_call | solution.py:405
  96.9 9.0 %collective-permute-done.19 = f32[192,256]{1,0:T(8,128)S(1)} collective-permute-done((f32[192,256]{1,0:T(8,128)S(1)}, f32[192,256]{1,0:T(8,128)S(1)}, u32[]{:S(2)}, u32[]{:S(2)}) %collective-permute-start.19) | collective-permute-done | bytes 196640 | tf_op jit(solution)/shard_map/ppermute | solution.py:449
  105.9 4.0 %collective-permute-done.20 = f32[192,256]{1,0:T(8,128)S(1)} collective-permute-done((f32[192,256]{1,0:T(8,128)S(1)}, f32[192,256]{1,0:T(8,128)S(1)}, u32[]{:S(2)}, u32[]{:S(2)}) %collective-permute-start.20) | collective-permute-done | bytes 196640 | tf_op jit(solution)/shard_map/ppermute | solution.py:449
  110.0 1.3 %collective-permute-start.21 = (f32[192,256]{1,0:T(8,128)S(1)}, f32[192,256]{1,0:T(8,128)S(1)}, u32[]{:S(2)}, u32[]{:S(2)}) collective-permute-start(f32[192,256]{1,0:T(8,128)S(1)} %add_add_fusion), channel_id=1, source_target_pairs={{0,16},{8,24},{16,0},{24,8},{1,17},{9,25},{17,1},{25,9},{2,18},{10... | collective-permute-start | bytes 589832 | tf_op jit(solution)/shard_map/ppermute | solution.py:446
  111.3 1.4 %collective-permute-start.23 = (f32[1,64,256]{2,1,0:T(8,128)S(1)}, f32[1,64,256]{2,1,0:T(8,128)S(1)}, u32[]{:S(2)}, u32[]{:S(2)}) collective-permute-start(f32[1,64,256]{2,1,0:T(8,128)S(1)} %get-tuple-element.131), channel_id=1, source_target_pairs={{0,1},{1,0},{2,3},{3,2},{4,5},{5,4},{6,7},{7,6},{8,9},{9,8},{10,11... | collective-permute-start | bytes 196616 | tf_op jit(solution)/shard_map/ppermute | solution.py:536
  112.8 2.0 %collective-permute-done.23 = f32[1,64,256]{2,1,0:T(8,128)S(1)} collective-permute-done((f32[1,64,256]{2,1,0:T(8,128)S(1)}, f32[1,64,256]{2,1,0:T(8,128)S(1)}, u32[]{:S(2)}, u32[]{:S(2)}) %collective-permute-start.23) | collective-permute-done | bytes 65568 | tf_op jit(solution)/shard_map/ppermute | solution.py:536
  114.7 3.4 %collective-permute-done.24 = f32[1,64,256]{2,1,0:T(8,128)S(1)} collective-permute-done((f32[1,64,256]{2,1,0:T(8,128)S(1)}, f32[1,64,256]{2,1,0:T(8,128)S(1)}, u32[]{:S(2)}, u32[]{:S(2)}) %collective-permute-start.24) | collective-permute-done | bytes 65568 | tf_op jit(solution)/shard_map/ppermute | solution.py:538
  118.3 1.7 %collective-permute-start.25 = (f32[2,2,2,4,8,256]{5,4,3,2,1,0:T(8,128)S(1)}, f32[2,2,2,4,8,256]{5,4,3,2,1,0:T(8,128)S(1)}, u32[]{:S(2)}, u32[]{:S(2)}) collective-permute-start(f32[2,2,2,4,8,256]{5,4,3,2,1,0:T(8,128)S(1)} %maximum_select_fusion.e_ref), channel_id=1, source_target_pairs={{0,8},{8,0},{16,24},{24,16},{1,9},{9,1},{17,25},{25,17},{2,10},{10... | collective-permute-start | bytes 786440 | tf_op jit(solution)/shard_map/ppermute | solution.py:447
  120.1 1.0 collective-permute-done.25.f_ref
  121.1 0.5 collective-permute-done.22.other_ref
  121.6 1.0 last.1
  (47 shorter events, 1.2 us)
Async XLA Ops:
  0.6 8.4 %copy-start = (bf16[1024,1024]{1,0:T(8,128)(2,1)S(1)}, bf16[1024,1024]{1,0:T(8,128)(2,1)}, u32[]{:S(2)}) copy-start(bf16[1024,1024]{1,0:T(8,128)(2,1)} %w_ref.8) | copy-start | bytes 6291460
  7.7 11.2 %collective-permute-start.6 = (f32[200,512]{1,0:T(8,128)S(1)}, f32[200,512]{1,0:T(8,128)S(1)}, u32[]{:S(2)}, u32[]{:S(2)}) collective-permute-start(f32[200,512]{1,0:T(8,128)S(1)} %get-tuple-element.63.refs_0_), channel_id=1, source_target_pairs={{0,16},{8,24},{16,0},{24,8},{1,17},{9,25},{17,1},{25,9},{2,18},{10... | collective-permute-start | bytes 1228808 | tf_op jit(solution)/shard_map/ppermute | solution.py:446
  15.1 19.3 %collective-permute-start.3 = (f32[200,512]{1,0:T(8,128)S(1)}, f32[200,512]{1,0:T(8,128)S(1)}, u32[]{:S(2)}, u32[]{:S(2)}) collective-permute-start(f32[200,512]{1,0:T(8,128)S(1)} %get-tuple-element.65.f_ref), channel_id=1, source_target_pairs={{0,16},{8,24},{16,0},{24,8},{1,17},{9,25},{17,1},{25,9},{2,18},{10... | collective-permute-start | bytes 1228808 | tf_op jit(solution)/shard_map/ppermute | solution.py:446
  15.4 19.3 %collective-permute-start.5 = (f32[200,512]{1,0:T(8,128)S(1)}, f32[200,512]{1,0:T(8,128)S(1)}, u32[]{:S(2)}, u32[]{:S(2)}) collective-permute-start(f32[200,512]{1,0:T(8,128)S(1)} %get-tuple-element.63.refs_0_), channel_id=1, source_target_pairs={{0,8},{8,0},{16,24},{24,16},{1,9},{9,1},{17,25},{25,17},{2,10},{10... | collective-permute-start | bytes 1228808 | tf_op jit(solution)/shard_map/ppermute | solution.py:447
  16.7 25.7 %collective-permute-start.2 = (f32[200,512]{1,0:T(8,128)S(1)}, f32[200,512]{1,0:T(8,128)S(1)}, u32[]{:S(2)}, u32[]{:S(2)}) collective-permute-start(f32[200,512]{1,0:T(8,128)S(1)} %get-tuple-element.65.f_ref), channel_id=1, source_target_pairs={{0,8},{8,0},{16,24},{24,16},{1,9},{9,1},{17,25},{25,17},{2,10},{10... | collective-permute-start | bytes 1228808 | tf_op jit(solution)/shard_map/ppermute | solution.py:447
  18.9 16.1 %collective-permute-start.7 = (f32[200,512]{1,0:T(8,128)S(1)}, f32[200,512]{1,0:T(8,128)S(1)}, u32[]{:S(2)}, u32[]{:S(2)}) collective-permute-start(f32[200,512]{1,0:T(8,128)S(1)} %collective-permute-done.6.refs_2_), channel_id=1, source_target_pairs={{0,8},{8,0},{16,24},{24,16},{1,9},{9,1},{17,25},{25,17},{2,10},{10... | collective-permute-start | bytes 1228808 | tf_op jit(solution)/shard_map/ppermute | solution.py:447
  26.9 8.6 %copy-start.1 = (f32[100,2048]{1,0:T(8,128)S(1)}, f32[100,2048]{1,0:T(8,128)}, u32[]{:S(2)}) copy-start(f32[100,2048]{1,0:T(8,128)} %target_ref.5) | copy-start | bytes 2457604
  26.9 8.6 %copy-start.2 = (f32[2048]{0:T(1024)S(1)}, f32[2048]{0:T(1024)}, u32[]{:S(2)}) copy-start(f32[2048]{0:T(1024)} %param.10) | copy-start | bytes 24580
  27.0 8.6 %copy-start.3 = (f32[100]{0:T(128)S(1)}, f32[100]{0:T(128)}, u32[]{:S(2)}) copy-start(f32[100]{0:T(128)} %param.11) | copy-start | bytes 1204
  27.0 15.3 %collective-permute-start.10 = (f32[200,512]{1,0:T(8,128)S(1)}, f32[200,512]{1,0:T(8,128)S(1)}, u32[]{:S(2)}, u32[]{:S(2)}) collective-permute-start(f32[200,512]{1,0:T(8,128)S(1)} %get-tuple-element.70.f_ref), channel_id=1, source_target_pairs={{0,16},{8,24},{16,0},{24,8},{1,17},{9,25},{17,1},{25,9},{2,18},{10... | collective-permute-start | bytes 1228808 | tf_op jit(solution)/shard_map/ppermute | solution.py:446
  34.4 8.4 %collective-permute-start.4 = (f32[200,512]{1,0:T(8,128)S(1)}, f32[200,512]{1,0:T(8,128)S(1)}, u32[]{:S(2)}, u32[]{:S(2)}) collective-permute-start(f32[200,512]{1,0:T(8,128)S(1)} %collective-permute-done.3.fx_ref), channel_id=1, source_target_pairs={{0,8},{8,0},{16,24},{24,16},{1,9},{9,1},{17,25},{25,17},{2,10},{10... | collective-permute-start | bytes 1228808 | tf_op jit(solution)/shard_map/ppermute | solution.py:447
  34.7 14.4 %collective-permute-start.1 = (f32[200,512]{1,0:T(8,128)S(1)}, f32[200,512]{1,0:T(8,128)S(1)}, u32[]{:S(2)}, u32[]{:S(2)}) collective-permute-start(f32[200,512]{1,0:T(8,128)S(1)} %get-tuple-element.72.f_ref), channel_id=1, source_target_pairs={{0,16},{8,24},{16,0},{24,8},{1,17},{9,25},{17,1},{25,9},{2,18},{10... | collective-permute-start | bytes 1228808 | tf_op jit(solution)/shard_map/ppermute | solution.py:446
  35.0 14.3 %collective-permute-start.9 = (f32[200,512]{1,0:T(8,128)S(1)}, f32[200,512]{1,0:T(8,128)S(1)}, u32[]{:S(2)}, u32[]{:S(2)}) collective-permute-start(f32[200,512]{1,0:T(8,128)S(1)} %get-tuple-element.70.f_ref), channel_id=1, source_target_pairs={{0,8},{8,0},{16,24},{24,16},{1,9},{9,1},{17,25},{25,17},{2,10},{10... | collective-permute-start | bytes 1228808 | tf_op jit(solution)/shard_map/ppermute | solution.py:447
  42.2 13.6 %collective-permute-start = (f32[200,512]{1,0:T(8,128)S(1)}, f32[200,512]{1,0:T(8,128)S(1)}, u32[]{:S(2)}, u32[]{:S(2)}) collective-permute-start(f32[200,512]{1,0:T(8,128)S(1)} %get-tuple-element.72.f_ref), channel_id=1, source_target_pairs={{0,8},{8,0},{16,24},{24,16},{1,9},{9,1},{17,25},{25,17},{2,10},{10... | collective-permute-start | bytes 1228808 | tf_op jit(solution)/shard_map/ppermute | solution.py:447
  42.3 7.0 %collective-permute-start.11 = (f32[200,512]{1,0:T(8,128)S(1)}, f32[200,512]{1,0:T(8,128)S(1)}, u32[]{:S(2)}, u32[]{:S(2)}) collective-permute-start(f32[200,512]{1,0:T(8,128)S(1)} %collective-permute-done.10.fx_ref), channel_id=1, source_target_pairs={{0,8},{8,0},{16,24},{24,16},{1,9},{9,1},{17,25},{25,17},{2,10},{10... | collective-permute-start | bytes 1228808 | tf_op jit(solution)/shard_map/ppermute | solution.py:447
  49.2 6.7 %collective-permute-start.8 = (f32[200,512]{1,0:T(8,128)S(1)}, f32[200,512]{1,0:T(8,128)S(1)}, u32[]{:S(2)}, u32[]{:S(2)}) collective-permute-start(f32[200,512]{1,0:T(8,128)S(1)} %collective-permute-done.1.fx_ref), channel_id=1, source_target_pairs={{0,8},{8,0},{16,24},{24,16},{1,9},{9,1},{17,25},{25,17},{2,10},{10... | collective-permute-start | bytes 1228808 | tf_op jit(solution)/shard_map/ppermute | solution.py:447
  62.6 2.9 %collective-permute-start.12 = (f32[2,2,4,72,256]{4,3,2,1,0:T(8,128)S(1)}, f32[2,2,4,72,256]{4,3,2,1,0:T(8,128)S(1)}, u32[]{:S(2)}, u32[]{:S(2)}) collective-permute-start(f32[2,2,4,72,256]{4,3,2,1,0:T(8,128)S(1)} %get-tuple-element.96), channel_id=1, source_target_pairs={{0,8},{8,0},{16,24},{24,16},{1,9},{9,1},{17,25},{25,17},{2,10},{10... | collective-permute-start | bytes 3538952 | tf_op jit(solution)/shard_map/ppermute | solution.py:447
  62.9 4.2 %collective-permute-start.13 = (f32[2,2,4,72,256]{4,3,2,1,0:T(8,128)S(1)}, f32[2,2,4,72,256]{4,3,2,1,0:T(8,128)S(1)}, u32[]{:S(2)}, u32[]{:S(2)}) collective-permute-start(f32[2,2,4,72,256]{4,3,2,1,0:T(8,128)S(1)} %get-tuple-element.98), channel_id=1, source_target_pairs={{0,8},{8,0},{16,24},{24,16},{1,9},{9,1},{17,25},{25,17},{2,10},{10... | collective-permute-start | bytes 3538952 | tf_op jit(solution)/shard_map/ppermute | solution.py:447
  65.6 14.7 %collective-permute-start.14 = (f32[2,4,72,256]{3,2,1,0:T(8,128)S(1)}, f32[2,4,72,256]{3,2,1,0:T(8,128)S(1)}, u32[]{:S(2)}, u32[]{:S(2)}) collective-permute-start(f32[2,4,72,256]{3,2,1,0:T(8,128)S(1)} %fusion.5), channel_id=1, source_target_pairs={{0,16},{8,24},{16,0},{24,8},{1,17},{9,25},{17,1},{25,9},{2,18},{10... | collective-permute-start | bytes 1769480 | tf_op jit(solution)/shard_map/ppermute | solution.py:446
  67.2 14.7 %collective-permute-start.15 = (f32[2,4,72,256]{3,2,1,0:T(8,128)S(1)}, f32[2,4,72,256]{3,2,1,0:T(8,128)S(1)}, u32[]{:S(2)}, u32[]{:S(2)}) collective-permute-start(f32[2,4,72,256]{3,2,1,0:T(8,128)S(1)} %fusion.4), channel_id=1, source_target_pairs={{0,1},{1,0},{2,3},{3,2},{4,5},{5,4},{6,7},{7,6},{8,9},{9,8},{10,11... | collective-permute-start | bytes 1769480 | tf_op jit(solution)/shard_map/ppermute | solution.py:448
  80.4 7.4 %collective-permute-start.16 = (f32[4,72,256]{2,1,0:T(8,128)S(1)}, f32[4,72,256]{2,1,0:T(8,128)S(1)}, u32[]{:S(2)}, u32[]{:S(2)}) collective-permute-start(f32[4,72,256]{2,1,0:T(8,128)S(1)} %get-tuple-element.121), channel_id=1, source_target_pairs={{0,1},{1,0},{2,3},{3,2},{4,5},{5,4},{6,7},{7,6},{8,9},{9,8},{10,11... | collective-permute-start | bytes 884744 | tf_op jit(solution)/shard_map/ppermute | solution.py:448
  82.1 7.3 %collective-permute-start.17 = (f32[4,72,256]{2,1,0:T(8,128)S(1)}, f32[4,72,256]{2,1,0:T(8,128)S(1)}, u32[]{:S(2)}, u32[]{:S(2)}) collective-permute-start(f32[4,72,256]{2,1,0:T(8,128)S(1)} %get-tuple-element.119), channel_id=1, source_target_pairs={{0,16},{8,24},{16,0},{24,8},{1,17},{9,25},{17,1},{25,9},{2,18},{10... | collective-permute-start | bytes 884744 | tf_op jit(solution)/shard_map/ppermute | solution.py:446
  89.6 7.3 %collective-permute-start.18 = (f32[192,256]{1,0:T(8,128)S(1)}, f32[192,256]{1,0:T(8,128)S(1)}, u32[]{:S(2)}, u32[]{:S(2)}) collective-permute-start(f32[192,256]{1,0:T(8,128)S(1)} %get-tuple-element.140), channel_id=1, source_target_pairs={{0,2},{1,3},{2,4},{3,5},{4,6},{5,7},{6,0},{7,1},{8,10},{9,11},{10,... | collective-permute-start | bytes 589832 | tf_op jit(solution)/shard_map/ppermute | solution.py:449
  90.9 15.0 %collective-permute-start.19 = (f32[192,256]{1,0:T(8,128)S(1)}, f32[192,256]{1,0:T(8,128)S(1)}, u32[]{:S(2)}, u32[]{:S(2)}) collective-permute-start(f32[192,256]{1,0:T(8,128)S(1)} %get-tuple-element.138), channel_id=1, source_target_pairs={{0,4},{1,5},{2,6},{3,7},{4,0},{5,1},{6,2},{7,3},{8,12},{9,13},{10,... | collective-permute-start | bytes 589832 | tf_op jit(solution)/shard_map/ppermute | solution.py:449
  92.0 17.9 %collective-permute-start.20 = (f32[192,256]{1,0:T(8,128)S(1)}, f32[192,256]{1,0:T(8,128)S(1)}, u32[]{:S(2)}, u32[]{:S(2)}) collective-permute-start(f32[192,256]{1,0:T(8,128)S(1)} %get-tuple-element.139), channel_id=1, source_target_pairs={{0,6},{1,7},{2,0},{3,1},{4,2},{5,3},{6,4},{7,5},{8,14},{9,15},{10,... | collective-permute-start | bytes 589832 | tf_op jit(solution)/shard_map/ppermute | solution.py:449
  110.0 8.2 %collective-permute-start.21 = (f32[192,256]{1,0:T(8,128)S(1)}, f32[192,256]{1,0:T(8,128)S(1)}, u32[]{:S(2)}, u32[]{:S(2)}) collective-permute-start(f32[192,256]{1,0:T(8,128)S(1)} %add_add_fusion), channel_id=1, source_target_pairs={{0,16},{8,24},{16,0},{24,8},{1,17},{9,25},{17,1},{25,9},{2,18},{10... | collective-permute-start | bytes 589832 | tf_op jit(solution)/shard_map/ppermute | solution.py:446
  111.3 3.5 %collective-permute-start.23 = (f32[1,64,256]{2,1,0:T(8,128)S(1)}, f32[1,64,256]{2,1,0:T(8,128)S(1)}, u32[]{:S(2)}, u32[]{:S(2)}) collective-permute-start(f32[1,64,256]{2,1,0:T(8,128)S(1)} %get-tuple-element.131), channel_id=1, source_target_pairs={{0,1},{1,0},{2,3},{3,2},{4,5},{5,4},{6,7},{7,6},{8,9},{9,8},{10,11... | collective-permute-start | bytes 196616 | tf_op jit(solution)/shard_map/ppermute | solution.py:536
  112.7 5.5 %collective-permute-start.24 = (f32[1,64,256]{2,1,0:T(8,128)S(1)}, f32[1,64,256]{2,1,0:T(8,128)S(1)}, u32[]{:S(2)}, u32[]{:S(2)}) collective-permute-start(f32[1,64,256]{2,1,0:T(8,128)S(1)} %get-tuple-element.131), channel_id=1, source_target_pairs={{0,17},{1,16},{2,19},{3,18},{4,21},{5,20},{6,23},{7,22},{8,25},{9,... | collective-permute-start | bytes 196616 | tf_op jit(solution)/shard_map/ppermute | solution.py:538
  118.3 2.9 %collective-permute-start.25 = (f32[2,2,2,4,8,256]{5,4,3,2,1,0:T(8,128)S(1)}, f32[2,2,2,4,8,256]{5,4,3,2,1,0:T(8,128)S(1)}, u32[]{:S(2)}, u32[]{:S(2)}) collective-permute-start(f32[2,2,2,4,8,256]{5,4,3,2,1,0:T(8,128)S(1)} %maximum_select_fusion.e_ref), channel_id=1, source_target_pairs={{0,8},{8,0},{16,24},{24,16},{1,9},{9,1},{17,25},{25,17},{2,10},{10... | collective-permute-start | bytes 786440 | tf_op jit(solution)/shard_map/ppermute | solution.py:447
  120.0 1.6 %collective-permute-start.22 = (f32[64,1024]{1,0:T(8,128)S(1)}, f32[64,1024]{1,0:T(8,128)S(1)}, u32[]{:S(2)}, u32[]{:S(2)}) collective-permute-start(f32[64,1024]{1,0:T(8,128)S(1)} %pad_maximum_fusion.8.own_ref), channel_id=1, source_target_pairs={{0,8},{8,0},{16,24},{24,16},{1,9},{9,1},{17,25},{25,17},{2,10},{10... | collective-permute-start | bytes 786440 | tf_op jit(solution)/shard_map/ppermute | solution.py:447

commit v4 on v3

--- a/solution.py
+++ b/solution.py
@@ -46,6 +46,7 @@
             )
         half[...] = wo_ref[...] * jnp.bfloat16(0.5)
 
+    cols = pl.ds(pl.multiple_of(step * t, t), t)
     hid = jnp.concatenate([hid_ref[m] for m in range(mloc)], axis=1)
     out = jnp.broadcast_to(column(bo_ref[...], v), (v, mloc * t))
     for k in range(len(slabs) + 1):
@@ -71,7 +72,7 @@
         out = out + jnp.dot(half[:, rows], act, preferred_element_type=jnp.float32)
     for m in range(mloc):
         for r0 in range(0, v, 8):
-            f_ref[field_rows(v, mloc, m, r0), :] = out[r0 : r0 + 8, m * t : (m + 1) * t]
+            f_ref[field_rows(v, mloc, m, r0), cols] = out[r0 : r0 + 8, m * t : (m + 1) * t]
 
 
 def forward(start, p, hidden, w_inner, b_inner, w_out, b_out, vmem):
@@ -96,12 +97,12 @@
         out_specs=[
             held,
             held,
-            pl.BlockSpec((mloc * v, t), lambda s: (0, s)),
+            pl.BlockSpec((mloc * v, p), whole),
         ],
         out_shape=[
             pltpu.VMEM(shape, jnp.bfloat16),
             pltpu.VMEM(shape, jnp.float32),
-            jax.ShapeDtypeStruct((mloc * v, p), jnp.float32),
+            pltpu.VMEM((mloc * v, p), jnp.float32),
         ],
         scratch_shapes=[
             pltpu.VMEM((h, 128), jnp.float32),
@@ -141,8 +142,9 @@
     def scores(r0, vw, area):
         rows = pl.ds(r0, min(8, v - r0))
         places = [field_rows(v, mloc, m, r0) for m in range(mloc)]
-        own = [f_ref[place, :] for place in places]
-        others = [ref[place, :] for ref in (fc_ref, fx_ref, fxc_ref) for place in places]
+        cols = pl.ds(pl.multiple_of(step * t, t), t)
+        own = [f_ref[place, cols] for place in places]
+        others = [ref[place, cols] for ref in (fc_ref, fx_ref, fxc_ref) for place in places]
         target = target_ref[rows, :]
         dsum = [jnp.zeros_like(target) for _ in range(mloc)]
         obs = []
@@ -263,8 +265,8 @@
     once = pl.Buffered(1)
     steps = p // t
     ahead = lambda s: jnp.minimum(s, steps - 1)
-    f_spec = pl.BlockSpec((mloc * v, t), lambda s: (0, ahead(s)))
     whole = lambda s: (0, 0)
+    f_spec = pl.BlockSpec((mloc * v, p), whole)
     const = lambda a: pl.BlockSpec(a.shape, whole, pipeline_mode=once)
     held = lambda a: pl.BlockSpec(a.shape, lambda s: (0,) * len(a.shape))
     in_specs = [f_spec] * 4 + [

time: 123 us -> 123 us (level)
  no operation moved by 1% of the time
where the time goes in v4:
time: 123 us; the launch traced here: 122 us
  Pallas kernels  68.3 us (56%)
  waiting for transfers between devices  30.1 us (24%)
  starting transfers between devices  22 us (18%)
    pallas_call x4, Pallas kernels, backward(): pl.pallas_call(kernel_fn, grid=(steps + 1,), in_specs=in_specs, out_specs...  25.9 us
    pallas_call x4, Pallas kernels, forward(): pl.pallas_call(forward_kernel, grid=(tiles,), in_specs=[pl.BlockSpec((mlo...  25.3 us
    pallas_call x4, Pallas kernels, input_gradient(): pl.pallas_call(input_kernel, grid=(steps,), in_specs=in_specs, out_specs=...  13.9 us
    ppermute x3, waiting for transfers between devices, shards(): to_hi = lambda a, k: lax.ppermute(a, 'grid', shift_hi(k))  13.1 us
    ppermute x12, starting transfers between devices, shards(): to_core = lambda a: lax.ppermute(a, 'mem', swap_core)  7.13 us
    ppermute x7, starting transfers between devices, shards(): to_x = lambda a: lax.ppermute(a, 'mem', swap_x)  6.92 us
    ppermute x7, waiting for transfers between devices, shards(): to_x = lambda a: lax.ppermute(a, 'mem', swap_x)  6.26 us
    ppermute x12, waiting for transfers between devices, shards(): to_core = lambda a: lax.ppermute(a, 'mem', swap_core)  4.22 us
  transfers between devices with their start and end apart: 26, of which 12 were waited for; matrix products, arithmetic and copies ran while one was open for 0% of the time, Pallas kernels for 44%

profile of v4, /device:TPU:9, one launch (start us, length us, event | category | flops | bytes accessed | tf_op | source)
XLA Modules:
  0.0 122.2 jit_solution(9179667421982623700)
XLA Ops:
  0.7 7.0 %forward_part.4 = (bf16[2,2,1024,256]{3,2,1,0:T(8,128)(2,1)S(1)}, f32[2,2,1024,256]{3,2,1,0:T(8,128)S(1)}, f32[200,512]{1,0:T(8,128)S(1)}) custom-call(bf16[2,1024,2048]{2,1,0:T(8,128)(2,1)} %hid_ref.6, bf16[1024,1024]{1,0:T(8,128)(2,1)} %w_ref.8, f32[1,1024]{1,0:T(1,128)} %bitcast.61, bf16[100,1024]{1,0:T(8,128)(2,1)} %wo_ref.9, f32[1,100]{1,0:T(1,128)} %bitcast.67), custom_call_target="tpu_custom_call" | custom-call | flops 2097152 | bytes 2097152 | tf_op jit(solution)/shard_map/forward_part/pallas_call | solution.py:87
  7.7 1.3 %collective-permute-start.6 = (f32[200,512]{1,0:T(8,128)S(1)}, f32[200,512]{1,0:T(8,128)S(1)}, u32[]{:S(2)}, u32[]{:S(2)}) collective-permute-start(f32[200,512]{1,0:T(8,128)S(1)} %get-tuple-element.63.refs_0_), channel_id=1, source_target_pairs={{0,16},{8,24},{16,0},{24,8},{1,17},{9,25},{17,1},{25,9},{2,18},{10... | collective-permute-start | bytes 1228808 | tf_op jit(solution)/shard_map/ppermute | solution.py:448
  9.0 6.1 %forward_part.5 = (bf16[2,2,1024,256]{3,2,1,0:T(8,128)(2,1)S(1)}, f32[2,2,1024,256]{3,2,1,0:T(8,128)S(1)}, f32[200,512]{1,0:T(8,128)S(1)}) custom-call(bf16[2,1024,2048]{2,1,0:T(8,128)(2,1)} %hid_ref.6, bf16[1024,1024]{1,0:T(8,128)(2,1)S(1)} %copy-done, f32[1,1024]{1,0:T(1,128)} %bitcast.62, bf16[100,1024]{1,0:T(8,128)(2,1)} %wo_ref.9, f32[1,100]{1,0:T(1,128)} %bitcast.68), custom_call_target="tpu_custom_call" | custom-call | flops 2097152 | bytes 2097152 | tf_op jit(solution)/shard_map/forward_part/pallas_call | solution.py:87
  15.1 0.3 collective-permute-start.3
  15.4 1.2 %collective-permute-start.5 = (f32[200,512]{1,0:T(8,128)S(1)}, f32[200,512]{1,0:T(8,128)S(1)}, u32[]{:S(2)}, u32[]{:S(2)}) collective-permute-start(f32[200,512]{1,0:T(8,128)S(1)} %get-tuple-element.63.refs_0_), channel_id=1, source_target_pairs={{0,8},{8,0},{16,24},{24,16},{1,9},{9,1},{17,25},{25,17},{2,10},{10... | collective-permute-start | bytes 1228808 | tf_op jit(solution)/shard_map/ppermute | solution.py:449
  16.6 2.2 %transposes.1 = (bf16[1024,1024]{1,0:T(8,128)(2,1)S(1)}, bf16[1024,128]{1,0:T(8,128)(2,1)S(1)}) custom-call(bf16[1024,1024]{1,0:T(8,128)(2,1)S(1)} %copy-done, bf16[100,1024]{1,0:T(8,128)(2,1)} %wo_ref.9), custom_call_target="tpu_custom_call" | custom-call | flops 2048 | bytes 2048 | tf_op jit(solution)/shard_map/transposes/pallas_call | solution.py:333
  18.8 2.0 %collective-permute-start.7 = (f32[200,512]{1,0:T(8,128)S(1)}, f32[200,512]{1,0:T(8,128)S(1)}, u32[]{:S(2)}, u32[]{:S(2)}) collective-permute-start(f32[200,512]{1,0:T(8,128)S(1)} %collective-permute-done.6.refs_2_), channel_id=1, source_target_pairs={{0,8},{8,0},{16,24},{24,16},{1,9},{9,1},{17,25},{25,17},{2,10},{10... | collective-permute-start | bytes 1228808 | tf_op jit(solution)/shard_map/ppermute | solution.py:449
  20.8 6.1 %forward_part.6 = (bf16[2,2,1024,256]{3,2,1,0:T(8,128)(2,1)S(1)}, f32[2,2,1024,256]{3,2,1,0:T(8,128)S(1)}, f32[200,512]{1,0:T(8,128)S(1)}) custom-call(bf16[2,1024,2048]{2,1,0:T(8,128)(2,1)} %hid_ref.6, bf16[1024,1024]{1,0:T(8,128)(2,1)S(1)} %copy-done, f32[1,1024]{1,0:T(1,128)} %bitcast.63, bf16[100,1024]{1,0:T(8,128)(2,1)} %wo_ref.9, f32[1,100]{1,0:T(1,128)} %bitcast.69), custom_call_target="tpu_custom_call" | custom-call | flops 2097152 | bytes 2097152 | tf_op jit(solution)/shard_map/forward_part/pallas_call | solution.py:87
  26.9 1.3 %collective-permute-start.10 = (f32[200,512]{1,0:T(8,128)S(1)}, f32[200,512]{1,0:T(8,128)S(1)}, u32[]{:S(2)}, u32[]{:S(2)}) collective-permute-start(f32[200,512]{1,0:T(8,128)S(1)} %get-tuple-element.70.f_ref), channel_id=1, source_target_pairs={{0,16},{8,24},{16,0},{24,8},{1,17},{9,25},{17,1},{25,9},{2,18},{10... | collective-permute-start | bytes 1228808 | tf_op jit(solution)/shard_map/ppermute | solution.py:448
  28.2 6.1 %forward_part.7 = (bf16[2,2,1024,256]{3,2,1,0:T(8,128)(2,1)S(1)}, f32[2,2,1024,256]{3,2,1,0:T(8,128)S(1)}, f32[200,512]{1,0:T(8,128)S(1)}) custom-call(bf16[2,1024,2048]{2,1,0:T(8,128)(2,1)} %hid_ref.6, bf16[1024,1024]{1,0:T(8,128)(2,1)S(1)} %copy-done, f32[1,1024]{1,0:T(1,128)} %bitcast.64, bf16[100,1024]{1,0:T(8,128)(2,1)} %wo_ref.9, f32[1,100]{1,0:T(1,128)} %bitcast.70), custom_call_target="tpu_custom_call" | custom-call | flops 2097152 | bytes 2097152 | tf_op jit(solution)/shard_map/forward_part/pallas_call | solution.py:87
  34.3 0.4 collective-permute-start.4
  34.6 0.3 collective-permute-start.1
  34.9 0.5 collective-permute-start.9
  35.4 6.7 %backward_part.4 = (bf16[2,1024,512]{2,1,0:T(8,128)(2,1)S(1)}, f32[128,1024]{1,0:T(8,128)S(1)}, f32[1024,1024]{1,0:T(8,128)S(1)}) custom-call(f32[200,512]{1,0:T(8,128)S(1)} %get-tuple-element.63.refs_0_, f32[200,512]{1,0:T(8,128)S(1)} %collective-permute-done.5.refs_1_, f32[200,512]{1,0:T(8,128)S(1)} %collective-permute-done.6.refs_2_, ...), custom_call_target="tpu_custom_call" | custom-call | flops 2097152 | bytes 2097152 | tf_op jit(solution)/shard_map/backward_part/pallas_call | solution.py:302
  42.2 0.5 collective-permute-start.11
  42.7 6.2 %backward_part.5 = (bf16[2,1024,512]{2,1,0:T(8,128)(2,1)S(1)}, f32[128,1024]{1,0:T(8,128)S(1)}, f32[1024,1024]{1,0:T(8,128)S(1)}) custom-call(f32[200,512]{1,0:T(8,128)S(1)} %get-tuple-element.65.f_ref, f32[200,512]{1,0:T(8,128)S(1)} %collective-permute-done.2.fc_ref, ...), custom_call_target="tpu_custom_call", output_to_operand_aliasing={{2}: (11, {}), {1}: (12, {})} | custom-call | flops 2097152 | bytes 2097152 | tf_op jit(solution)/shard_map/backward_part/pallas_call | solution.py:302
  48.9 0.1 collective-permute-start.8
  49.1 6.4 %backward_part.6 = (bf16[2,1024,512]{2,1,0:T(8,128)(2,1)S(1)}, f32[128,1024]{1,0:T(8,128)S(1)}, f32[1024,1024]{1,0:T(8,128)S(1)}) custom-call(f32[200,512]{1,0:T(8,128)S(1)} %get-tuple-element.70.f_ref, f32[200,512]{1,0:T(8,128)S(1)} %collective-permute-done.9.fc_ref, ...), custom_call_target="tpu_custom_call", output_to_operand_aliasing={{2}: (11, {}), {1}: (12, {})} | custom-call | flops 2097152 | bytes 2097152 | tf_op jit(solution)/shard_map/backward_part/pallas_call | solution.py:302
  55.5 6.6 %backward_part.7 = (bf16[2,1024,512]{2,1,0:T(8,128)(2,1)S(1)}, f32[128,1024]{1,0:T(8,128)S(1)}, f32[1024,1024]{1,0:T(8,128)S(1)}, f32[2,2,4,72,256]{4,3,2,1,0:T(...) custom-call(f32[200,512]{1,0:T(8,128)S(1)} %get-tuple-element.72.f_r, ...), custom_call_target="tpu_custom_call", output_to_operand_aliasing={{2}: (11, {}), {1}: (12, {})} | custom-call | flops 2097152 | bytes 2097152 | tf_op jit(solution)/shard_map/backward_part/pallas_call | solution.py:302
  62.1 0.4 collective-permute-start.12
  62.5 0.2 collective-permute-start.13
  62.7 2.3 %collective-permute-done.12 = f32[2,2,4,72,256]{4,3,2,1,0:T(8,128)S(1)} collective-permute-done((f32[2,2,4,72,256]{4,3,2,1,0:T(8,128)S(1)}, f32[2,2,4,72,256]{4,3,2,1,0:T(8,128)S(1)}, u32[]{:S(2)}, u32[]{:S(2)}) %collective-permute-start.12) | collective-permute-done | bytes 1179680 | tf_op jit(solution)/shard_map/ppermute | solution.py:449
  65.1 1.3 %collective-permute-start.14 = (f32[2,4,72,256]{3,2,1,0:T(8,128)S(1)}, f32[2,4,72,256]{3,2,1,0:T(8,128)S(1)}, u32[]{:S(2)}, u32[]{:S(2)}) collective-permute-start(f32[2,4,72,256]{3,2,1,0:T(8,128)S(1)} %fusion.5), channel_id=1, source_target_pairs={{0,16},{8,24},{16,0},{24,8},{1,17},{9,25},{17,1},{25,9},{2,18},{10... | collective-permute-start | bytes 1769480 | tf_op jit(solution)/shard_map/ppermute | solution.py:448
  66.4 0.3 collective-permute-done.13
  66.8 1.3 %collective-permute-start.15 = (f32[2,4,72,256]{3,2,1,0:T(8,128)S(1)}, f32[2,4,72,256]{3,2,1,0:T(8,128)S(1)}, u32[]{:S(2)}, u32[]{:S(2)}) collective-permute-start(f32[2,4,72,256]{3,2,1,0:T(8,128)S(1)} %fusion.4), channel_id=1, source_target_pairs={{0,1},{1,0},{2,3},{3,2},{4,5},{5,4},{6,7},{7,6},{8,9},{9,8},{10,11... | collective-permute-start | bytes 1769480 | tf_op jit(solution)/shard_map/ppermute | solution.py:450
  68.1 3.5 %grad_hidden_part.4.refs_0_ = bf16[2,1024,2048]{2,1,0:T(8,128)(2,1)} custom-call(bf16[1024,1024]{1,0:T(8,128)(2,1)S(1)} %get-tuple-element.67.wt_ref, bf16[2,1024,512]{2,1,0:T(8,128)(2,1)S(1)} %get-tuple-element.100.gp_ref), custom_call_target="tpu_custom_call" | custom-call | flops 2097152 | bytes 2097152 | tf_op jit(solution)/shard_map/grad_hidden_part/pallas_call | solution.py:407
  71.6 3.5 %grad_hidden_part.5.refs_0_ = bf16[2,1024,2048]{2,1,0:T(8,128)(2,1)} custom-call(bf16[1024,1024]{1,0:T(8,128)(2,1)S(1)} %get-tuple-element.67.wt_ref, bf16[2,1024,512]{2,1,0:T(8,128)(2,1)S(1)} %get-tuple-element.99.gp_ref, bf16[2,1024,2048]{2,1,0:T(8,128)(2,1)} %grad_hidden_part.4.refs_0_), custom_call_target="tpu_custom_call", output_to_operand_aliasing={{}: (2, {})} | custom-call | flops 2097152 | bytes 2097152 | tf_op jit(solution)/shard_map/grad_hidden_part/pallas_call | solution.py:407
  75.1 4.7 %collective-permute-done.14 = f32[2,4,72,256]{3,2,1,0:T(8,128)S(1)} collective-permute-done((f32[2,4,72,256]{3,2,1,0:T(8,128)S(1)}, f32[2,4,72,256]{3,2,1,0:T(8,128)S(1)}, u32[]{:S(2)}, u32[]{:S(2)}) %collective-permute-start.14) | collective-permute-done | bytes 589856 | tf_op jit(solution)/shard_map/ppermute | solution.py:448
  79.9 1.3 %collective-permute-start.16 = (f32[4,72,256]{2,1,0:T(8,128)S(1)}, f32[4,72,256]{2,1,0:T(8,128)S(1)}, u32[]{:S(2)}, u32[]{:S(2)}) collective-permute-start(f32[4,72,256]{2,1,0:T(8,128)S(1)} %get-tuple-element.121), channel_id=1, source_target_pairs={{0,1},{1,0},{2,3},{3,2},{4,5},{5,4},{6,7},{7,6},{8,9},{9,8},{10,11... | collective-permute-start | bytes 884744 | tf_op jit(solution)/shard_map/ppermute | solution.py:450
  81.2 0.2 collective-permute-done.15
  81.6 1.3 %collective-permute-start.17 = (f32[4,72,256]{2,1,0:T(8,128)S(1)}, f32[4,72,256]{2,1,0:T(8,128)S(1)}, u32[]{:S(2)}, u32[]{:S(2)}) collective-permute-start(f32[4,72,256]{2,1,0:T(8,128)S(1)} %get-tuple-element.119), channel_id=1, source_target_pairs={{0,16},{8,24},{16,0},{24,8},{1,17},{9,25},{17,1},{25,9},{2,18},{10... | collective-permute-start | bytes 884744 | tf_op jit(solution)/shard_map/ppermute | solution.py:448
  82.9 3.5 %grad_hidden_part.6.refs_0_ = bf16[2,1024,2048]{2,1,0:T(8,128)(2,1)} custom-call(bf16[1024,1024]{1,0:T(8,128)(2,1)S(1)} %get-tuple-element.67.wt_ref, bf16[2,1024,512]{2,1,0:T(8,128)(2,1)S(1)} %get-tuple-element.106.gp_ref, bf16[2,1024,2048]{2,1,0:T(8,128)(2,1)} %grad_hidden_part.5.refs_0_), custom_call_target="tpu_custom_call", output_to_operand_aliasing={{}: (2, {})} | custom-call | flops 2097152 | bytes 2097152 | tf_op jit(solution)/shard_map/grad_hidden_part/pallas_call | solution.py:407
  86.4 1.0 collective-permute-done.16
  87.4 1.5 %collective-permute-done.17 = f32[4,72,256]{2,1,0:T(8,128)S(1)} collective-permute-done((f32[4,72,256]{2,1,0:T(8,128)S(1)}, f32[4,72,256]{2,1,0:T(8,128)S(1)}, u32[]{:S(2)}, u32[]{:S(2)}) %collective-permute-start.17) | collective-permute-done | bytes 294944 | tf_op jit(solution)/shard_map/ppermute | solution.py:448
  89.1 1.4 %collective-permute-start.18 = (f32[192,256]{1,0:T(8,128)S(1)}, f32[192,256]{1,0:T(8,128)S(1)}, u32[]{:S(2)}, u32[]{:S(2)}) collective-permute-start(f32[192,256]{1,0:T(8,128)S(1)} %get-tuple-element.140), channel_id=1, source_target_pairs={{0,2},{1,3},{2,4},{3,5},{4,6},{5,7},{6,0},{7,1},{8,10},{9,11},{10,... | collective-permute-start | bytes 589832 | tf_op jit(solution)/shard_map/ppermute | solution.py:451
  90.5 1.1 collective-permute-start.19
  91.6 1.4 %collective-permute-start.20 = (f32[192,256]{1,0:T(8,128)S(1)}, f32[192,256]{1,0:T(8,128)S(1)}, u32[]{:S(2)}, u32[]{:S(2)}) collective-permute-start(f32[192,256]{1,0:T(8,128)S(1)} %get-tuple-element.139), channel_id=1, source_target_pairs={{0,6},{1,7},{2,0},{3,1},{4,2},{5,3},{6,4},{7,5},{8,14},{9,15},{10,... | collective-permute-start | bytes 589832 | tf_op jit(solution)/shard_map/ppermute | solution.py:451
  93.0 3.5 %grad_hidden_part.7 = bf16[2,1024,2048]{2,1,0:T(8,128)(2,1)} custom-call(bf16[1024,1024]{1,0:T(8,128)(2,1)S(1)} %get-tuple-element.67.wt_ref, bf16[2,1024,512]{2,1,0:T(8,128)(2,1)S(1)} %get-tuple-element.110.gp_ref, bf16[2,1024,2048]{2,1,0:T(8,128)(2,1)} %grad_hidden_part.6.refs_0_), custom_call_target="tpu_custom_call", output_to_operand_aliasing={{}: (2, {})} | custom-call | flops 2097152 | bytes 2097152 | tf_op jit(solution)/shard_map/grad_hidden_part/pallas_call | solution.py:407
  96.4 9.0 %collective-permute-done.19 = f32[192,256]{1,0:T(8,128)S(1)} collective-permute-done((f32[192,256]{1,0:T(8,128)S(1)}, f32[192,256]{1,0:T(8,128)S(1)}, u32[]{:S(2)}, u32[]{:S(2)}) %collective-permute-start.19) | collective-permute-done | bytes 196640 | tf_op jit(solution)/shard_map/ppermute | solution.py:451
  105.5 4.0 %collective-permute-done.20 = f32[192,256]{1,0:T(8,128)S(1)} collective-permute-done((f32[192,256]{1,0:T(8,128)S(1)}, f32[192,256]{1,0:T(8,128)S(1)}, u32[]{:S(2)}, u32[]{:S(2)}) %collective-permute-start.20) | collective-permute-done | bytes 196640 | tf_op jit(solution)/shard_map/ppermute | solution.py:451
  109.5 1.3 %collective-permute-start.21 = (f32[192,256]{1,0:T(8,128)S(1)}, f32[192,256]{1,0:T(8,128)S(1)}, u32[]{:S(2)}, u32[]{:S(2)}) collective-permute-start(f32[192,256]{1,0:T(8,128)S(1)} %add_add_fusion), channel_id=1, source_target_pairs={{0,16},{8,24},{16,0},{24,8},{1,17},{9,25},{17,1},{25,9},{2,18},{10... | collective-permute-start | bytes 589832 | tf_op jit(solution)/shard_map/ppermute | solution.py:448
  110.8 1.4 %collective-permute-start.23 = (f32[1,64,256]{2,1,0:T(8,128)S(1)}, f32[1,64,256]{2,1,0:T(8,128)S(1)}, u32[]{:S(2)}, u32[]{:S(2)}) collective-permute-start(f32[1,64,256]{2,1,0:T(8,128)S(1)} %get-tuple-element.131), channel_id=1, source_target_pairs={{0,1},{1,0},{2,3},{3,2},{4,5},{5,4},{6,7},{7,6},{8,9},{9,8},{10,11... | collective-permute-start | bytes 196616 | tf_op jit(solution)/shard_map/ppermute | solution.py:538
  112.3 2.0 %collective-permute-done.23 = f32[1,64,256]{2,1,0:T(8,128)S(1)} collective-permute-done((f32[1,64,256]{2,1,0:T(8,128)S(1)}, f32[1,64,256]{2,1,0:T(8,128)S(1)}, u32[]{:S(2)}, u32[]{:S(2)}) %collective-permute-start.23) | collective-permute-done | bytes 65568 | tf_op jit(solution)/shard_map/ppermute | solution.py:538
  114.3 3.4 %collective-permute-done.24 = f32[1,64,256]{2,1,0:T(8,128)S(1)} collective-permute-done((f32[1,64,256]{2,1,0:T(8,128)S(1)}, f32[1,64,256]{2,1,0:T(8,128)S(1)}, u32[]{:S(2)}, u32[]{:S(2)}) %collective-permute-start.24) | collective-permute-done | bytes 65568 | tf_op jit(solution)/shard_map/ppermute | solution.py:540
  117.8 1.7 %collective-permute-start.25 = (f32[2,2,2,4,8,256]{5,4,3,2,1,0:T(8,128)S(1)}, f32[2,2,2,4,8,256]{5,4,3,2,1,0:T(8,128)S(1)}, u32[]{:S(2)}, u32[]{:S(2)}) collective-permute-start(f32[2,2,2,4,8,256]{5,4,3,2,1,0:T(8,128)S(1)} %maximum_select_fusion.e_ref), channel_id=1, source_target_pairs={{0,8},{8,0},{16,24},{24,16},{1,9},{9,1},{17,25},{25,17},{2,10},{10... | collective-permute-start | bytes 786440 | tf_op jit(solution)/shard_map/ppermute | solution.py:449
  119.7 1.0 collective-permute-done.25.f_ref
  120.7 0.5 collective-permute-done.22.other_ref
  121.2 1.0 last.1
  (47 shorter events, 1.2 us)
Async XLA Ops:
  0.6 8.3 %copy-start = (bf16[1024,1024]{1,0:T(8,128)(2,1)S(1)}, bf16[1024,1024]{1,0:T(8,128)(2,1)}, u32[]{:S(2)}) copy-start(bf16[1024,1024]{1,0:T(8,128)(2,1)} %w_ref.8) | copy-start | bytes 6291460
  7.7 11.1 %collective-permute-start.6 = (f32[200,512]{1,0:T(8,128)S(1)}, f32[200,512]{1,0:T(8,128)S(1)}, u32[]{:S(2)}, u32[]{:S(2)}) collective-permute-start(f32[200,512]{1,0:T(8,128)S(1)} %get-tuple-element.63.refs_0_), channel_id=1, source_target_pairs={{0,16},{8,24},{16,0},{24,8},{1,17},{9,25},{17,1},{25,9},{2,18},{10... | collective-permute-start | bytes 1228808 | tf_op jit(solution)/shard_map/ppermute | solution.py:448
  15.1 19.2 %collective-permute-start.3 = (f32[200,512]{1,0:T(8,128)S(1)}, f32[200,512]{1,0:T(8,128)S(1)}, u32[]{:S(2)}, u32[]{:S(2)}) collective-permute-start(f32[200,512]{1,0:T(8,128)S(1)} %get-tuple-element.65.f_ref), channel_id=1, source_target_pairs={{0,16},{8,24},{16,0},{24,8},{1,17},{9,25},{17,1},{25,9},{2,18},{10... | collective-permute-start | bytes 1228808 | tf_op jit(solution)/shard_map/ppermute | solution.py:448
  15.4 19.3 %collective-permute-start.5 = (f32[200,512]{1,0:T(8,128)S(1)}, f32[200,512]{1,0:T(8,128)S(1)}, u32[]{:S(2)}, u32[]{:S(2)}) collective-permute-start(f32[200,512]{1,0:T(8,128)S(1)} %get-tuple-element.63.refs_0_), channel_id=1, source_target_pairs={{0,8},{8,0},{16,24},{24,16},{1,9},{9,1},{17,25},{25,17},{2,10},{10... | collective-permute-start | bytes 1228808 | tf_op jit(solution)/shard_map/ppermute | solution.py:449
  16.6 25.6 %collective-permute-start.2 = (f32[200,512]{1,0:T(8,128)S(1)}, f32[200,512]{1,0:T(8,128)S(1)}, u32[]{:S(2)}, u32[]{:S(2)}) collective-permute-start(f32[200,512]{1,0:T(8,128)S(1)} %get-tuple-element.65.f_ref), channel_id=1, source_target_pairs={{0,8},{8,0},{16,24},{24,16},{1,9},{9,1},{17,25},{25,17},{2,10},{10... | collective-permute-start | bytes 1228808 | tf_op jit(solution)/shard_map/ppermute | solution.py:449
  18.8 16.1 %collective-permute-start.7 = (f32[200,512]{1,0:T(8,128)S(1)}, f32[200,512]{1,0:T(8,128)S(1)}, u32[]{:S(2)}, u32[]{:S(2)}) collective-permute-start(f32[200,512]{1,0:T(8,128)S(1)} %collective-permute-done.6.refs_2_), channel_id=1, source_target_pairs={{0,8},{8,0},{16,24},{24,16},{1,9},{9,1},{17,25},{25,17},{2,10},{10... | collective-permute-start | bytes 1228808 | tf_op jit(solution)/shard_map/ppermute | solution.py:449
  26.9 8.5 %copy-start.1 = (f32[100,2048]{1,0:T(8,128)S(1)}, f32[100,2048]{1,0:T(8,128)}, u32[]{:S(2)}) copy-start(f32[100,2048]{1,0:T(8,128)} %target_ref.5) | copy-start | bytes 2457604
  26.9 8.5 %copy-start.2 = (f32[2048]{0:T(1024)S(1)}, f32[2048]{0:T(1024)}, u32[]{:S(2)}) copy-start(f32[2048]{0:T(1024)} %param.10) | copy-start | bytes 24580
  26.9 8.5 %copy-start.3 = (f32[100]{0:T(128)S(1)}, f32[100]{0:T(128)}, u32[]{:S(2)}) copy-start(f32[100]{0:T(128)} %param.11) | copy-start | bytes 1204
  26.9 15.2 %collective-permute-start.10 = (f32[200,512]{1,0:T(8,128)S(1)}, f32[200,512]{1,0:T(8,128)S(1)}, u32[]{:S(2)}, u32[]{:S(2)}) collective-permute-start(f32[200,512]{1,0:T(8,128)S(1)} %get-tuple-element.70.f_ref), channel_id=1, source_target_pairs={{0,16},{8,24},{16,0},{24,8},{1,17},{9,25},{17,1},{25,9},{2,18},{10... | collective-permute-start | bytes 1228808 | tf_op jit(solution)/shard_map/ppermute | solution.py:448
  34.3 8.4 %collective-permute-start.4 = (f32[200,512]{1,0:T(8,128)S(1)}, f32[200,512]{1,0:T(8,128)S(1)}, u32[]{:S(2)}, u32[]{:S(2)}) collective-permute-start(f32[200,512]{1,0:T(8,128)S(1)} %collective-permute-done.3.fx_ref), channel_id=1, source_target_pairs={{0,8},{8,0},{16,24},{24,16},{1,9},{9,1},{17,25},{25,17},{2,10},{10... | collective-permute-start | bytes 1228808 | tf_op jit(solution)/shard_map/ppermute | solution.py:449
  34.6 14.3 %collective-permute-start.1 = (f32[200,512]{1,0:T(8,128)S(1)}, f32[200,512]{1,0:T(8,128)S(1)}, u32[]{:S(2)}, u32[]{:S(2)}) collective-permute-start(f32[200,512]{1,0:T(8,128)S(1)} %get-tuple-element.72.f_ref), channel_id=1, source_target_pairs={{0,16},{8,24},{16,0},{24,8},{1,17},{9,25},{17,1},{25,9},{2,18},{10... | collective-permute-start | bytes 1228808 | tf_op jit(solution)/shard_map/ppermute | solution.py:448
  34.9 14.2 %collective-permute-start.9 = (f32[200,512]{1,0:T(8,128)S(1)}, f32[200,512]{1,0:T(8,128)S(1)}, u32[]{:S(2)}, u32[]{:S(2)}) collective-permute-start(f32[200,512]{1,0:T(8,128)S(1)} %get-tuple-element.70.f_ref), channel_id=1, source_target_pairs={{0,8},{8,0},{16,24},{24,16},{1,9},{9,1},{17,25},{25,17},{2,10},{10... | collective-permute-start | bytes 1228808 | tf_op jit(solution)/shard_map/ppermute | solution.py:449
  42.1 13.4 %collective-permute-start = (f32[200,512]{1,0:T(8,128)S(1)}, f32[200,512]{1,0:T(8,128)S(1)}, u32[]{:S(2)}, u32[]{:S(2)}) collective-permute-start(f32[200,512]{1,0:T(8,128)S(1)} %get-tuple-element.72.f_ref), channel_id=1, source_target_pairs={{0,8},{8,0},{16,24},{24,16},{1,9},{9,1},{17,25},{25,17},{2,10},{10... | collective-permute-start | bytes 1228808 | tf_op jit(solution)/shard_map/ppermute | solution.py:449
  42.2 6.9 %collective-permute-start.11 = (f32[200,512]{1,0:T(8,128)S(1)}, f32[200,512]{1,0:T(8,128)S(1)}, u32[]{:S(2)}, u32[]{:S(2)}) collective-permute-start(f32[200,512]{1,0:T(8,128)S(1)} %collective-permute-done.10.fx_ref), channel_id=1, source_target_pairs={{0,8},{8,0},{16,24},{24,16},{1,9},{9,1},{17,25},{25,17},{2,10},{10... | collective-permute-start | bytes 1228808 | tf_op jit(solution)/shard_map/ppermute | solution.py:449
  48.9 6.6 %collective-permute-start.8 = (f32[200,512]{1,0:T(8,128)S(1)}, f32[200,512]{1,0:T(8,128)S(1)}, u32[]{:S(2)}, u32[]{:S(2)}) collective-permute-start(f32[200,512]{1,0:T(8,128)S(1)} %collective-permute-done.1.fx_ref), channel_id=1, source_target_pairs={{0,8},{8,0},{16,24},{24,16},{1,9},{9,1},{17,25},{25,17},{2,10},{10... | collective-permute-start | bytes 1228808 | tf_op jit(solution)/shard_map/ppermute | solution.py:449
  62.1 2.9 %collective-permute-start.12 = (f32[2,2,4,72,256]{4,3,2,1,0:T(8,128)S(1)}, f32[2,2,4,72,256]{4,3,2,1,0:T(8,128)S(1)}, u32[]{:S(2)}, u32[]{:S(2)}) collective-permute-start(f32[2,2,4,72,256]{4,3,2,1,0:T(8,128)S(1)} %get-tuple-element.96), channel_id=1, source_target_pairs={{0,8},{8,0},{16,24},{24,16},{1,9},{9,1},{17,25},{25,17},{2,10},{10... | collective-permute-start | bytes 3538952 | tf_op jit(solution)/shard_map/ppermute | solution.py:449
  62.5 4.2 %collective-permute-start.13 = (f32[2,2,4,72,256]{4,3,2,1,0:T(8,128)S(1)}, f32[2,2,4,72,256]{4,3,2,1,0:T(8,128)S(1)}, u32[]{:S(2)}, u32[]{:S(2)}) collective-permute-start(f32[2,2,4,72,256]{4,3,2,1,0:T(8,128)S(1)} %get-tuple-element.98), channel_id=1, source_target_pairs={{0,8},{8,0},{16,24},{24,16},{1,9},{9,1},{17,25},{25,17},{2,10},{10... | collective-permute-start | bytes 3538952 | tf_op jit(solution)/shard_map/ppermute | solution.py:449
  65.1 14.7 %collective-permute-start.14 = (f32[2,4,72,256]{3,2,1,0:T(8,128)S(1)}, f32[2,4,72,256]{3,2,1,0:T(8,128)S(1)}, u32[]{:S(2)}, u32[]{:S(2)}) collective-permute-start(f32[2,4,72,256]{3,2,1,0:T(8,128)S(1)} %fusion.5), channel_id=1, source_target_pairs={{0,16},{8,24},{16,0},{24,8},{1,17},{9,25},{17,1},{25,9},{2,18},{10... | collective-permute-start | bytes 1769480 | tf_op jit(solution)/shard_map/ppermute | solution.py:448
  66.8 14.7 %collective-permute-start.15 = (f32[2,4,72,256]{3,2,1,0:T(8,128)S(1)}, f32[2,4,72,256]{3,2,1,0:T(8,128)S(1)}, u32[]{:S(2)}, u32[]{:S(2)}) collective-permute-start(f32[2,4,72,256]{3,2,1,0:T(8,128)S(1)} %fusion.4), channel_id=1, source_target_pairs={{0,1},{1,0},{2,3},{3,2},{4,5},{5,4},{6,7},{7,6},{8,9},{9,8},{10,11... | collective-permute-start | bytes 1769480 | tf_op jit(solution)/shard_map/ppermute | solution.py:450
  79.9 7.4 %collective-permute-start.16 = (f32[4,72,256]{2,1,0:T(8,128)S(1)}, f32[4,72,256]{2,1,0:T(8,128)S(1)}, u32[]{:S(2)}, u32[]{:S(2)}) collective-permute-start(f32[4,72,256]{2,1,0:T(8,128)S(1)} %get-tuple-element.121), channel_id=1, source_target_pairs={{0,1},{1,0},{2,3},{3,2},{4,5},{5,4},{6,7},{7,6},{8,9},{9,8},{10,11... | collective-permute-start | bytes 884744 | tf_op jit(solution)/shard_map/ppermute | solution.py:450
  81.6 7.3 %collective-permute-start.17 = (f32[4,72,256]{2,1,0:T(8,128)S(1)}, f32[4,72,256]{2,1,0:T(8,128)S(1)}, u32[]{:S(2)}, u32[]{:S(2)}) collective-permute-start(f32[4,72,256]{2,1,0:T(8,128)S(1)} %get-tuple-element.119), channel_id=1, source_target_pairs={{0,16},{8,24},{16,0},{24,8},{1,17},{9,25},{17,1},{25,9},{2,18},{10... | collective-permute-start | bytes 884744 | tf_op jit(solution)/shard_map/ppermute | solution.py:448
  89.1 7.3 %collective-permute-start.18 = (f32[192,256]{1,0:T(8,128)S(1)}, f32[192,256]{1,0:T(8,128)S(1)}, u32[]{:S(2)}, u32[]{:S(2)}) collective-permute-start(f32[192,256]{1,0:T(8,128)S(1)} %get-tuple-element.140), channel_id=1, source_target_pairs={{0,2},{1,3},{2,4},{3,5},{4,6},{5,7},{6,0},{7,1},{8,10},{9,11},{10,... | collective-permute-start | bytes 589832 | tf_op jit(solution)/shard_map/ppermute | solution.py:451
  90.5 15.0 %collective-permute-start.19 = (f32[192,256]{1,0:T(8,128)S(1)}, f32[192,256]{1,0:T(8,128)S(1)}, u32[]{:S(2)}, u32[]{:S(2)}) collective-permute-start(f32[192,256]{1,0:T(8,128)S(1)} %get-tuple-element.138), channel_id=1, source_target_pairs={{0,4},{1,5},{2,6},{3,7},{4,0},{5,1},{6,2},{7,3},{8,12},{9,13},{10,... | collective-permute-start | bytes 589832 | tf_op jit(solution)/shard_map/ppermute | solution.py:451
  91.6 17.9 %collective-permute-start.20 = (f32[192,256]{1,0:T(8,128)S(1)}, f32[192,256]{1,0:T(8,128)S(1)}, u32[]{:S(2)}, u32[]{:S(2)}) collective-permute-start(f32[192,256]{1,0:T(8,128)S(1)} %get-tuple-element.139), channel_id=1, source_target_pairs={{0,6},{1,7},{2,0},{3,1},{4,2},{5,3},{6,4},{7,5},{8,14},{9,15},{10,... | collective-permute-start | bytes 589832 | tf_op jit(solution)/shard_map/ppermute | solution.py:451
  109.5 8.2 %collective-permute-start.21 = (f32[192,256]{1,0:T(8,128)S(1)}, f32[192,256]{1,0:T(8,128)S(1)}, u32[]{:S(2)}, u32[]{:S(2)}) collective-permute-start(f32[192,256]{1,0:T(8,128)S(1)} %add_add_fusion), channel_id=1, source_target_pairs={{0,16},{8,24},{16,0},{24,8},{1,17},{9,25},{17,1},{25,9},{2,18},{10... | collective-permute-start | bytes 589832 | tf_op jit(solution)/shard_map/ppermute | solution.py:448
  110.8 3.5 %collective-permute-start.23 = (f32[1,64,256]{2,1,0:T(8,128)S(1)}, f32[1,64,256]{2,1,0:T(8,128)S(1)}, u32[]{:S(2)}, u32[]{:S(2)}) collective-permute-start(f32[1,64,256]{2,1,0:T(8,128)S(1)} %get-tuple-element.131), channel_id=1, source_target_pairs={{0,1},{1,0},{2,3},{3,2},{4,5},{5,4},{6,7},{7,6},{8,9},{9,8},{10,11... | collective-permute-start | bytes 196616 | tf_op jit(solution)/shard_map/ppermute | solution.py:538
  112.2 5.5 %collective-permute-start.24 = (f32[1,64,256]{2,1,0:T(8,128)S(1)}, f32[1,64,256]{2,1,0:T(8,128)S(1)}, u32[]{:S(2)}, u32[]{:S(2)}) collective-permute-start(f32[1,64,256]{2,1,0:T(8,128)S(1)} %get-tuple-element.131), channel_id=1, source_target_pairs={{0,17},{1,16},{2,19},{3,18},{4,21},{5,20},{6,23},{7,22},{8,25},{9,... | collective-permute-start | bytes 196616 | tf_op jit(solution)/shard_map/ppermute | solution.py:540
  117.8 2.9 %collective-permute-start.25 = (f32[2,2,2,4,8,256]{5,4,3,2,1,0:T(8,128)S(1)}, f32[2,2,2,4,8,256]{5,4,3,2,1,0:T(8,128)S(1)}, u32[]{:S(2)}, u32[]{:S(2)}) collective-permute-start(f32[2,2,2,4,8,256]{5,4,3,2,1,0:T(8,128)S(1)} %maximum_select_fusion.e_ref), channel_id=1, source_target_pairs={{0,8},{8,0},{16,24},{24,16},{1,9},{9,1},{17,25},{25,17},{2,10},{10... | collective-permute-start | bytes 786440 | tf_op jit(solution)/shard_map/ppermute | solution.py:449
  119.6 1.6 %collective-permute-start.22 = (f32[64,1024]{1,0:T(8,128)S(1)}, f32[64,1024]{1,0:T(8,128)S(1)}, u32[]{:S(2)}, u32[]{:S(2)}) collective-permute-start(f32[64,1024]{1,0:T(8,128)S(1)} %pad_maximum_fusion.8.own_ref), channel_id=1, source_target_pairs={{0,8},{8,0},{16,24},{24,16},{1,9},{9,1},{17,25},{25,17},{2,10},{10... | collective-permute-start | bytes 786440 | tf_op jit(solution)/shard_map/ppermute | solution.py:449

commit v5 on v4

--- a/solution.py
+++ b/solution.py
@@ -32,19 +32,21 @@
     return pl.ds(mloc * full + m * (v - full), v - full)
 
 
-def forward_kernel(hid_ref, w_ref, b_ref, wo_ref, bo_ref, act_ref, slope_ref, f_ref, bias, half, *slabs):
+def forward_kernel(first, hid_ref, w_ref, b_ref, wo_ref, bo_ref, act_ref, slope_ref, f_ref, bias, half, *slabs):
     step = pl.program_id(0)
     mloc, h, t = hid_ref.shape
     v = half.shape[0]
     size = h // len(slabs)
 
-    @pl.when(step == 0)
-    def _():
-        for k in range(h // 128):
-            bias[pl.ds(k * 128, 128), :] = jnp.broadcast_to(
-                column(b_ref[:, pl.ds(k * 128, 128)], 128), (128, 128)
-            )
-        half[...] = wo_ref[...] * jnp.bfloat16(0.5)
+    if first:
+
+        @pl.when(step == 0)
+        def _():
+            for k in range(h // 128):
+                bias[pl.ds(k * 128, 128), :] = jnp.broadcast_to(
+                    column(b_ref[:, pl.ds(k * 128, 128)], 128), (128, 128)
+                )
+            half[...] = wo_ref[...] * jnp.bfloat16(0.5)
 
     cols = pl.ds(pl.multiple_of(step * t, t), t)
     hid = jnp.concatenate([hid_ref[m] for m in range(mloc)], axis=1)
@@ -75,7 +77,7 @@
             f_ref[field_rows(v, mloc, m, r0), cols] = out[r0 : r0 + 8, m * t : (m + 1) * t]
 
 
-def forward(start, p, hidden, w_inner, b_inner, w_out, b_out, vmem):
+def forward(start, p, hidden, w_inner, b_inner, w_out, b_out, vmem, first):
     mloc, h, n = hidden.shape
     v = w_out.shape[0]
     t = TILE
@@ -84,13 +86,22 @@
     once = pl.Buffered(1)
     shape = (p // t, mloc, h, t)
     held = pl.BlockSpec(shape, lambda s: (0, 0, 0, 0))
+    made = []
+    if first:
+        made = [pltpu.VMEM((h, 128), jnp.float32), pltpu.VMEM((v, h), jnp.bfloat16)]
+        kernel = functools.partial(forward_kernel, True)
+    else:
+
+        def kernel(hid, w, bias, half, bo, act, slope, fields, *slabs):
+            forward_kernel(False, hid, w, None, None, bo, act, slope, fields, bias, half, *slabs)
+
     return pl.pallas_call(
-        forward_kernel,
+        kernel,
         grid=(tiles,),
         in_specs=[
             pl.BlockSpec((mloc, h, t), lambda s: (0, 0, start // t + s)),
             pl.BlockSpec((h, h), whole, pipeline_mode=once),
-            pl.BlockSpec((1, h), whole, pipeline_mode=once),
+            pl.BlockSpec(b_inner.shape, whole, pipeline_mode=once),
             pl.BlockSpec((v, h), whole, pipeline_mode=once),
             pl.BlockSpec((1, v), whole, pipeline_mode=once),
         ],
@@ -98,17 +109,15 @@
             held,
             held,
             pl.BlockSpec((mloc * v, p), whole),
-        ],
+        ]
+        + [pl.BlockSpec(a.shape, whole) for a in made],
         out_shape=[
             pltpu.VMEM(shape, jnp.bfloat16),
             pltpu.VMEM(shape, jnp.float32),
             pltpu.VMEM((mloc * v, p), jnp.float32),
-        ],
-        scratch_shapes=[
-            pltpu.VMEM((h, 128), jnp.float32),
-            pltpu.VMEM((v, h), jnp.bfloat16),
         ]
-        + [pltpu.VMEM((SLAB, mloc * t), jnp.float32)] * (h // SLAB),
+        + made,
+        scratch_shapes=[pltpu.VMEM((SLAB, mloc * t), jnp.float32)] * (h // SLAB),
         compiler_params=pltpu.CompilerParams(vmem_limit_bytes=vmem),
         cost_estimate=pl.CostEstimate(
             flops=2 * h * h, bytes_accessed=2 * h * h, transcendentals=0
@@ -464,7 +473,7 @@
     unit = n // sum(EIGHTHS)
     starts = [unit * sum(EIGHTHS[:k]) for k in range(len(EIGHTHS))]
     spans = [(start, unit * size) for start, size in zip(starts, EIGHTHS)]
-    parts, far = [], []
+    parts, far, made = [], [], []
     for start, p in spans:
         w, vmem = w_inner, VMEM
         if len(parts) == 2:
@@ -475,7 +484,10 @@
         else:
             w = pltpu.with_memory_space_constraint(w_inner, pltpu.HBM)
             vmem += 4 * h * h
-        parts.append(forward(start, p, hidden, w, b_inner, w_out, b_out, vmem))
+        spread = made or (b_inner, w_out)
+        *part, = forward(start, p, hidden, w, *spread, b_out, vmem, not parts)
+        made = made or part[3:]
+        parts.append(part[:3])
         far.append(to_x(parts[-1][2]))
     near = [to_core(fields) for _, _, fields in parts]
     vw, area = var_weight.reshape(1, v), area.reshape(1, n)

time: 123 us -> 122 us (level)
  transfers between devices with their start and end apart: 26 -> 26, of which waited for: 12 -> 12; matrix products, arithmetic and copies ran while one was open for 0% -> 0% of each run, Pallas kernels for 44% -> 43%
where the time goes in v5:
time: 122 us
  Pallas kernels  67.5 us (55%)
  waiting for transfers between devices  30 us (25%)
  starting transfers between devices  22.3 us (18%)
    pallas_call x4, Pallas kernels, backward(): pl.pallas_call(kernel_fn, grid=(steps + 1,), in_specs=in_specs, out_specs...  25.8 us
    pallas_call x4, Pallas kernels, forward(): pl.pallas_call(kernel, grid=(tiles,), in_specs=[pl.BlockSpec((mloc, h, t)...  24.5 us
    pallas_call x4, Pallas kernels, input_gradient(): pl.pallas_call(input_kernel, grid=(steps,), in_specs=in_specs, out_specs=...  13.9 us
    ppermute x3, waiting for transfers between devices, shards(): to_hi = lambda a, k: lax.ppermute(a, 'grid', shift_hi(k))  13.1 us
    ppermute x12, starting transfers between devices, shards(): to_core = lambda a: lax.ppermute(a, 'mem', swap_core)  7.32 us
    ppermute x7, starting transfers between devices, shards(): to_x = lambda a: lax.ppermute(a, 'mem', swap_x)  7.06 us
    ppermute x7, waiting for transfers between devices, shards(): to_x = lambda a: lax.ppermute(a, 'mem', swap_x)  6.26 us
    ppermute x12, waiting for transfers between devices, shards(): to_core = lambda a: lax.ppermute(a, 'mem', swap_core)  4.16 us
  transfers between devices with their start and end apart: 26, of which 12 were waited for; matrix products, arithmetic and copies ran while one was open for 0% of the time, Pallas kernels for 43%

profile of v5, /device:TPU:9, one launch (start us, length us, event | category | flops | bytes accessed | tf_op | source)
XLA Modules:
  0.0 121.6 jit_solution(13308521641222502233)
XLA Ops:
  0.7 7.0 %forward_part.4 = (bf16[2,2,1024,256]{3,2,1,0:T(8,128)(2,1)S(1)}, f32[2,2,1024,256]{3,2,1,0:T(8,128)S(1)}, f32[200,512]{1,0:T(8,128)S(1)}, f32[1024,128]{1,0:T(8,128)S(1)}, bf16[100,1024]{1,0:T(8,128)(2,1)S(1)}) custom-call(bf16[2,1024,2048]{2,1,0:T(8,128)(2,1)} %hid_ref.3, bf16[1024,1024]{1,0:T(8,128)(2,1)} %w.5, f32[1,1024]{1,0:T(1,128)} %bitcast.67, ...), custom_call_target="tpu_custom_call" | custom-call | flops 2097152 | bytes 2097152 | tf_op jit(solution)/shard_map/forward_part/pallas_call | solution.py:98
  7.7 1.3 %collective-permute-start.6 = (f32[200,512]{1,0:T(8,128)S(1)}, f32[200,512]{1,0:T(8,128)S(1)}, u32[]{:S(2)}, u32[]{:S(2)}) collective-permute-start(f32[200,512]{1,0:T(8,128)S(1)} %get-tuple-element.67.refs_0_), channel_id=1, source_target_pairs={{0,16},{8,24},{16,0},{24,8},{1,17},{9,25},{17,1},{25,9},{2,18},{10... | collective-permute-start | bytes 1228808 | tf_op jit(solution)/shard_map/ppermute | solution.py:457
  9.0 5.8 %forward_part.5 = (bf16[2,2,1024,256]{3,2,1,0:T(8,128)(2,1)S(1)}, f32[2,2,1024,256]{3,2,1,0:T(8,128)S(1)}, f32[200,512]{1,0:T(8,128)S(1)}) custom-call(bf16[2,1024,2048]{2,1,0:T(8,128)(2,1)} %hid_ref.3, bf16[1024,1024]{1,0:T(8,128)(2,1)S(1)} %copy-done, f32[1024,128]{1,0:T(8,128)S(1)} %get-tuple-element.65.bias, ...), custom_call_target="tpu_custom_call" | custom-call | flops 2097152 | bytes 2097152 | tf_op jit(solution)/shard_map/forward_part/pallas_call | solution.py:98
  14.8 0.3 collective-permute-start.3
  15.1 1.2 %collective-permute-start.5 = (f32[200,512]{1,0:T(8,128)S(1)}, f32[200,512]{1,0:T(8,128)S(1)}, u32[]{:S(2)}, u32[]{:S(2)}) collective-permute-start(f32[200,512]{1,0:T(8,128)S(1)} %get-tuple-element.67.refs_0_), channel_id=1, source_target_pairs={{0,8},{8,0},{16,24},{24,16},{1,9},{9,1},{17,25},{25,17},{2,10},{10... | collective-permute-start | bytes 1228808 | tf_op jit(solution)/shard_map/ppermute | solution.py:458
  16.4 2.2 %transposes.1 = (bf16[1024,1024]{1,0:T(8,128)(2,1)S(1)}, bf16[1024,128]{1,0:T(8,128)(2,1)S(1)}) custom-call(bf16[1024,1024]{1,0:T(8,128)(2,1)S(1)} %copy-done, bf16[100,1024]{1,0:T(8,128)(2,1)} %wo_ref.3), custom_call_target="tpu_custom_call" | custom-call | flops 2048 | bytes 2048 | tf_op jit(solution)/shard_map/transposes/pallas_call | solution.py:342
  18.6 2.2 %collective-permute-start.7 = (f32[200,512]{1,0:T(8,128)S(1)}, f32[200,512]{1,0:T(8,128)S(1)}, u32[]{:S(2)}, u32[]{:S(2)}) collective-permute-start(f32[200,512]{1,0:T(8,128)S(1)} %collective-permute-done.6.refs_2_), channel_id=1, source_target_pairs={{0,8},{8,0},{16,24},{24,16},{1,9},{9,1},{17,25},{25,17},{2,10},{10... | collective-permute-start | bytes 1228808 | tf_op jit(solution)/shard_map/ppermute | solution.py:458
  20.8 5.8 %forward_part.6 = (bf16[2,2,1024,256]{3,2,1,0:T(8,128)(2,1)S(1)}, f32[2,2,1024,256]{3,2,1,0:T(8,128)S(1)}, f32[200,512]{1,0:T(8,128)S(1)}) custom-call(bf16[2,1024,2048]{2,1,0:T(8,128)(2,1)} %hid_ref.3, bf16[1024,1024]{1,0:T(8,128)(2,1)S(1)} %copy-done, f32[1024,128]{1,0:T(8,128)S(1)} %get-tuple-element.65.bias, ...), custom_call_target="tpu_custom_call" | custom-call | flops 2097152 | bytes 2097152 | tf_op jit(solution)/shard_map/forward_part/pallas_call | solution.py:98
  26.7 1.3 %collective-permute-start.10 = (f32[200,512]{1,0:T(8,128)S(1)}, f32[200,512]{1,0:T(8,128)S(1)}, u32[]{:S(2)}, u32[]{:S(2)}) collective-permute-start(f32[200,512]{1,0:T(8,128)S(1)} %get-tuple-element.74.f_ref), channel_id=1, source_target_pairs={{0,16},{8,24},{16,0},{24,8},{1,17},{9,25},{17,1},{25,9},{2,18},{10... | collective-permute-start | bytes 1228808 | tf_op jit(solution)/shard_map/ppermute | solution.py:457
  28.0 5.8 %forward_part.7 = (bf16[2,2,1024,256]{3,2,1,0:T(8,128)(2,1)S(1)}, f32[2,2,1024,256]{3,2,1,0:T(8,128)S(1)}, f32[200,512]{1,0:T(8,128)S(1)}) custom-call(bf16[2,1024,2048]{2,1,0:T(8,128)(2,1)} %hid_ref.3, bf16[1024,1024]{1,0:T(8,128)(2,1)S(1)} %copy-done, f32[1024,128]{1,0:T(8,128)S(1)} %get-tuple-element.65.bias, ...), custom_call_target="tpu_custom_call" | custom-call | flops 2097152 | bytes 2097152 | tf_op jit(solution)/shard_map/forward_part/pallas_call | solution.py:98
  33.8 0.4 collective-permute-start.4
  34.2 0.3 collective-permute-start.1
  34.4 0.4 collective-permute-start.9
  34.9 6.7 %backward_part.4 = (bf16[2,1024,512]{2,1,0:T(8,128)(2,1)S(1)}, f32[128,1024]{1,0:T(8,128)S(1)}, f32[1024,1024]{1,0:T(8,128)S(1)}) custom-call(f32[200,512]{1,0:T(8,128)S(1)} %get-tuple-element.67.refs_0_, f32[200,512]{1,0:T(8,128)S(1)} %collective-permute-done.5.refs_1_, f32[200,512]{1,0:T(8,128)S(1)} %collective-permute-done.6.refs_2_, ...), custom_call_target="tpu_custom_call" | custom-call | flops 2097152 | bytes 2097152 | tf_op jit(solution)/shard_map/backward_part/pallas_call | solution.py:311
  41.7 0.4 collective-permute-start.11
  42.1 6.2 %backward_part.5 = (bf16[2,1024,512]{2,1,0:T(8,128)(2,1)S(1)}, f32[128,1024]{1,0:T(8,128)S(1)}, f32[1024,1024]{1,0:T(8,128)S(1)}) custom-call(f32[200,512]{1,0:T(8,128)S(1)} %get-tuple-element.69.f_ref, f32[200,512]{1,0:T(8,128)S(1)} %collective-permute-done.2.fc_ref, ...), custom_call_target="tpu_custom_call", output_to_operand_aliasing={{2}: (11, {}), {1}: (12, {})} | custom-call | flops 2097152 | bytes 2097152 | tf_op jit(solution)/shard_map/backward_part/pallas_call | solution.py:311
  48.3 0.1 collective-permute-start.8
  48.5 6.4 %backward_part.6 = (bf16[2,1024,512]{2,1,0:T(8,128)(2,1)S(1)}, f32[128,1024]{1,0:T(8,128)S(1)}, f32[1024,1024]{1,0:T(8,128)S(1)}) custom-call(f32[200,512]{1,0:T(8,128)S(1)} %get-tuple-element.74.f_ref, f32[200,512]{1,0:T(8,128)S(1)} %collective-permute-done.9.fc_ref, ...), custom_call_target="tpu_custom_call", output_to_operand_aliasing={{2}: (11, {}), {1}: (12, {})} | custom-call | flops 2097152 | bytes 2097152 | tf_op jit(solution)/shard_map/backward_part/pallas_call | solution.py:311
  55.0 6.6 %backward_part.7 = (bf16[2,1024,512]{2,1,0:T(8,128)(2,1)S(1)}, f32[128,1024]{1,0:T(8,128)S(1)}, f32[1024,1024]{1,0:T(8,128)S(1)}, f32[2,2,4,72,256]{4,3,2,1,0:T(...) custom-call(f32[200,512]{1,0:T(8,128)S(1)} %get-tuple-element.76.f_r, ...), custom_call_target="tpu_custom_call", output_to_operand_aliasing={{2}: (11, {}), {1}: (12, {})} | custom-call | flops 2097152 | bytes 2097152 | tf_op jit(solution)/shard_map/backward_part/pallas_call | solution.py:311
  61.5 0.4 collective-permute-start.12
  61.9 0.2 collective-permute-start.13
  62.1 2.3 %collective-permute-done.12 = f32[2,2,4,72,256]{4,3,2,1,0:T(8,128)S(1)} collective-permute-done((f32[2,2,4,72,256]{4,3,2,1,0:T(8,128)S(1)}, f32[2,2,4,72,256]{4,3,2,1,0:T(8,128)S(1)}, u32[]{:S(2)}, u32[]{:S(2)}) %collective-permute-start.12) | collective-permute-done | bytes 1179680 | tf_op jit(solution)/shard_map/ppermute | solution.py:458
  64.5 1.3 %collective-permute-start.14 = (f32[2,4,72,256]{3,2,1,0:T(8,128)S(1)}, f32[2,4,72,256]{3,2,1,0:T(8,128)S(1)}, u32[]{:S(2)}, u32[]{:S(2)}) collective-permute-start(f32[2,4,72,256]{3,2,1,0:T(8,128)S(1)} %fusion.5), channel_id=1, source_target_pairs={{0,16},{8,24},{16,0},{24,8},{1,17},{9,25},{17,1},{25,9},{2,18},{10... | collective-permute-start | bytes 1769480 | tf_op jit(solution)/shard_map/ppermute | solution.py:457
  65.9 0.3 collective-permute-done.13
  66.2 1.3 %collective-permute-start.15 = (f32[2,4,72,256]{3,2,1,0:T(8,128)S(1)}, f32[2,4,72,256]{3,2,1,0:T(8,128)S(1)}, u32[]{:S(2)}, u32[]{:S(2)}) collective-permute-start(f32[2,4,72,256]{3,2,1,0:T(8,128)S(1)} %fusion.4), channel_id=1, source_target_pairs={{0,1},{1,0},{2,3},{3,2},{4,5},{5,4},{6,7},{7,6},{8,9},{9,8},{10,11... | collective-permute-start | bytes 1769480 | tf_op jit(solution)/shard_map/ppermute | solution.py:459
  67.5 3.5 %grad_hidden_part.4.refs_0_ = bf16[2,1024,2048]{2,1,0:T(8,128)(2,1)} custom-call(bf16[1024,1024]{1,0:T(8,128)(2,1)S(1)} %get-tuple-element.71.wt_ref, bf16[2,1024,512]{2,1,0:T(8,128)(2,1)S(1)} %get-tuple-element.104.gp_ref), custom_call_target="tpu_custom_call" | custom-call | flops 2097152 | bytes 2097152 | tf_op jit(solution)/shard_map/grad_hidden_part/pallas_call | solution.py:416
  71.0 3.5 %grad_hidden_part.5.refs_0_ = bf16[2,1024,2048]{2,1,0:T(8,128)(2,1)} custom-call(bf16[1024,1024]{1,0:T(8,128)(2,1)S(1)} %get-tuple-element.71.wt_ref, bf16[2,1024,512]{2,1,0:T(8,128)(2,1)S(1)} %get-tuple-element.103.gp_ref, bf16[2,1024,2048]{2,1,0:T(8,128)(2,1)} %grad_hidden_part.4.refs_0_), custom_call_target="tpu_custom_call", output_to_operand_aliasing={{}: (2, {})} | custom-call | flops 2097152 | bytes 2097152 | tf_op jit(solution)/shard_map/grad_hidden_part/pallas_call | solution.py:416
  74.5 4.7 %collective-permute-done.14 = f32[2,4,72,256]{3,2,1,0:T(8,128)S(1)} collective-permute-done((f32[2,4,72,256]{3,2,1,0:T(8,128)S(1)}, f32[2,4,72,256]{3,2,1,0:T(8,128)S(1)}, u32[]{:S(2)}, u32[]{:S(2)}) %collective-permute-start.14) | collective-permute-done | bytes 589856 | tf_op jit(solution)/shard_map/ppermute | solution.py:457
  79.4 1.3 %collective-permute-start.16 = (f32[4,72,256]{2,1,0:T(8,128)S(1)}, f32[4,72,256]{2,1,0:T(8,128)S(1)}, u32[]{:S(2)}, u32[]{:S(2)}) collective-permute-start(f32[4,72,256]{2,1,0:T(8,128)S(1)} %get-tuple-element.125), channel_id=1, source_target_pairs={{0,1},{1,0},{2,3},{3,2},{4,5},{5,4},{6,7},{7,6},{8,9},{9,8},{10,11... | collective-permute-start | bytes 884744 | tf_op jit(solution)/shard_map/ppermute | solution.py:459
  80.7 0.2 collective-permute-done.15
  81.1 1.3 %collective-permute-start.17 = (f32[4,72,256]{2,1,0:T(8,128)S(1)}, f32[4,72,256]{2,1,0:T(8,128)S(1)}, u32[]{:S(2)}, u32[]{:S(2)}) collective-permute-start(f32[4,72,256]{2,1,0:T(8,128)S(1)} %get-tuple-element.123), channel_id=1, source_target_pairs={{0,16},{8,24},{16,0},{24,8},{1,17},{9,25},{17,1},{25,9},{2,18},{10... | collective-permute-start | bytes 884744 | tf_op jit(solution)/shard_map/ppermute | solution.py:457
  82.4 3.5 %grad_hidden_part.6.refs_0_ = bf16[2,1024,2048]{2,1,0:T(8,128)(2,1)} custom-call(bf16[1024,1024]{1,0:T(8,128)(2,1)S(1)} %get-tuple-element.71.wt_ref, bf16[2,1024,512]{2,1,0:T(8,128)(2,1)S(1)} %get-tuple-element.110.gp_ref, bf16[2,1024,2048]{2,1,0:T(8,128)(2,1)} %grad_hidden_part.5.refs_0_), custom_call_target="tpu_custom_call", output_to_operand_aliasing={{}: (2, {})} | custom-call | flops 2097152 | bytes 2097152 | tf_op jit(solution)/shard_map/grad_hidden_part/pallas_call | solution.py:416
  85.9 0.9 collective-permute-done.16
  86.9 1.5 %collective-permute-done.17 = f32[4,72,256]{2,1,0:T(8,128)S(1)} collective-permute-done((f32[4,72,256]{2,1,0:T(8,128)S(1)}, f32[4,72,256]{2,1,0:T(8,128)S(1)}, u32[]{:S(2)}, u32[]{:S(2)}) %collective-permute-start.17) | collective-permute-done | bytes 294944 | tf_op jit(solution)/shard_map/ppermute | solution.py:457
  88.6 1.4 %collective-permute-start.18 = (f32[192,256]{1,0:T(8,128)S(1)}, f32[192,256]{1,0:T(8,128)S(1)}, u32[]{:S(2)}, u32[]{:S(2)}) collective-permute-start(f32[192,256]{1,0:T(8,128)S(1)} %get-tuple-element.144), channel_id=1, source_target_pairs={{0,2},{1,3},{2,4},{3,5},{4,6},{5,7},{6,0},{7,1},{8,10},{9,11},{10,... | collective-permute-start | bytes 589832 | tf_op jit(solution)/shard_map/ppermute | solution.py:460
  89.9 1.1 collective-permute-start.19
  91.0 1.4 %collective-permute-start.20 = (f32[192,256]{1,0:T(8,128)S(1)}, f32[192,256]{1,0:T(8,128)S(1)}, u32[]{:S(2)}, u32[]{:S(2)}) collective-permute-start(f32[192,256]{1,0:T(8,128)S(1)} %get-tuple-element.143), channel_id=1, source_target_pairs={{0,6},{1,7},{2,0},{3,1},{4,2},{5,3},{6,4},{7,5},{8,14},{9,15},{10,... | collective-permute-start | bytes 589832 | tf_op jit(solution)/shard_map/ppermute | solution.py:460
  92.4 3.5 %grad_hidden_part.7 = bf16[2,1024,2048]{2,1,0:T(8,128)(2,1)} custom-call(bf16[1024,1024]{1,0:T(8,128)(2,1)S(1)} %get-tuple-element.71.wt_ref, bf16[2,1024,512]{2,1,0:T(8,128)(2,1)S(1)} %get-tuple-element.114.gp_ref, bf16[2,1024,2048]{2,1,0:T(8,128)(2,1)} %grad_hidden_part.6.refs_0_), custom_call_target="tpu_custom_call", output_to_operand_aliasing={{}: (2, {})} | custom-call | flops 2097152 | bytes 2097152 | tf_op jit(solution)/shard_map/grad_hidden_part/pallas_call | solution.py:416
  95.9 9.0 %collective-permute-done.19 = f32[192,256]{1,0:T(8,128)S(1)} collective-permute-done((f32[192,256]{1,0:T(8,128)S(1)}, f32[192,256]{1,0:T(8,128)S(1)}, u32[]{:S(2)}, u32[]{:S(2)}) %collective-permute-start.19) | collective-permute-done | bytes 196640 | tf_op jit(solution)/shard_map/ppermute | solution.py:460
  104.9 4.0 %collective-permute-done.20 = f32[192,256]{1,0:T(8,128)S(1)} collective-permute-done((f32[192,256]{1,0:T(8,128)S(1)}, f32[192,256]{1,0:T(8,128)S(1)}, u32[]{:S(2)}, u32[]{:S(2)}) %collective-permute-start.20) | collective-permute-done | bytes 196640 | tf_op jit(solution)/shard_map/ppermute | solution.py:460
  109.0 1.3 %collective-permute-start.21 = (f32[192,256]{1,0:T(8,128)S(1)}, f32[192,256]{1,0:T(8,128)S(1)}, u32[]{:S(2)}, u32[]{:S(2)}) collective-permute-start(f32[192,256]{1,0:T(8,128)S(1)} %add_add_fusion), channel_id=1, source_target_pairs={{0,16},{8,24},{16,0},{24,8},{1,17},{9,25},{17,1},{25,9},{2,18},{10... | collective-permute-start | bytes 589832 | tf_op jit(solution)/shard_map/ppermute | solution.py:457
  110.3 1.4 %collective-permute-start.23 = (f32[1,64,256]{2,1,0:T(8,128)S(1)}, f32[1,64,256]{2,1,0:T(8,128)S(1)}, u32[]{:S(2)}, u32[]{:S(2)}) collective-permute-start(f32[1,64,256]{2,1,0:T(8,128)S(1)} %get-tuple-element.135), channel_id=1, source_target_pairs={{0,1},{1,0},{2,3},{3,2},{4,5},{5,4},{6,7},{7,6},{8,9},{9,8},{10,11... | collective-permute-start | bytes 196616 | tf_op jit(solution)/shard_map/ppermute | solution.py:550
  111.8 2.0 %collective-permute-done.23 = f32[1,64,256]{2,1,0:T(8,128)S(1)} collective-permute-done((f32[1,64,256]{2,1,0:T(8,128)S(1)}, f32[1,64,256]{2,1,0:T(8,128)S(1)}, u32[]{:S(2)}, u32[]{:S(2)}) %collective-permute-start.23) | collective-permute-done | bytes 65568 | tf_op jit(solution)/shard_map/ppermute | solution.py:550
  113.8 3.4 %collective-permute-done.24 = f32[1,64,256]{2,1,0:T(8,128)S(1)} collective-permute-done((f32[1,64,256]{2,1,0:T(8,128)S(1)}, f32[1,64,256]{2,1,0:T(8,128)S(1)}, u32[]{:S(2)}, u32[]{:S(2)}) %collective-permute-start.24) | collective-permute-done | bytes 65568 | tf_op jit(solution)/shard_map/ppermute | solution.py:552
  117.3 1.7 %collective-permute-start.25 = (f32[2,2,2,4,8,256]{5,4,3,2,1,0:T(8,128)S(1)}, f32[2,2,2,4,8,256]{5,4,3,2,1,0:T(8,128)S(1)}, u32[]{:S(2)}, u32[]{:S(2)}) collective-permute-start(f32[2,2,2,4,8,256]{5,4,3,2,1,0:T(8,128)S(1)} %maximum_select_fusion.e_ref), channel_id=1, source_target_pairs={{0,8},{8,0},{16,24},{24,16},{1,9},{9,1},{17,25},{25,17},{2,10},{10... | collective-permute-start | bytes 786440 | tf_op jit(solution)/shard_map/ppermute | solution.py:458
  119.1 1.0 collective-permute-done.25.f_ref
  120.1 0.5 collective-permute-done.22.other_ref
  120.6 1.0 last.1
  (47 shorter events, 1.2 us)
Async XLA Ops:
  0.6 8.3 %copy-start = (bf16[1024,1024]{1,0:T(8,128)(2,1)S(1)}, bf16[1024,1024]{1,0:T(8,128)(2,1)}, u32[]{:S(2)}) copy-start(bf16[1024,1024]{1,0:T(8,128)(2,1)} %w.5) | copy-start | bytes 6291460
  7.7 10.9 %collective-permute-start.6 = (f32[200,512]{1,0:T(8,128)S(1)}, f32[200,512]{1,0:T(8,128)S(1)}, u32[]{:S(2)}, u32[]{:S(2)}) collective-permute-start(f32[200,512]{1,0:T(8,128)S(1)} %get-tuple-element.67.refs_0_), channel_id=1, source_target_pairs={{0,16},{8,24},{16,0},{24,8},{1,17},{9,25},{17,1},{25,9},{2,18},{10... | collective-permute-start | bytes 1228808 | tf_op jit(solution)/shard_map/ppermute | solution.py:457
  14.8 19.0 %collective-permute-start.3 = (f32[200,512]{1,0:T(8,128)S(1)}, f32[200,512]{1,0:T(8,128)S(1)}, u32[]{:S(2)}, u32[]{:S(2)}) collective-permute-start(f32[200,512]{1,0:T(8,128)S(1)} %get-tuple-element.69.f_ref), channel_id=1, source_target_pairs={{0,16},{8,24},{16,0},{24,8},{1,17},{9,25},{17,1},{25,9},{2,18},{10... | collective-permute-start | bytes 1228808 | tf_op jit(solution)/shard_map/ppermute | solution.py:457
  15.1 19.0 %collective-permute-start.5 = (f32[200,512]{1,0:T(8,128)S(1)}, f32[200,512]{1,0:T(8,128)S(1)}, u32[]{:S(2)}, u32[]{:S(2)}) collective-permute-start(f32[200,512]{1,0:T(8,128)S(1)} %get-tuple-element.67.refs_0_), channel_id=1, source_target_pairs={{0,8},{8,0},{16,24},{24,16},{1,9},{9,1},{17,25},{25,17},{2,10},{10... | collective-permute-start | bytes 1228808 | tf_op jit(solution)/shard_map/ppermute | solution.py:458
  16.4 25.3 %collective-permute-start.2 = (f32[200,512]{1,0:T(8,128)S(1)}, f32[200,512]{1,0:T(8,128)S(1)}, u32[]{:S(2)}, u32[]{:S(2)}) collective-permute-start(f32[200,512]{1,0:T(8,128)S(1)} %get-tuple-element.69.f_ref), channel_id=1, source_target_pairs={{0,8},{8,0},{16,24},{24,16},{1,9},{9,1},{17,25},{25,17},{2,10},{10... | collective-permute-start | bytes 1228808 | tf_op jit(solution)/shard_map/ppermute | solution.py:458
  18.6 15.8 %collective-permute-start.7 = (f32[200,512]{1,0:T(8,128)S(1)}, f32[200,512]{1,0:T(8,128)S(1)}, u32[]{:S(2)}, u32[]{:S(2)}) collective-permute-start(f32[200,512]{1,0:T(8,128)S(1)} %collective-permute-done.6.refs_2_), channel_id=1, source_target_pairs={{0,8},{8,0},{16,24},{24,16},{1,9},{9,1},{17,25},{25,17},{2,10},{10... | collective-permute-start | bytes 1228808 | tf_op jit(solution)/shard_map/ppermute | solution.py:458
  26.6 8.3 %copy-start.1 = (f32[100,2048]{1,0:T(8,128)S(1)}, f32[100,2048]{1,0:T(8,128)}, u32[]{:S(2)}) copy-start(f32[100,2048]{1,0:T(8,128)} %target_ref.5) | copy-start | bytes 2457604
  26.6 8.3 %copy-start.2 = (f32[2048]{0:T(1024)S(1)}, f32[2048]{0:T(1024)}, u32[]{:S(2)}) copy-start(f32[2048]{0:T(1024)} %param.10) | copy-start | bytes 24580
  26.6 8.2 %copy-start.3 = (f32[100]{0:T(128)S(1)}, f32[100]{0:T(128)}, u32[]{:S(2)}) copy-start(f32[100]{0:T(128)} %param.11) | copy-start | bytes 1204
  26.7 14.9 %collective-permute-start.10 = (f32[200,512]{1,0:T(8,128)S(1)}, f32[200,512]{1,0:T(8,128)S(1)}, u32[]{:S(2)}, u32[]{:S(2)}) collective-permute-start(f32[200,512]{1,0:T(8,128)S(1)} %get-tuple-element.74.f_ref), channel_id=1, source_target_pairs={{0,16},{8,24},{16,0},{24,8},{1,17},{9,25},{17,1},{25,9},{2,18},{10... | collective-permute-start | bytes 1228808 | tf_op jit(solution)/shard_map/ppermute | solution.py:457
  33.8 8.3 %collective-permute-start.4 = (f32[200,512]{1,0:T(8,128)S(1)}, f32[200,512]{1,0:T(8,128)S(1)}, u32[]{:S(2)}, u32[]{:S(2)}) collective-permute-start(f32[200,512]{1,0:T(8,128)S(1)} %collective-permute-done.3.fx_ref), channel_id=1, source_target_pairs={{0,8},{8,0},{16,24},{24,16},{1,9},{9,1},{17,25},{25,17},{2,10},{10... | collective-permute-start | bytes 1228808 | tf_op jit(solution)/shard_map/ppermute | solution.py:458
  34.2 14.2 %collective-permute-start.1 = (f32[200,512]{1,0:T(8,128)S(1)}, f32[200,512]{1,0:T(8,128)S(1)}, u32[]{:S(2)}, u32[]{:S(2)}) collective-permute-start(f32[200,512]{1,0:T(8,128)S(1)} %get-tuple-element.76.f_ref), channel_id=1, source_target_pairs={{0,16},{8,24},{16,0},{24,8},{1,17},{9,25},{17,1},{25,9},{2,18},{10... | collective-permute-start | bytes 1228808 | tf_op jit(solution)/shard_map/ppermute | solution.py:457
  34.4 14.0 %collective-permute-start.9 = (f32[200,512]{1,0:T(8,128)S(1)}, f32[200,512]{1,0:T(8,128)S(1)}, u32[]{:S(2)}, u32[]{:S(2)}) collective-permute-start(f32[200,512]{1,0:T(8,128)S(1)} %get-tuple-element.74.f_ref), channel_id=1, source_target_pairs={{0,8},{8,0},{16,24},{24,16},{1,9},{9,1},{17,25},{25,17},{2,10},{10... | collective-permute-start | bytes 1228808 | tf_op jit(solution)/shard_map/ppermute | solution.py:458
  41.6 13.4 %collective-permute-start = (f32[200,512]{1,0:T(8,128)S(1)}, f32[200,512]{1,0:T(8,128)S(1)}, u32[]{:S(2)}, u32[]{:S(2)}) collective-permute-start(f32[200,512]{1,0:T(8,128)S(1)} %get-tuple-element.76.f_ref), channel_id=1, source_target_pairs={{0,8},{8,0},{16,24},{24,16},{1,9},{9,1},{17,25},{25,17},{2,10},{10... | collective-permute-start | bytes 1228808 | tf_op jit(solution)/shard_map/ppermute | solution.py:458
  41.7 6.8 %collective-permute-start.11 = (f32[200,512]{1,0:T(8,128)S(1)}, f32[200,512]{1,0:T(8,128)S(1)}, u32[]{:S(2)}, u32[]{:S(2)}) collective-permute-start(f32[200,512]{1,0:T(8,128)S(1)} %collective-permute-done.10.fx_ref), channel_id=1, source_target_pairs={{0,8},{8,0},{16,24},{24,16},{1,9},{9,1},{17,25},{25,17},{2,10},{10... | collective-permute-start | bytes 1228808 | tf_op jit(solution)/shard_map/ppermute | solution.py:458
  48.3 6.6 %collective-permute-start.8 = (f32[200,512]{1,0:T(8,128)S(1)}, f32[200,512]{1,0:T(8,128)S(1)}, u32[]{:S(2)}, u32[]{:S(2)}) collective-permute-start(f32[200,512]{1,0:T(8,128)S(1)} %collective-permute-done.1.fx_ref), channel_id=1, source_target_pairs={{0,8},{8,0},{16,24},{24,16},{1,9},{9,1},{17,25},{25,17},{2,10},{10... | collective-permute-start | bytes 1228808 | tf_op jit(solution)/shard_map/ppermute | solution.py:458
  61.5 2.9 %collective-permute-start.12 = (f32[2,2,4,72,256]{4,3,2,1,0:T(8,128)S(1)}, f32[2,2,4,72,256]{4,3,2,1,0:T(8,128)S(1)}, u32[]{:S(2)}, u32[]{:S(2)}) collective-permute-start(f32[2,2,4,72,256]{4,3,2,1,0:T(8,128)S(1)} %get-tuple-element.100), channel_id=1, source_target_pairs={{0,8},{8,0},{16,24},{24,16},{1,9},{9,1},{17,25},{25,17},{2,10},{10... | collective-permute-start | bytes 3538952 | tf_op jit(solution)/shard_map/ppermute | solution.py:458
  61.9 4.2 %collective-permute-start.13 = (f32[2,2,4,72,256]{4,3,2,1,0:T(8,128)S(1)}, f32[2,2,4,72,256]{4,3,2,1,0:T(8,128)S(1)}, u32[]{:S(2)}, u32[]{:S(2)}) collective-permute-start(f32[2,2,4,72,256]{4,3,2,1,0:T(8,128)S(1)} %get-tuple-element.102), channel_id=1, source_target_pairs={{0,8},{8,0},{16,24},{24,16},{1,9},{9,1},{17,25},{25,17},{2,10},{10... | collective-permute-start | bytes 3538952 | tf_op jit(solution)/shard_map/ppermute | solution.py:458
  64.5 14.7 %collective-permute-start.14 = (f32[2,4,72,256]{3,2,1,0:T(8,128)S(1)}, f32[2,4,72,256]{3,2,1,0:T(8,128)S(1)}, u32[]{:S(2)}, u32[]{:S(2)}) collective-permute-start(f32[2,4,72,256]{3,2,1,0:T(8,128)S(1)} %fusion.5), channel_id=1, source_target_pairs={{0,16},{8,24},{16,0},{24,8},{1,17},{9,25},{17,1},{25,9},{2,18},{10... | collective-permute-start | bytes 1769480 | tf_op jit(solution)/shard_map/ppermute | solution.py:457
  66.2 14.7 %collective-permute-start.15 = (f32[2,4,72,256]{3,2,1,0:T(8,128)S(1)}, f32[2,4,72,256]{3,2,1,0:T(8,128)S(1)}, u32[]{:S(2)}, u32[]{:S(2)}) collective-permute-start(f32[2,4,72,256]{3,2,1,0:T(8,128)S(1)} %fusion.4), channel_id=1, source_target_pairs={{0,1},{1,0},{2,3},{3,2},{4,5},{5,4},{6,7},{7,6},{8,9},{9,8},{10,11... | collective-permute-start | bytes 1769480 | tf_op jit(solution)/shard_map/ppermute | solution.py:459
  79.4 7.4 %collective-permute-start.16 = (f32[4,72,256]{2,1,0:T(8,128)S(1)}, f32[4,72,256]{2,1,0:T(8,128)S(1)}, u32[]{:S(2)}, u32[]{:S(2)}) collective-permute-start(f32[4,72,256]{2,1,0:T(8,128)S(1)} %get-tuple-element.125), channel_id=1, source_target_pairs={{0,1},{1,0},{2,3},{3,2},{4,5},{5,4},{6,7},{7,6},{8,9},{9,8},{10,11... | collective-permute-start | bytes 884744 | tf_op jit(solution)/shard_map/ppermute | solution.py:459
  81.1 7.3 %collective-permute-start.17 = (f32[4,72,256]{2,1,0:T(8,128)S(1)}, f32[4,72,256]{2,1,0:T(8,128)S(1)}, u32[]{:S(2)}, u32[]{:S(2)}) collective-permute-start(f32[4,72,256]{2,1,0:T(8,128)S(1)} %get-tuple-element.123), channel_id=1, source_target_pairs={{0,16},{8,24},{16,0},{24,8},{1,17},{9,25},{17,1},{25,9},{2,18},{10... | collective-permute-start | bytes 884744 | tf_op jit(solution)/shard_map/ppermute | solution.py:457
  88.6 7.3 %collective-permute-start.18 = (f32[192,256]{1,0:T(8,128)S(1)}, f32[192,256]{1,0:T(8,128)S(1)}, u32[]{:S(2)}, u32[]{:S(2)}) collective-permute-start(f32[192,256]{1,0:T(8,128)S(1)} %get-tuple-element.144), channel_id=1, source_target_pairs={{0,2},{1,3},{2,4},{3,5},{4,6},{5,7},{6,0},{7,1},{8,10},{9,11},{10,... | collective-permute-start | bytes 589832 | tf_op jit(solution)/shard_map/ppermute | solution.py:460
  89.9 15.0 %collective-permute-start.19 = (f32[192,256]{1,0:T(8,128)S(1)}, f32[192,256]{1,0:T(8,128)S(1)}, u32[]{:S(2)}, u32[]{:S(2)}) collective-permute-start(f32[192,256]{1,0:T(8,128)S(1)} %get-tuple-element.142), channel_id=1, source_target_pairs={{0,4},{1,5},{2,6},{3,7},{4,0},{5,1},{6,2},{7,3},{8,12},{9,13},{10,... | collective-permute-start | bytes 589832 | tf_op jit(solution)/shard_map/ppermute | solution.py:460
  91.0 17.9 %collective-permute-start.20 = (f32[192,256]{1,0:T(8,128)S(1)}, f32[192,256]{1,0:T(8,128)S(1)}, u32[]{:S(2)}, u32[]{:S(2)}) collective-permute-start(f32[192,256]{1,0:T(8,128)S(1)} %get-tuple-element.143), channel_id=1, source_target_pairs={{0,6},{1,7},{2,0},{3,1},{4,2},{5,3},{6,4},{7,5},{8,14},{9,15},{10,... | collective-permute-start | bytes 589832 | tf_op jit(solution)/shard_map/ppermute | solution.py:460
  109.0 8.2 %collective-permute-start.21 = (f32[192,256]{1,0:T(8,128)S(1)}, f32[192,256]{1,0:T(8,128)S(1)}, u32[]{:S(2)}, u32[]{:S(2)}) collective-permute-start(f32[192,256]{1,0:T(8,128)S(1)} %add_add_fusion), channel_id=1, source_target_pairs={{0,16},{8,24},{16,0},{24,8},{1,17},{9,25},{17,1},{25,9},{2,18},{10... | collective-permute-start | bytes 589832 | tf_op jit(solution)/shard_map/ppermute | solution.py:457
  110.3 3.5 %collective-permute-start.23 = (f32[1,64,256]{2,1,0:T(8,128)S(1)}, f32[1,64,256]{2,1,0:T(8,128)S(1)}, u32[]{:S(2)}, u32[]{:S(2)}) collective-permute-start(f32[1,64,256]{2,1,0:T(8,128)S(1)} %get-tuple-element.135), channel_id=1, source_target_pairs={{0,1},{1,0},{2,3},{3,2},{4,5},{5,4},{6,7},{7,6},{8,9},{9,8},{10,11... | collective-permute-start | bytes 196616 | tf_op jit(solution)/shard_map/ppermute | solution.py:550
  111.7 5.5 %collective-permute-start.24 = (f32[1,64,256]{2,1,0:T(8,128)S(1)}, f32[1,64,256]{2,1,0:T(8,128)S(1)}, u32[]{:S(2)}, u32[]{:S(2)}) collective-permute-start(f32[1,64,256]{2,1,0:T(8,128)S(1)} %get-tuple-element.135), channel_id=1, source_target_pairs={{0,17},{1,16},{2,19},{3,18},{4,21},{5,20},{6,23},{7,22},{8,25},{9,... | collective-permute-start | bytes 196616 | tf_op jit(solution)/shard_map/ppermute | solution.py:552
  117.3 2.9 %collective-permute-start.25 = (f32[2,2,2,4,8,256]{5,4,3,2,1,0:T(8,128)S(1)}, f32[2,2,2,4,8,256]{5,4,3,2,1,0:T(8,128)S(1)}, u32[]{:S(2)}, u32[]{:S(2)}) collective-permute-start(f32[2,2,2,4,8,256]{5,4,3,2,1,0:T(8,128)S(1)} %maximum_select_fusion.e_ref), channel_id=1, source_target_pairs={{0,8},{8,0},{16,24},{24,16},{1,9},{9,1},{17,25},{25,17},{2,10},{10... | collective-permute-start | bytes 786440 | tf_op jit(solution)/shard_map/ppermute | solution.py:458
  119.0 1.6 %collective-permute-start.22 = (f32[64,1024]{1,0:T(8,128)S(1)}, f32[64,1024]{1,0:T(8,128)S(1)}, u32[]{:S(2)}, u32[]{:S(2)}) collective-permute-start(f32[64,1024]{1,0:T(8,128)S(1)} %pad_maximum_fusion.8.own_ref), channel_id=1, source_target_pairs={{0,8},{8,0},{16,24},{24,16},{1,9},{9,1},{17,25},{25,17},{2,10},{10... | collective-permute-start | bytes 786440 | tf_op jit(solution)/shard_map/ppermute | solution.py:458
